TPU v7x, 512 devices: a whole 4x4x16 slice. The times are simulated.
512 devices in a mesh: layer: 8 (over z_lo), row: 8 (over x, core), col: 8 (over z_hi, y).
Axes of the slice: x: 4, y: 4, z: 16 (z_hi: 2, z_lo: 8; z = z_hi * 8 + z_lo), core: 2. Of those that a mesh axis runs over, the one named last changes fastest.
Arguments:
- grad: bfloat16 [40960, 1024], P(('layer', 'row'), 'col'), parts along dimension 0, may hold values from -6 to 6
- left_basis: bfloat16 [40960, 5120], P(('layer', 'row'), 'col'), parts along dimension 0, may hold values from -0.078125 to 0.078125
- right_rows: bfloat16 [8192, 1024], P('layer', 'col'), parts along dimension 0, may hold values from -0.1875 to 0.1875
- exp_avg: float32 [40960, 1024], P(('layer', 'col'), 'row'), parts along dimension 0, may hold values from -2 to 2
- exp_avg_sq: float32 [40960, 1024], P(('layer', 'col'), 'row'), parts along dimension 0, may hold values from 0.05 to 2
Outputs:
- update: bfloat16 [40960, 1024], P(('layer', 'row'), 'col'), parts along dimension 0
- exp_avg_new: float32 [40960, 1024], P(('layer', 'col'), 'row'), parts along dimension 0
- exp_avg_sq_new: float32 [40960, 1024], P(('layer', 'col'), 'row'), parts along dimension 0
- left_gram: float32 [40960, 5120], P(('layer', 'row'), 'col'), parts along dimension 0
- right_gram: float32 [8192, 1024], P(('layer', 'col'), 'row'), parts along dimension 0
There are 8 independent parts, one for each index of `layer`. A program takes and returns all parts, laid end to end along the dimension named above; each array names one. Nothing has to cross between parts.
All inputs are finite; a program needn't handle non-finite values.
Results may differ from a plain program's by a relative error of at most 0.02.
Values may be sent and summed in bfloat16 or wider, within the bound.
No kernel may reach another device: no remote copies, remote signals or barrier semaphores. Data moves between devices by JAX's collectives and lax.ppermute only.
A program may use at most 64 MiB of HBM per device.

v0:
```python
import jax
import jax.numpy as jnp
from jax import lax
from jax.sharding import PartitionSpec as P

M = 5120
C = 1024


first_beta = 0.9
second_beta = 0.95
epsilon = 1e-08


def body(grad, left_basis, right_rows, exp_avg, exp_avg_sq):
    grad_piece = lax.all_gather(grad, "col", axis=1, tiled=True)
    basis_piece = lax.all_gather(right_rows, "col", axis=1, tiled=True)
    right_sum = lax.dot_general(
        grad_piece, basis_piece, (((1,), (1,)), ((), ())), preferred_element_type=jnp.float32
    )
    row_panel = grad_piece
    gram_piece = lax.dot_general(
        grad, grad_piece, (((0,), (0,)), ((), ())), preferred_element_type=jnp.float32
    )
    gram_rows = gram_piece
    right_sum, row_panel, gram_rows = (right_sum, row_panel, gram_rows)
    rotated_right = right_sum.astype(jnp.bfloat16)
    left_terms = lax.dot_general(
        left_basis, rotated_right, (((0,), (0,)), ((), ())), preferred_element_type=jnp.float32
    )
    rotated, right_gram = (
        lax.psum_scatter(
            left_terms.astype(jnp.bfloat16), "row", scatter_dimension=1, tiled=True
        ).astype(jnp.float32),
        lax.psum_scatter(
            (gram_rows * (1.0 / M)).astype(jnp.bfloat16), "row", scatter_dimension=1, tiled=True
        ).astype(jnp.float32),
    )
    exp_avg_new = first_beta * exp_avg + (1.0 - first_beta) * rotated
    exp_avg_sq_new = second_beta * exp_avg_sq + (1.0 - second_beta) * rotated * rotated
    direction = (exp_avg_new / (jnp.sqrt(exp_avg_sq_new) + epsilon)).astype(jnp.bfloat16)
    columns, direction_panel = (
        lax.all_gather(grad, "row", axis=0, tiled=True),
        lax.all_gather(direction, "row", axis=1, tiled=True),
    )
    back_terms = jnp.dot(left_basis, direction_panel, preferred_element_type=jnp.float32)
    back_whole = lax.psum(back_terms.astype(jnp.bfloat16), "col")
    update = jnp.dot(back_whole, right_rows, preferred_element_type=jnp.float32).astype(
        jnp.bfloat16
    )
    received = lax.all_to_all(columns, "col", split_axis=0, concat_axis=1, tiled=True)
    left_gram = lax.dot_general(
        row_panel, received, (((1,), (1,)), ((), ())), preferred_element_type=jnp.float32
    ) * (1.0 / C)
    return (update, exp_avg_new, exp_avg_sq_new, left_gram, right_gram)


def solution(mesh):
    placed = (
        P(("layer", "row"), "col"),
        P(("layer", "row"), "col"),
        P("layer", "col"),
        P(("layer", "col"), "row"),
        P(("layer", "col"), "row"),
    )
    return jax.shard_map(
        body,
        mesh=mesh,
        in_specs=placed,
        out_specs=(
            P(("layer", "row"), "col"),
            P(("layer", "col"), "row"),
            P(("layer", "col"), "row"),
            P(("layer", "row"), "col"),
            P(("layer", "col"), "row"),
        ),
        check_vma=False,
    )
```

profile of v0, /device:TPU:24, one launch (start us, length us, event | category | flops | bytes accessed | tf_op | source)
XLA Modules:
  0.0 567.8 jit_solution(9618165773220053474)
XLA Ops:
  7.2 0.0 copy-start
  7.2 0.0 all-gather.5.cloned.1.call-start
  7.2 0.7 all-gather.5.cloned.1.call-update
  7.9 0.0 all-gather.7.cloned.1.call-start
  8.0 0.7 all-gather.7.cloned.1.call-update
  8.7 0.0 all-gather.11.cloned.1.call-start
  8.7 0.7 all-gather.11.cloned.1.call-update
  9.4 0.0 reduce-scatter.5.cloned.1.call-start
  9.4 102.1 %all-gather.5.cloned.1.call-done = bf16[640,1024]{1,0:T(8,128)(2,1)} async-done(((bf16[640,128]{1,0:T(8,128)(2,1)}), bf16[640,1024]{1,0:T(8,128)(2,1)}) %all-gather.5.cloned.1.call-update) | async-done | bytes 1310736 | tf_op jit(solution)/shard_map/all_gather | solution.py:16
  111.5 111.2 %all-gather.7.cloned.1.call-done = bf16[1024,1024]{1,0:T(8,128)(2,1)} async-done(((bf16[1024,128]{1,0:T(8,128)(2,1)}), bf16[1024,1024]{1,0:T(8,128)(2,1)}) %all-gather.7.cloned.1.call-update) | async-done | bytes 2097168 | tf_op jit(solution)/shard_map/all_gather | solution.py:17
  222.7 0.0 copy-done
  222.7 5.8 %fusion = bf16[640,1024]{0,1:T(8,128)(2,1)} fusion(bf16[640,640]{1,0:T(8,128)(2,1)S(1)} %copy-done, bf16[640,1024]{1,0:T(8,128)(2,1)} %all-gather.5.cloned.1.call-done, bf16[1024,1024]{1,0:T(8,128)(2,1)} %all-gather.7.cloned.1.call-done), kind=kOutput, calls=%fused_computation.4 | convolution fusion | flops 2182348800 | bytes 5537792 | tf_op jit(solution)/shard_map/dot_general | solution.py:28
  228.5 0.0 reduce-scatter.5.cloned.1.call-update
  228.5 23.1 %all-gather.11.cloned.1.call-done = bf16[5120,128]{1,0:T(8,128)(2,1)} async-done(((bf16[640,128]{1,0:T(8,128)(2,1)}), bf16[5120,128]{1,0:T(8,128)(2,1)}) %all-gather.11.cloned.1.call-update) | async-done | bytes 1310736 | tf_op jit(solution)/shard_map/all_gather | solution.py:43
  251.6 0.0 copy-start.4
  251.6 0.0 copy-start.5
  251.6 15.3 %all-to-all-start = ((bf16[8,640,128]{2,1,0:T(8,128)(2,1)}), bf16[8,640,128]{2,1,0:T(8,128)(2,1)S(1)}, u32[]{:S(2)}, u32[]{:S(2)}) async-start(bf16[8,640,128]{2,1,0:T(8,128)(2,1)} %bitcast.21), calls=%async_computation.1 | async-start | bytes 2621440 | tf_op jit(solution)/shard_map/all_to_all | solution.py:51
  266.9 0.0 all-gather.9.cloned.1.call-start
  266.9 0.0 copy-done.4
  266.9 0.2 copy.23
  267.0 0.0 copy-done.5
  267.1 0.0 copy-start.1
  267.1 0.9 copy.24
  268.0 27.4 %reduce-scatter.5.cloned.1.call-done = bf16[640,128]{0,1:T(8,128)(2,1)} async-done(((bf16[640,1024]{0,1:T(8,128)(2,1)}), bf16[640,128]{0,1:T(8,128)(2,1)}) %reduce-scatter.5.cloned.1.call-update) | async-done | bytes 163856 | tf_op jit(solution)/shard_map/reduce_scatter | solution.py:32
  295.3 1.9 divide_convert_fusion
  297.3 0.0 all-gather.9.cloned.1.call-update
  297.3 0.0 reduce-scatter.7.cloned.1.call-start
  297.4 0.0 copy-done.1
  297.4 1.7 fusion.2
  299.1 0.8 copy.28
  299.9 0.0 reduce-scatter.7.cloned.1.call-update
  300.0 0.0 all-reduce.2.cloned.1.call-start
  300.0 28.3 %all-gather.9.cloned.1.call-done = bf16[640,1024]{0,1:T(8,128)(2,1)} async-done(((bf16[640,128]{0,1:T(8,128)(2,1)}), bf16[640,1024]{0,1:T(8,128)(2,1)}) %all-gather.9.cloned.1.call-update) | async-done | bytes 1310736 | tf_op jit(solution)/shard_map/all_gather | solution.py:44
  328.3 3.7 fusion.1
  332.0 0.0 all-reduce.2.cloned.1.call-update
  332.0 37.9 %reduce-scatter.7.cloned.1.call-done = bf16[128,128]{1,0:T(8,128)(2,1)} async-done(((bf16[1024,128]{1,0:T(8,128)(2,1)}), bf16[128,128]{1,0:T(8,128)(2,1)}) %reduce-scatter.7.cloned.1.call-update) | async-done | bytes 32784
  369.9 0.9 copy.29
  370.8 0.6 convert_element_type.39
  371.4 0.9 copy.26
  372.3 0.9 copy.27
  373.2 0.0 all-to-all-done
  373.2 0.0 copy-start.2
  373.2 1.4 copy.25
  374.6 0.0 copy-done.2
  374.6 3.7 convolution_multiply_fusion
  378.3 180.1 %all-reduce.2.cloned.1.call-done = bf16[640,1024]{0,1:T(8,128)(2,1)} async-done(((bf16[640,1024]{0,1:T(8,128)(2,1)}), bf16[640,1024]{0,1:T(8,128)(2,1)}) %all-reduce.2.cloned.1.call-update) | async-done | bytes 1310736 | tf_op jit(solution)/shard_map/psum | solution.py:47
  558.4 0.0 copy-done.3
  558.4 2.5 convolution_convert_fusion.3
  (1 shorter events, 0.0 us)
Async XLA Ops:
  7.2 215.5 %copy-start = (bf16[640,640]{1,0:T(8,128)(2,1)S(1)}, bf16[640,640]{1,0:T(8,128)(2,1)}, u32[]{:S(2)}) copy-start(bf16[640,640]{1,0:T(8,128)(2,1)} %param.6) | copy-start | bytes 2457604
  7.2 104.3 %all-gather.5.cloned.1.call-start = ((), (), s32[]{:S(2)}) async-start(), calls=%async_computation.3 | async-start | bytes 1474560 | tf_op jit(solution)/shard_map/all_gather | solution.py:16
  7.9 214.8 %all-gather.7.cloned.1.call-start = ((), (), s32[]{:S(2)}) async-start(), calls=%async_computation.4 | async-start | bytes 2359296 | tf_op jit(solution)/shard_map/all_gather | solution.py:17
  8.7 242.9 %all-gather.11.cloned.1.call-start = ((), (), s32[]{:S(2)}) async-start(), calls=%async_computation.8 | async-start | bytes 1474560 | tf_op jit(solution)/shard_map/all_gather | solution.py:43
  9.4 285.9 %reduce-scatter.5.cloned.1.call-start = ((), (), s32[]{:S(2)}) async-start(), calls=%async_computation.5 | async-start | bytes 1474560 | tf_op jit(solution)/shard_map/reduce_scatter | solution.py:32
  251.6 15.3 %copy-start.4 = (f32[640,128]{1,0:T(8,128)S(1)}, f32[640,128]{1,0:T(8,128)}, u32[]{:S(2)}) copy-start(f32[640,128]{1,0:T(8,128)} %param.8) | copy-start | bytes 983044
  251.6 15.4 %copy-start.5 = (f32[640,128]{1,0:T(8,128)S(1)}, f32[640,128]{1,0:T(8,128)}, u32[]{:S(2)}) copy-start(f32[640,128]{1,0:T(8,128)} %param.9) | copy-start | bytes 983044
  251.6 121.6 %all-to-all-start = ((bf16[8,640,128]{2,1,0:T(8,128)(2,1)}), bf16[8,640,128]{2,1,0:T(8,128)(2,1)S(1)}, u32[]{:S(2)}, u32[]{:S(2)}) async-start(bf16[8,640,128]{2,1,0:T(8,128)(2,1)} %bitcast.21), calls=%async_computation.1 | async-start | bytes 2621440 | tf_op jit(solution)/shard_map/all_to_all | solution.py:51
  266.9 61.4 %all-gather.9.cloned.1.call-start = ((), (), s32[]{:S(2)}) async-start(), calls=%async_computation.6 | async-start | bytes 1474560 | tf_op jit(solution)/shard_map/all_gather | solution.py:44
  267.1 30.3 %copy-start.1 = (bf16[640,128]{1,0:T(8,128)(2,1)S(1)}, bf16[640,128]{1,0:T(8,128)(2,1)}, u32[]{:S(2)}) copy-start(bf16[640,128]{1,0:T(8,128)(2,1)} %param.5) | copy-start | bytes 491524
  297.3 72.6 %reduce-scatter.7.cloned.1.call-start = ((), (), s32[]{:S(2)}) async-start(), calls=%async_computation.9 | async-start | bytes 294912
  300.0 258.4 %all-reduce.2.cloned.1.call-start = ((), (), s32[]{:S(2)}) async-start(), calls=%async_computation.7 | async-start | bytes 2621440 | tf_op jit(solution)/shard_map/psum | solution.py:47
  373.2 1.4 copy-start.2
  374.6 183.8 %copy-start.3 = (bf16[1024,128]{1,0:T(8,128)(2,1)S(1)}, bf16[1024,128]{1,0:T(8,128)(2,1)}, u32[]{:S(2)}) copy-start(bf16[1024,128]{1,0:T(8,128)(2,1)} %param.7) | copy-start | bytes 786436
Sparse Core Ops, SparseCore 0:
  11.1 100.3 all-gather.4
  114.6 108.0 all-gather.6
  224.8 26.7 all-gather.10
  254.9 40.4 reduce-scatter.4
  297.9 30.3 all-gather.8
  331.5 38.3 reduce-scatter.6
  373.1 185.2 all-reduce.1
where the time goes:
time: 568 us
  waiting for transfers between devices  512 us (90%)
  matrix products  17.4 us (3%)
  starting transfers between devices  15.5 us (3%)
  between operations  14.2 us (2%)
  local copies, waits for them, and re-layouts  6 us (1%)
    psum x1, waiting for transfers between devices, body(): back_whole = lax.psum(back_terms.astype(jnp.bfloat16), 'col')  180 us
    all_gather x1, waiting for transfers between devices, body(): basis_piece = lax.all_gather(right_rows, 'col', axis=1, tiled=True)  111 us
    all_gather x1, waiting for transfers between devices, body(): grad_piece = lax.all_gather(grad, 'col', axis=1, tiled=True)  102 us
    unnamed x8, waiting for transfers between devices  40 us
    all_gather x1, waiting for transfers between devices, body(): lax.all_gather(direction, 'row', axis=1, tiled=True)  28.3 us
    reduce_scatter x1, waiting for transfers between devices, body(): lax.psum_scatter(left_terms.astype(jnp.bfloat16), 'row', scatter_dimensio...  27.4 us
    all_gather x1, waiting for transfers between devices, body(): lax.all_gather(grad, 'row', axis=0, tiled=True)  23.1 us
    all_to_all x1, starting transfers between devices, body(): lax.all_to_all(columns, 'col', split_axis=0, concat_axis=1, tiled=True)  15.3 us
  transfers between devices with their start and end apart: 8, of which 7 were waited for; matrix products, arithmetic and copies ran while one was open for 4% of the time, Pallas kernels for 0%

commit v1 on v0

v1 whole, which is shorter than its diff:
```python
import itertools

import jax
import jax.numpy as jnp
from jax import lax
from jax.sharding import Mesh, PartitionSpec as P

M = 5120
C = 1024

first_beta = 0.9
second_beta = 0.95
epsilon = 1e-08

SIZES = {"x": 4, "core": 2, "zh": 2, "y": 4}
ROW = ("x", "core")
f32 = jnp.float32
bf16 = jnp.bfloat16


def pairs(axes, target):
    found = []
    for place in itertools.product(*[range(SIZES[a]) for a in axes]):
        there = target(*place)
        if there is None:
            continue
        src = dst = 0
        for a, s, d in zip(axes, place, there):
            src, dst = src * SIZES[a] + s, dst * SIZES[a] + d
        found.append((src, dst))
    return found


def dot(a, b, over_a, over_b):
    return lax.dot_general(
        a, b, (((over_a,), (over_b,)), ((), ())), preferred_element_type=f32
    )


def lanes(blocks):
    return jnp.concatenate([blocks[k] for k in range(blocks.shape[0])], axis=1)


def other_core(value):
    return lax.ppermute(value, "core", [(0, 1), (1, 0)])


def other_half(value):
    return lax.ppermute(value, "zh", [(0, 1), (1, 0)])


def spread(value, axis):
    return lax.all_to_all(
        jnp.broadcast_to(value[None], (4,) + value.shape), axis, 0, 0, tiled=True
    )


def left_source(core):
    def target(x, c, z, y):
        if x // 2 != z:
            return None
        return (y, core, z, 2 * (x % 2) + c)

    return pairs(("x", "core", "zh", "y"), target)


def body(grad, left_basis, right_rows, exp_avg, exp_avg_sq):
    x, core = lax.axis_index("x"), lax.axis_index("core")
    z, y = lax.axis_index("zh"), lax.axis_index("y")
    row = 2 * x + core

    moments = lax.all_gather(
        jnp.concatenate([exp_avg, exp_avg_sq], axis=0).astype(bf16), ROW, axis=0
    )

    slab = lax.dynamic_slice_in_dim(right_rows, row * 128, 128, 0)
    mine = jnp.concatenate([grad, slab], axis=0)
    far = other_half(mine)

    near_all = spread(mine, "y")
    far_all = spread(far, "y")
    first = z == 0
    whole = jnp.concatenate(
        [
            lanes(jnp.where(first, near_all, far_all)),
            lanes(jnp.where(first, far_all, near_all)),
        ],
        axis=1,
    )
    panel, basis_slab = whole[:640], whole[640:]
    basis = lax.all_gather(basis_slab, ROW, axis=0, tiled=True)

    left = dot(left_basis, panel, 0, 0).astype(bf16)
    gram = (dot(grad, panel, 0, 0) * (1.0 / M)).astype(bf16)

    def for_core(t):
        cols = []
        for k in range(4):
            at = (2 * k + t) * 128
            cols += [gram[:64, at : at + 128], gram[64:, at : at + 128]]
        return jnp.concatenate(
            [left[320 * t : 320 * t + 320], jnp.concatenate(cols, axis=1)], axis=0
        )

    low, high = for_core(0), for_core(1)
    is_low = core == 0
    summed = jnp.where(is_low, low, high).astype(f32) + other_core(
        jnp.where(is_low, high, low)
    ).astype(f32)
    summed = summed.astype(bf16)
    summed = jnp.stack([summed[:, 256 * k : 256 * k + 256] for k in range(4)])
    summed = lax.all_to_all(summed, "x", 0, 0, tiled=True).astype(f32).sum(0)
    right_gram = jnp.concatenate([summed[320:, :128], summed[320:, 128:]], axis=0)
    half = lanes(spread(summed[:320].astype(bf16), "x"))

    rotated_half = dot(half, basis, 1, 1)
    old = lax.dynamic_slice_in_dim(moments, core * 320, 320, 1)
    old_sq = lax.dynamic_slice_in_dim(moments, 640 + core * 320, 320, 1)
    new = first_beta * lanes(old).astype(f32) + (1.0 - first_beta) * rotated_half
    new_sq = (
        second_beta * lanes(old_sq).astype(f32)
        + (1.0 - second_beta) * rotated_half * rotated_half
    )
    direction = (new / (jnp.sqrt(new_sq) + epsilon)).astype(bf16)
    turned = dot(direction, basis, 1, 0).astype(bf16)
    turned_far = other_core(turned)
    basis_swapped = jnp.where(
        is_low,
        left_basis,
        jnp.concatenate([left_basis[:, 320:], left_basis[:, :320]], axis=1),
    )
    back = dot(
        basis_swapped, jnp.concatenate([turned, turned_far], axis=0), 1, 0
    ).astype(bf16)
    back = jnp.stack(
        [
            jnp.concatenate(
                [back[:, 128 * k : 128 * k + 128], back[:, 512 + 128 * k : 640 + 128 * k]], axis=0
            )
            for k in range(4)
        ]
    )
    back = lax.all_to_all(back, "y", 0, 0, tiled=True).astype(f32).sum(0)
    keep = jnp.where(first, back[:640], back[640:])
    send = jnp.where(first, back[640:], back[:640]).astype(bf16)
    update = (keep + other_half(send).astype(f32)).astype(bf16)

    own = lax.dynamic_slice_in_dim(rotated_half, row * 128, 128, 1)
    theirs = lax.dynamic_slice_in_dim(rotated_half, (2 * x + 1 - core) * 128, 128, 1)
    theirs = other_core(theirs)
    rotated = jnp.where(
        is_low,
        jnp.concatenate([own, theirs], axis=0),
        jnp.concatenate([theirs, own], axis=0),
    )
    exp_avg_new = first_beta * exp_avg + (1.0 - first_beta) * rotated
    exp_avg_sq_new = second_beta * exp_avg_sq + (1.0 - second_beta) * rotated * rotated

    piece = lax.dynamic_slice_in_dim(panel, y * 256, 256, 1)
    axes = ("x", "core", "zh", "y")
    pair = lax.ppermute(piece[:, :128], axes, left_source(0)) + lax.ppermute(
        piece[:, 128:], axes, left_source(1)
    )
    paired = lanes(lax.all_gather(pair, ROW, axis=0))
    left_gram = dot(panel, paired, 1, 1) * (1.0 / C)
    return (update, exp_avg_new, exp_avg_sq_new, left_gram, right_gram)


def solution(mesh):
    wide = Mesh(
        mesh.devices.reshape(8, 4, 2, 2, 4), ("layer", "x", "core", "zh", "y")
    )
    row, col = ("x", "core"), ("zh", "y")
    return jax.shard_map(
        body,
        mesh=wide,
        in_specs=(
            P(("layer",) + row, col),
            P(("layer",) + row, col),
            P("layer", col),
            P(("layer",) + col, row),
            P(("layer",) + col, row),
        ),
        out_specs=(
            P(("layer",) + row, col),
            P(("layer",) + col, row),
            P(("layer",) + col, row),
            P(("layer",) + row, col),
            P(("layer",) + col, row),
        ),
        check_vma=False,
    )
```

time: 568 us -> 246 us (0.43)
  the two profiles are of different devices: /device:TPU:24 before, /device:TPU:193 now
where the time goes in v1:
time: 246 us; the launch traced here: 244 us
  waiting for transfers between devices  113 us (46%)
  starting transfers between devices  47.7 us (19%)
  local copies, waits for them, and re-layouts  30.4 us (12%)
  blocking collectives  18.4 us (7%)
  between operations  14.3 us (6%)
  matrix products  13.3 us (5%)
  other arithmetic  7.29 us (3%)
    ppermute x2, waiting for transfers between devices, other_half(): return lax.ppermute(value, 'zh', [(0, 1), (1, 0)])  38.9 us
    all_gather x1, waiting for transfers between devices, body(): paired = lanes(lax.all_gather(pair, ROW, axis=0))  20.2 us
    unnamed x48, local copies, waits for them, and re-layouts  20 us
    all_gather x1, waiting for transfers between devices, body(): lax.all_gather(jnp.concatenate([exp_avg, exp_avg_sq], axis=0).astype(bf16...  19.4 us
    all_to_all x3, waiting for transfers between devices, spread(): lax.all_to_all(jnp.broadcast_to(value[None], (4,) + value.shape), axis, 0...  18.9 us
    all_to_all x1, blocking collectives, body(): summed = lax.all_to_all(summed, 'x', 0, 0, tiled=True).astype(f32).sum(0)  18.4 us
    ppermute x2, starting transfers between devices, other_half(): return lax.ppermute(value, 'zh', [(0, 1), (1, 0)])  14.9 us
    dot_general x6, matrix products, dot(): lax.dot_general(a, b, (((over_a,), (over_b,)), ((), ())), preferred_eleme...  13.3 us
  transfers between devices with their start and end apart: 14, of which 11 were waited for; matrix products, arithmetic and copies ran while one was open for 14% of the time, Pallas kernels for 0%

profile of v1, /device:TPU:193, one launch (start us, length us, event | category | flops | bytes accessed | tf_op | source)
XLA Modules:
  0.0 244.4 jit_solution(3973388508982573506)
XLA Ops:
  9.1 1.0 broadcast_in_dim.6
  10.0 4.2 %all-to-all-start = ((bf16[4,768,128]{2,1,0:T(8,128)(2,1)}), bf16[4,768,128]{2,1,0:T(8,128)(2,1)S(1)}, u32[]{:S(2)}, u32[]{:S(2)}) async-start(bf16[4,768,128]{2,1,0:T(8,128)(2,1)} %broadcast_in_dim.6), calls=%async_computation | async-start | bytes 1572864 | tf_op jit(solution)/shard_map/all_to_all | solution.py:53
  14.2 8.8 %collective-permute-start = (bf16[768,128]{1,0:T(8,128)(2,1)S(1)}, bf16[768,128]{1,0:T(8,128)(2,1)S(1)}, u32[]{:S(2)}, u32[]{:S(2)}) collective-permute-start(bf16[768,128]{1,0:T(8,128)(2,1)S(1)} %pad_maximum_fusion.5), channel_id=1, source_target_pairs={{0,4},{4,0},{1,5},{5,1},{2,6},{6,2},{3,7},{7,3},{8,12},{12,8},{9,1... | collective-permute-start | bytes 589832 | tf_op jit(solution)/shard_map/ppermute | solution.py:49
  23.1 20.3 %collective-permute-done = bf16[768,128]{1,0:T(8,128)(2,1)S(1)} collective-permute-done((bf16[768,128]{1,0:T(8,128)(2,1)S(1)}, bf16[768,128]{1,0:T(8,128)(2,1)S(1)}, u32[]{:S(2)}, u32[]{:S(2)}) %collective-permute-start) | collective-permute-done | bytes 196640 | tf_op jit(solution)/shard_map/ppermute | solution.py:49
  43.4 1.0 broadcast_in_dim.7
  44.4 4.2 %all-to-all-start.1 = ((bf16[4,768,128]{2,1,0:T(8,128)(2,1)}), bf16[4,768,128]{2,1,0:T(8,128)(2,1)S(1)}, u32[]{:S(2)}, u32[]{:S(2)}) async-start(bf16[4,768,128]{2,1,0:T(8,128)(2,1)} %broadcast_in_dim.7), calls=%async_computation.1 | async-start | bytes 1572864 | tf_op jit(solution)/shard_map/all_to_all | solution.py:53
  48.6 11.3 %all-to-all-done.1 = bf16[4,768,128]{2,1,0:T(8,128)(2,1)S(1)} async-done(((bf16[4,768,128]{2,1,0:T(8,128)(2,1)}), bf16[4,768,128]{2,1,0:T(8,128)(2,1)S(1)}, u32[]{:S(2)}, u32[]{:S(2)}) %all-to-all-start.1) | async-done | bytes 786464 | tf_op jit(solution)/shard_map/all_to_all | solution.py:53
  62.4 1.2 fusion
  64.0 3.8 %collective-permute-start.1 = (bf16[384,1024]{1,0:T(8,128)(2,1)S(1)}, bf16[384,1024]{1,0:T(8,128)(2,1)S(1)}, u32[]{:S(2)}, u32[]{:S(2)}) collective-permute-start(bf16[384,1024]{1,0:T(8,128)(2,1)S(1)} %broadcast_select_fusion.2), channel_id=1, source_target_pairs={{0,8},{8,0},{1,9},{9,1},{2,10},{10,2},{3,11},{11,3},{4,12},{12,4},... | collective-permute-start | bytes 2359304 | tf_op jit(solution)/shard_map/ppermute | solution.py:45
  67.8 1.9 collective-permute-done.1
  70.4 18.4 %all_to_all.25 = bf16[4,384,256]{2,1,0:T(8,128)(2,1)S(1)} all-to-all(bf16[4,384,256]{2,1,0:T(8,128)(2,1)S(1)} %pad_maximum_fusion.3), channel_id=1, replica_groups=mesh['layer'=8,'x'=4,'core'=2,'zh'=2,'y'=4] {'x'}, dimensions={0} | all-to-all | bytes 1572864 | tf_op jit(solution)/shard_map/all_to_all | solution.py:112
  90.5 3.5 %all-to-all-start.3 = ((bf16[4,320,256]{2,1,0:T(8,128)(2,1)}), bf16[4,320,256]{2,1,0:T(8,128)(2,1)S(1)}, u32[]{:S(2)}, u32[]{:S(2)}) async-start(bf16[4,320,256]{2,1,0:T(8,128)(2,1)} %broadcast_in_dim.8), calls=%async_computation.3 | async-start | bytes 1310720 | tf_op jit(solution)/shard_map/all_to_all | solution.py:53
  94.0 7.5 %all-to-all-done.3 = bf16[4,320,256]{2,1,0:T(8,128)(2,1)S(1)} async-done(((bf16[4,320,256]{2,1,0:T(8,128)(2,1)}), bf16[4,320,256]{2,1,0:T(8,128)(2,1)S(1)}, u32[]{:S(2)}, u32[]{:S(2)}) %all-to-all-start.3) | async-done | bytes 655392 | tf_op jit(solution)/shard_map/all_to_all | solution.py:53
  102.4 2.8 %fusion.15 = f32[320,1024]{1,0:T(8,128)S(1)} fusion(bf16[1024,1024]{1,0:T(8,128)(2,1)} %all-gather.7.cloned.1.call-done, bf16[320,256]{1,0:T(8,128)(2,1)} %get-tuple-element.42, bf16[320,256]{1,0:T(8,128)(2,1)} %get-tuple-element.43, bf16[320,256]{1,0:T(8,128)(2,1)} %get-tuple-element.44, bf16[320,256]{1,0:T(8,128)(2,1)S(1)} %get-tuple-element.41), kind=kOutput, calls=%fused_computation.31 | convolution fusion | flops 673710080 | bytes 4063232 | tf_op jit(solution)/shard_map/dot_general | solution.py:35
  105.2 7.0 %collective-permute-start.4 = (f32[320,128]{1,0:T(8,128)S(1)}, f32[320,128]{1,0:T(8,128)S(1)}, u32[]{:S(2)}, u32[]{:S(2)}) collective-permute-start(f32[320,128]{1,0:T(8,128)S(1)} %get-tuple-element.23), channel_id=1, source_target_pairs={{0,8},{8,0},{1,9},{9,1},{2,10},{10,2},{3,11},{11,3},{4,12},{12,4},... | collective-permute-start | bytes 491528 | tf_op jit(solution)/shard_map/ppermute | solution.py:45
  112.3 1.0 collective-permute-done.4
  113.3 1.0 fusion.28
  115.3 1.6 collective-permute-start.5
  116.9 2.2 collective-permute-start.6
  119.8 2.8 %collective-permute-done.6 = bf16[640,128]{1,0:T(8,128)(2,1)S(1)} collective-permute-done((bf16[640,128]{1,0:T(8,128)(2,1)S(1)}, bf16[640,128]{1,0:T(8,128)(2,1)S(1)}, u32[]{:S(2)}, u32[]{:S(2)}) %collective-permute-start.6) | collective-permute-done | bytes 163872 | tf_op jit(solution)/shard_map/ppermute | solution.py:161
  123.3 1.0 fusion.49
  125.8 19.4 %all-gather.5.cloned.1.call-done = bf16[8,1280,128]{2,1,0:T(8,128)(2,1)} async-done(((bf16[1,1280,128]{2,1,0:T(8,128)(2,1)}), bf16[8,1280,128]{2,1,0:T(8,128)(2,1)}) %all-gather.5.cloned.1.call-update) | async-done | bytes 2621456 | tf_op jit(solution)/shard_map/all_gather | solution.py:72
  145.1 1.0 constant_dynamic-update-slice_fusion.7
  146.1 1.0 constant_dynamic-update-slice_fusion.6
  147.1 1.0 constant_dynamic-update-slice_fusion.5
  148.1 1.0 constant_dynamic-update-slice_fusion.4
  149.1 1.0 constant_dynamic-update-slice_fusion.3
  150.1 1.0 constant_dynamic-update-slice_fusion.2
  151.1 1.0 constant_dynamic-update-slice_fusion.1
  152.1 1.0 constant_dynamic-update-slice_fusion
  154.0 3.8 %convolution_convert_fusion.2 = bf16[320,1024]{1,0:T(8,128)(2,1)} fusion(bf16[1024,1024]{1,0:T(8,128)(2,1)} %all-gather.7.cloned.1.call-done, f32[320,1024]{1,0:T(8,128)S(1)} %copy-done.7, bf16[320,1024]{1,0:T(8,128)(2,1)S(1)} %constant_dynamic-update-slice_fusion.24, bf16[320,1024]{1,0:T(8,128)(2,1)S(1)} %get-tuple-element.5), kind=kOutput, calls=%fused_computation.8 | convolution fusion | flops 675348480 | bytes 5373952 | tf_op jit(solution)/shard_map/dot_general | solution.py:35
  157.8 2.2 collective-permute-start.2
  160.0 20.2 %all-gather.9.cloned.1.call-done = bf16[5120,128]{1,0:T(8,128)(2,1)} async-done(((bf16[640,128]{1,0:T(8,128)(2,1)}), bf16[5120,128]{1,0:T(8,128)(2,1)}) %all-gather.9.cloned.1.call-update) | async-done | bytes 1310736 | tf_op jit(solution)/shard_map/all_gather | solution.py:164
  181.2 1.0 slice_dynamic-update-slice_fusion.6
  182.1 1.0 slice_dynamic-update-slice_fusion.5
  183.1 1.1 copy-done.8
  184.2 2.6 %convolution_convert_fusion = bf16[640,1024]{1,0:T(8,128)(2,1)S(1)} fusion(bf16[320,1024]{1,0:T(8,128)(2,1)} %collective-permute-done.2, bf16[320,1024]{1,0:T(8,128)(2,1)} %convolution_convert_fusion.2, bf16[640,640]{1,0:T(8,128)(2,1)S(1)} %copy-done.1, bf16[640,320]{1,0:T(8,128)(2,1)} %get-tuple-element.36, bf16[640,320]{1,0:T(8,128)(2,1)S(1)} %get-tuple-element.35, ...), kind=kOutput, calls=%fused_computation.2 | convolution fusion | flops 844185600 | bytes 4259841 | tf_op jit(solution)/shard_map/dot_general | solution.py:35
  187.2 1.2 pad_maximum_fusion
  188.4 4.0 %all-to-all-start.4 = ((bf16[4,1280,128]{2,1,0:T(8,128)(2,1)}), bf16[4,1280,128]{2,1,0:T(8,128)(2,1)S(1)}, u32[]{:S(2)}, u32[]{:S(2)}) async-start(bf16[4,1280,128]{2,1,0:T(8,128)(2,1)} %pad_maximum_fusion), calls=%async_computation.4 | async-start | bytes 2621440 | tf_op jit(solution)/shard_map/all_to_all | solution.py:143
  192.4 1.6 slice_dynamic-update-slice_fusion.4
  194.1 1.6 slice_dynamic-update-slice_fusion.3
  195.7 1.6 slice_dynamic-update-slice_fusion.2
  197.3 1.6 slice_dynamic-update-slice_fusion.1
  198.9 1.6 slice_dynamic-update-slice_fusion
  200.6 9.4 %all-to-all-done.4 = bf16[4,1280,128]{2,1,0:T(8,128)(2,1)S(1)} async-done(((bf16[4,1280,128]{2,1,0:T(8,128)(2,1)}), bf16[4,1280,128]{2,1,0:T(8,128)(2,1)S(1)}, u32[]{:S(2)}, u32[]{:S(2)}) %all-to-all-start.4) | async-done | bytes 1310752 | tf_op jit(solution)/shard_map/all_to_all | solution.py:143
  210.1 6.1 %collective-permute-start.3 = (bf16[640,128]{1,0:T(8,128)(2,1)S(1)}, bf16[640,128]{1,0:T(8,128)(2,1)S(1)}, u32[]{:S(2)}, u32[]{:S(2)}) collective-permute-start(bf16[640,128]{1,0:T(8,128)(2,1)S(1)} %select_convert_fusion), channel_id=1, source_target_pairs={{0,4},{4,0},{1,5},{5,1},{2,6},{6,2},{3,7},{7,3},{8,12},{12,8},{9,1... | collective-permute-start | bytes 491528 | tf_op jit(solution)/shard_map/ppermute | solution.py:49
  216.2 2.4 convolution_multiply_fusion
  218.6 18.5 %collective-permute-done.3 = bf16[640,128]{1,0:T(8,128)(2,1)S(1)} collective-permute-done((bf16[640,128]{1,0:T(8,128)(2,1)S(1)}, bf16[640,128]{1,0:T(8,128)(2,1)S(1)}, u32[]{:S(2)}, u32[]{:S(2)}) %collective-permute-start.3) | collective-permute-done | bytes 163872 | tf_op jit(solution)/shard_map/ppermute | solution.py:49
  (74 shorter events, 14.8 us)
Async XLA Ops:
  7.2 1.0 copy-start
  10.0 33.3 %all-to-all-start = ((bf16[4,768,128]{2,1,0:T(8,128)(2,1)}), bf16[4,768,128]{2,1,0:T(8,128)(2,1)S(1)}, u32[]{:S(2)}, u32[]{:S(2)}) async-start(bf16[4,768,128]{2,1,0:T(8,128)(2,1)} %broadcast_in_dim.6), calls=%async_computation | async-start | bytes 1572864 | tf_op jit(solution)/shard_map/all_to_all | solution.py:53
  14.2 29.1 %collective-permute-start = (bf16[768,128]{1,0:T(8,128)(2,1)S(1)}, bf16[768,128]{1,0:T(8,128)(2,1)S(1)}, u32[]{:S(2)}, u32[]{:S(2)}) collective-permute-start(bf16[768,128]{1,0:T(8,128)(2,1)S(1)} %pad_maximum_fusion.5), channel_id=1, source_target_pairs={{0,4},{4,0},{1,5},{5,1},{2,6},{6,2},{3,7},{7,3},{8,12},{12,8},{9,1... | collective-permute-start | bytes 589832 | tf_op jit(solution)/shard_map/ppermute | solution.py:49
  44.4 15.6 %all-to-all-start.1 = ((bf16[4,768,128]{2,1,0:T(8,128)(2,1)}), bf16[4,768,128]{2,1,0:T(8,128)(2,1)S(1)}, u32[]{:S(2)}, u32[]{:S(2)}) async-start(bf16[4,768,128]{2,1,0:T(8,128)(2,1)} %broadcast_in_dim.7), calls=%async_computation.1 | async-start | bytes 1572864 | tf_op jit(solution)/shard_map/all_to_all | solution.py:53
  48.6 53.8 %all-gather.7.cloned.1.call-start = ((), (), s32[]{:S(2)}) async-start(), calls=%async_computation.6 | async-start | bytes 2359296 | tf_op jit(solution)/shard_map/all_gather | solution.py:91
  60.1 0.9 copy-start.5
  61.0 1.3 copy-start.1
  64.0 5.7 %collective-permute-start.1 = (bf16[384,1024]{1,0:T(8,128)(2,1)S(1)}, bf16[384,1024]{1,0:T(8,128)(2,1)S(1)}, u32[]{:S(2)}, u32[]{:S(2)}) collective-permute-start(bf16[384,1024]{1,0:T(8,128)(2,1)S(1)} %broadcast_select_fusion.2), channel_id=1, source_target_pairs={{0,8},{8,0},{1,9},{9,1},{2,10},{10,2},{3,11},{11,3},{4,12},{12,4},... | collective-permute-start | bytes 2359304 | tf_op jit(solution)/shard_map/ppermute | solution.py:45
  88.8 0.7 copy-start.2
  90.5 11.1 %all-to-all-start.3 = ((bf16[4,320,256]{2,1,0:T(8,128)(2,1)}), bf16[4,320,256]{2,1,0:T(8,128)(2,1)S(1)}, u32[]{:S(2)}, u32[]{:S(2)}) async-start(bf16[4,320,256]{2,1,0:T(8,128)(2,1)} %broadcast_in_dim.8), calls=%async_computation.3 | async-start | bytes 1310720 | tf_op jit(solution)/shard_map/all_to_all | solution.py:53
  94.0 51.1 %all-gather.5.cloned.1.call-start = ((), (), s32[]{:S(2)}) async-start(), calls=%async_computation.5 | async-start | bytes 2949120 | tf_op jit(solution)/shard_map/all_gather | solution.py:72
  102.4 10.9 %copy-start.3 = (f32[640,128]{1,0:T(8,128)S(1)}, f32[640,128]{1,0:T(8,128)}, u32[]{:S(2)}) copy-start(f32[640,128]{1,0:T(8,128)} %param.9) | copy-start | bytes 983044
  102.4 10.9 %copy-start.4 = (f32[640,128]{1,0:T(8,128)S(1)}, f32[640,128]{1,0:T(8,128)}, u32[]{:S(2)}) copy-start(f32[640,128]{1,0:T(8,128)} %param.8) | copy-start | bytes 983044
  105.2 9.1 %copy-start.6 = (f32[320,1024]{1,0:T(8,128)}, f32[320,1024]{1,0:T(8,128)S(1)}, u32[]{:S(2)}) copy-start(f32[320,1024]{1,0:T(8,128)S(1)} %fusion.15) | copy-start | bytes 3932164
  105.2 8.0 %collective-permute-start.4 = (f32[320,128]{1,0:T(8,128)S(1)}, f32[320,128]{1,0:T(8,128)S(1)}, u32[]{:S(2)}, u32[]{:S(2)}) collective-permute-start(f32[320,128]{1,0:T(8,128)S(1)} %get-tuple-element.23), channel_id=1, source_target_pairs={{0,8},{8,0},{1,9},{9,1},{2,10},{10,2},{3,11},{11,3},{4,12},{12,4},... | collective-permute-start | bytes 491528 | tf_op jit(solution)/shard_map/ppermute | solution.py:45
  115.0 65.2 %all-gather.9.cloned.1.call-start = ((), (), s32[]{:S(2)}) async-start(), calls=%async_computation.7 | async-start | bytes 1474560 | tf_op jit(solution)/shard_map/all_gather | solution.py:164
  115.3 4.5 %collective-permute-start.5 = (bf16[640,128]{1,0:T(8,128)(2,1)S(1)}, bf16[640,128]{1,0:T(8,128)(2,1)S(1)}, u32[]{:S(2)}, u32[]{:S(2)}) collective-permute-start(bf16[640,128]{1,0:T(8,128)(2,1)S(1)} %get-tuple-element.22), channel_id=1, source_target_pairs={{0,0},{1,16},{2,32},{3,48},{8,1},{9,17},{10,33},{11,49},{16,2},{17... | collective-permute-start | bytes 491528 | tf_op jit(solution)/shard_map/ppermute | solution.py:161
  116.9 5.7 %collective-permute-start.6 = (bf16[640,128]{1,0:T(8,128)(2,1)S(1)}, bf16[640,128]{1,0:T(8,128)(2,1)S(1)}, u32[]{:S(2)}, u32[]{:S(2)}) collective-permute-start(bf16[640,128]{1,0:T(8,128)(2,1)S(1)} %get-tuple-element.21), channel_id=1, source_target_pairs={{0,8},{1,24},{2,40},{3,56},{8,9},{9,25},{10,41},{11,57},{16,10},{1... | collective-permute-start | bytes 491528 | tf_op jit(solution)/shard_map/ppermute | solution.py:161
  145.1 8.9 %copy-start.7 = (f32[320,1024]{1,0:T(8,128)S(1)}, f32[320,1024]{1,0:T(8,128)}, u32[]{:S(2)}) copy-start(f32[320,1024]{1,0:T(8,128)} %copy-done.6) | copy-start | bytes 3932164
  157.8 25.3 %collective-permute-start.2 = (bf16[320,1024]{1,0:T(8,128)(2,1)}, bf16[320,1024]{1,0:T(8,128)(2,1)}, u32[]{:S(2)}, u32[]{:S(2)}) collective-permute-start(bf16[320,1024]{1,0:T(8,128)(2,1)} %convolution_convert_fusion.2), channel_id=1, source_target_pairs={{0,8},{8,0},{1,9},{9,1},{2,10},{10,2},{3,11},{11,3},{4,12},{12,4},... | collective-permute-start | bytes 1966088 | tf_op jit(solution)/shard_map/ppermute | solution.py:45
  183.1 1.1 copy-start.8
  188.4 21.5 %all-to-all-start.4 = ((bf16[4,1280,128]{2,1,0:T(8,128)(2,1)}), bf16[4,1280,128]{2,1,0:T(8,128)(2,1)S(1)}, u32[]{:S(2)}, u32[]{:S(2)}) async-start(bf16[4,1280,128]{2,1,0:T(8,128)(2,1)} %pad_maximum_fusion), calls=%async_computation.4 | async-start | bytes 2621440 | tf_op jit(solution)/shard_map/all_to_all | solution.py:143
  209.9 6.3 %copy-start.9 = (bf16[640,1024]{1,0:T(8,128)(2,1)S(1)}, bf16[640,1024]{1,0:T(8,128)(2,1)}, u32[]{:S(2)}) copy-start(bf16[640,1024]{1,0:T(8,128)(2,1)} %slice_dynamic-update-slice_fusion) | copy-start | bytes 3932164
  210.1 27.0 %collective-permute-start.3 = (bf16[640,128]{1,0:T(8,128)(2,1)S(1)}, bf16[640,128]{1,0:T(8,128)(2,1)S(1)}, u32[]{:S(2)}, u32[]{:S(2)}) collective-permute-start(bf16[640,128]{1,0:T(8,128)(2,1)S(1)} %select_convert_fusion), channel_id=1, source_target_pairs={{0,4},{4,0},{1,5},{5,1},{2,6},{6,2},{3,7},{7,3},{8,12},{12,8},{9,1... | collective-permute-start | bytes 491528 | tf_op jit(solution)/shard_map/ppermute | solution.py:49
Sparse Core Ops, SparseCore 0:
  62.3 34.8 all-gather.6
  115.1 29.9 all-gather.4
  147.8 32.3 all-gather.8

commit v2 on v1

v2 whole, which is shorter than its diff:
```python
import itertools

import jax
import jax.numpy as jnp
from jax import lax
from jax.experimental import pallas as pl
from jax.experimental.pallas import tpu as pltpu
from jax.sharding import Mesh, PartitionSpec as P

M = 5120
C = 1024

first_beta = 0.9
second_beta = 0.95
epsilon = 1e-08

SIZES = {"x": 4, "core": 2, "zh": 2, "y": 4}
ROW = ("x", "core")
f32 = jnp.float32
bf16 = jnp.bfloat16


def pairs(axes, target):
    found = []
    for place in itertools.product(*[range(SIZES[a]) for a in axes]):
        there = target(*place)
        if there is None:
            continue
        src = dst = 0
        for a, s, d in zip(axes, place, there):
            src, dst = src * SIZES[a] + s, dst * SIZES[a] + d
        found.append((src, dst))
    return found


def dot(a, b, over_a, over_b):
    return lax.dot_general(
        a, b, (((over_a,), (over_b,)), ((), ())), preferred_element_type=f32
    )


def other_core(value):
    return lax.ppermute(value, "core", [(0, 1), (1, 0)])


def other_half(value):
    return lax.ppermute(value, "zh", [(0, 1), (1, 0)])


def spread(value, axis):
    return lax.all_to_all(
        jnp.broadcast_to(value[None], (4,) + value.shape), axis, 0, 0, tiled=True
    )


def left_source(core):
    def target(x, c, z, y):
        if x // 2 != z:
            return None
        return (y, core, z, 2 * (x % 2) + c)

    return pairs(("x", "core", "zh", "y"), target)


def shaped(shape, dtype):
    return jax.ShapeDtypeStruct(shape, dtype)


def call(kernel, outs, where, *operands, after=(), scratch=(), flops=0, moved=0):
    n = len(operands)

    def inner(*refs):
        kernel(*refs[: n + 1], *refs[n + 1 + len(after) :])

    return pl.pallas_call(
        inner,
        out_shape=outs,
        in_specs=[pl.BlockSpec(memory_space=pltpu.SMEM)]
        + [pl.BlockSpec(memory_space=pltpu.VMEM)] * n
        + [pl.BlockSpec(memory_space=pl.ANY)] * len(after),
        scratch_shapes=scratch,
        compiler_params=pltpu.CompilerParams(vmem_limit_bytes=40 * 1024 * 1024),
        cost_estimate=pl.CostEstimate(
            flops=flops, bytes_accessed=moved, transcendentals=0
        ),
    )(where, *operands, *after)


def first_kernel(where, grad, right, mine, four):
    at = pl.multiple_of(where[0] * 128, 128)
    slab = right[pl.ds(at, 128)]
    mine[:640] = grad[...]
    mine[640:] = slab
    for k in range(4):
        four[k, :640] = grad[...]
        four[k, 640:] = slab


def four_kernel(where, value, four):
    for k in range(4):
        four[k] = value[...]


def basis_kernel(where, near, far, out):
    for k in range(4):
        out[:, 128 * k : 128 * k + 128] = near[k, 640:]
        out[:, 512 + 128 * k : 640 + 128 * k] = far[k, 640:]


def left_kernel(where, near, far, grad, left, keep, send, panel):
    core, z = where[1], where[2]
    for k in range(4):
        panel[:, 128 * k : 128 * k + 128] = near[k, :640, :]
        panel[:, 512 + 128 * k : 640 + 128 * k] = far[k, :640, :]

    product = dot(left[...], panel[...], 0, 0).astype(bf16)
    gram = (dot(grad[...], panel[...], 0, 0) * (1.0 / M)).astype(bf16)

    def columns(t, flip):
        found = []
        for k in range(4):
            block = 2 * k + t
            if flip:
                block = (block + 4) % 8
            at = block * 128
            found += [gram[:64, at : at + 128], gram[64:, at : at + 128]]
        return jnp.concatenate(found, axis=1)

    for c in range(2):

        @pl.when(core == c)
        def _():
            keep[:320] = product[320 * c : 320 * c + 320]
            send[:320] = product[320 * (1 - c) : 320 * (1 - c) + 320]
            for half in range(2):

                @pl.when(z == half)
                def _():
                    keep[320:] = columns(c, half == 1)
                    send[320:] = columns(1 - c, half == 1)


def join_kernel(where, first, second, four):
    for k in range(4):
        at = slice(256 * k, 256 * k + 256)
        four[k] = (first[:, at].astype(f32) + second[:, at].astype(f32)).astype(bf16)


def sum_kernel(where, parts, rows, gram):
    total = (
        parts[0].astype(f32)
        + parts[1].astype(f32)
        + parts[2].astype(f32)
        + parts[3].astype(f32)
    )
    mine = total[:320].astype(bf16)
    for k in range(4):
        rows[k] = mine
    gram[:64] = total[320:, :128]
    gram[64:] = total[320:, 128:]


def turn_kernel(where, half, basis, moments, out, own, theirs, rows, rotated):
    row, core = where[0], where[1]
    for k in range(4):
        rows[:, 256 * k : 256 * k + 256] = half[k]
    rotated[...] = dot(rows[...], basis[...], 1, 1)
    at = pl.multiple_of(core * 320, 320)
    for i in range(8):
        turned = rotated[:, 128 * i : 128 * i + 128]
        old = moments[i, 0, pl.ds(at, 320)].astype(f32)
        old_sq = moments[i, 1, pl.ds(at, 320)].astype(f32)
        new = first_beta * old + (1.0 - first_beta) * turned
        new_sq = second_beta * old_sq + (1.0 - second_beta) * turned * turned
        rows[:, 128 * i : 128 * i + 128] = (new / (jnp.sqrt(new_sq) + epsilon)).astype(bf16)
    out[...] = dot(rows[...], basis[...], 1, 0).astype(bf16)
    own[...] = rotated[:, pl.ds(pl.multiple_of(row * 128, 128), 128)]
    next_row = row + 1 - 2 * core
    theirs[...] = rotated[:, pl.ds(pl.multiple_of(next_row * 128, 128), 128)]


def back_kernel(where, left, mine, other, top, bottom, joined):
    core = where[1]
    joined[pl.ds(pl.multiple_of(core * 320, 320), 320)] = mine[...]
    joined[pl.ds(pl.multiple_of(320 - core * 320, 320), 320)] = other[...]
    for out, at in ((top, 0), (bottom, 320)):
        product = dot(left[at : at + 320, :], joined[...], 1, 0).astype(bf16)
        for k in range(4):
            out[k, :320] = product[:, 128 * k : 128 * k + 128]
            out[k, 320:] = product[:, 512 + 128 * k : 640 + 128 * k]


def gram_kernel(where, near, far, paired, out, panel, other):
    for k in range(4):
        panel[:, 128 * k : 128 * k + 128] = near[k, :640, :]
        panel[:, 512 + 128 * k : 640 + 128 * k] = far[k, :640, :]
    for k in range(8):
        other[:, 128 * k : 128 * k + 128] = paired[k]
    out[...] = dot(panel[...], other[...], 1, 1) * (1.0 / C)


def body(grad, left_basis, right_rows, exp_avg, exp_avg_sq):
    x, core = lax.axis_index("x"), lax.axis_index("core")
    z, y = lax.axis_index("zh"), lax.axis_index("y")
    row = 2 * x + core
    where = jnp.stack([row, core, z, y]).astype(jnp.int32)
    is_low = core == 0

    mine, four = call(
        first_kernel,
        [shaped((768, 128), bf16), shaped((4, 768, 128), bf16)],
        where,
        grad,
        right_rows,
        moved=1_500_000,
    )
    far = other_half(mine)
    near_all = lax.all_to_all(four, "y", 0, 0, tiled=True)

    moments = lax.all_gather(
        jnp.stack([exp_avg, exp_avg_sq]).astype(bf16), ROW, axis=0
    )

    far_four = call(
        four_kernel, shaped((4, 768, 128), bf16), where, far, moved=1_000_000
    )
    far_all = lax.all_to_all(far_four, "y", 0, 0, tiled=True)
    slabs = call(
        basis_kernel,
        shaped((128, 1024), bf16),
        where,
        near_all,
        far_all,
        moved=1_800_000,
    )
    basis = lax.all_gather(slabs, ROW, axis=0, tiled=True)

    keep, send = call(
        left_kernel,
        [shaped((384, 1024), bf16)] * 2,
        where,
        near_all,
        far_all,
        grad,
        left_basis,
        after=(moments,),
        scratch=[pltpu.VMEM((640, 1024), bf16)],
        flops=1_000_000_000,
        moved=5_000_000,
    )
    summed = call(
        join_kernel,
        shaped((4, 384, 256), bf16),
        where,
        keep,
        other_core(send),
        moved=2_400_000,
    )
    summed = lax.all_to_all(summed, "x", 0, 0, tiled=True)
    rows, right_gram = call(
        sum_kernel,
        [shaped((4, 320, 256), bf16), shaped((128, 128), f32)],
        where,
        summed,
        moved=1_500_000,
    )
    half = lax.all_to_all(rows, "x", 0, 0, tiled=True)

    turned, own, theirs = call(
        turn_kernel,
        [shaped((320, 1024), bf16), shaped((320, 128), f32), shaped((320, 128), f32)],
        where,
        half,
        basis,
        moments,
        scratch=[
            pltpu.VMEM((320, 1024), bf16),
            pltpu.VMEM((320, 1024), f32),
        ],
        flops=1_400_000_000,
        moved=6_000_000,
    )
    top, bottom = call(
        back_kernel,
        [shaped((4, 640, 128), bf16)] * 2,
        where,
        left_basis,
        turned,
        other_core(turned),
        scratch=[pltpu.VMEM((640, 1024), bf16)],
        flops=840_000_000,
        moved=4_000_000,
    )
    top = lax.all_to_all(top, "y", 0, 0, tiled=True)
    bottom = lax.all_to_all(bottom, "y", 0, 0, tiled=True)
    updates = []
    for part in (top, bottom):
        part = part.astype(f32).sum(0)
        arrived = other_half(part[320:].astype(bf16))
        updates.append((part[:320] + arrived.astype(f32)).astype(bf16))
    update = jnp.concatenate(updates, axis=0)

    theirs = other_core(theirs)
    rotated = jnp.where(
        is_low,
        jnp.concatenate([own, theirs], axis=0),
        jnp.concatenate([theirs, own], axis=0),
    )
    exp_avg_new = first_beta * exp_avg + (1.0 - first_beta) * rotated
    exp_avg_sq_new = second_beta * exp_avg_sq + (1.0 - second_beta) * rotated * rotated

    axes = ("x", "core", "zh", "y")
    at = 2 * (y % 2)

    def piece(t):
        return jnp.where(
            y < 2,
            lax.dynamic_index_in_dim(near_all, at + t, 0, False)[:640],
            lax.dynamic_index_in_dim(far_all, at + t, 0, False)[:640],
        )

    pair = lax.ppermute(piece(0), axes, left_source(0)) + lax.ppermute(
        piece(1), axes, left_source(1)
    )
    paired = lax.all_gather(pair, ROW, axis=0)
    left_gram = call(
        gram_kernel,
        shaped((640, 640), f32),
        where,
        near_all,
        far_all,
        paired,
        after=(bottom,),
        scratch=[pltpu.VMEM((640, 1024), bf16), pltpu.VMEM((640, 1024), bf16)],
        flops=840_000_000,
        moved=6_000_000,
    )
    return (update, exp_avg_new, exp_avg_sq_new, left_gram, right_gram)


def solution(mesh):
    wide = Mesh(
        mesh.devices.reshape(8, 4, 2, 2, 4), ("layer", "x", "core", "zh", "y")
    )
    row, col = ("x", "core"), ("zh", "y")
    return jax.shard_map(
        body,
        mesh=wide,
        in_specs=(
            P(("layer",) + row, col),
            P(("layer",) + row, col),
            P("layer", col),
            P(("layer",) + col, row),
            P(("layer",) + col, row),
        ),
        out_specs=(
            P(("layer",) + row, col),
            P(("layer",) + col, row),
            P(("layer",) + col, row),
            P(("layer",) + row, col),
            P(("layer",) + col, row),
        ),
        check_vma=False,
    )
```

time: 246 us -> 197 us (0.80)
  the two profiles are of different devices: /device:TPU:193 before, /device:TPU:160 now
where the time goes in v2:
time: 197 us
  starting transfers between devices  82 us (42%)
  waiting for transfers between devices  54.7 us (28%)
  Pallas kernels  17.1 us (9%)
  blocking collectives  15.9 us (8%)
  between operations  14 us (7%)
  local copies, waits for them, and re-layouts  7.25 us (4%)
  other arithmetic  5.71 us (3%)
    ppermute x3, starting transfers between devices, other_half(): return lax.ppermute(value, 'zh', [(0, 1), (1, 0)])  42.1 us
    ppermute x3, waiting for transfers between devices, other_half(): return lax.ppermute(value, 'zh', [(0, 1), (1, 0)])  20.9 us
    pallas_call x9, Pallas kernels, call(): pl.pallas_call(inner, out_shape=outs, in_specs=[pl.BlockSpec(memory_space...  17.1 us
    all_to_all x1, blocking collectives, body(): far_all = lax.all_to_all(far_four, 'y', 0, 0, tiled=True)  15.9 us
    all_to_all x1, waiting for transfers between devices, body(): summed = lax.all_to_all(summed, 'x', 0, 0, tiled=True)  15.7 us
    all_to_all x1, starting transfers between devices, body(): top = lax.all_to_all(top, 'y', 0, 0, tiled=True)  14.8 us
    all_to_all x1, waiting for transfers between devices, body(): top = lax.all_to_all(top, 'y', 0, 0, tiled=True)  9.27 us
    unnamed x16, local copies, waits for them, and re-layouts  7.22 us
  transfers between devices with their start and end apart: 16, of which 8 were waited for; matrix products, arithmetic and copies ran while one was open for 2% of the time, Pallas kernels for 9%

profile of v2, /device:TPU:160, one launch (start us, length us, event | category | flops | bytes accessed | tf_op | source)
XLA Modules:
  0.0 196.7 jit_solution(9814379231171673191)
XLA Ops:
  7.2 0.0 all-gather.5.cloned.1.call-start
  7.2 1.2 convert_bitcast_fusion
  8.4 0.8 pad_maximum_fusion
  9.2 0.1 pad_add_fusion.refs_0_
  9.3 1.5 shard_map.92
  10.8 4.5 %all-to-all-start = ((bf16[4,768,128]{2,1,0:T(8,128)(2,1)}), bf16[4,768,128]{2,1,0:T(8,128)(2,1)S(1)}, u32[]{:S(2)}, u32[]{:S(2)}) async-start(bf16[4,768,128]{2,1,0:T(8,128)(2,1)} %get-tuple-element.16), calls=%async_computation | async-start | bytes 1572864 | tf_op jit(solution)/shard_map/all_to_all | solution.py:218
  15.3 10.0 %collective-permute-start = (bf16[768,128]{1,0:T(8,128)(2,1)S(1)}, bf16[768,128]{1,0:T(8,128)(2,1)S(1)}, u32[]{:S(2)}, u32[]{:S(2)}) collective-permute-start(bf16[768,128]{1,0:T(8,128)(2,1)S(1)} %get-tuple-element.17), channel_id=1, source_target_pairs={{0,4},{4,0},{1,5},{5,1},{2,6},{6,2},{3,7},{7,3},{8,12},{12,8},{9,1... | collective-permute-start | bytes 589832 | tf_op jit(solution)/shard_map/ppermute | solution.py:47
  25.3 14.5 %collective-permute-done.refs_1_ = bf16[768,128]{1,0:T(8,128)(2,1)S(1)} collective-permute-done((bf16[768,128]{1,0:T(8,128)(2,1)S(1)}, bf16[768,128]{1,0:T(8,128)(2,1)S(1)}, u32[]{:S(2)}, u32[]{:S(2)}) %collective-permute-start) | collective-permute-done | bytes 196640 | tf_op jit(solution)/shard_map/ppermute | solution.py:47
  39.8 0.6 shard_map.93
  40.5 15.9 %all_to_all.30.refs_2_ = bf16[4,768,128]{2,1,0:T(8,128)(2,1)S(1)} all-to-all(bf16[4,768,128]{2,1,0:T(8,128)(2,1)S(1)} %shard_map.93), channel_id=1, replica_groups=mesh['layer'=8,'x'=4,'core'=2,'zh'=2,'y'=4] {'y'}, dimensions={0} | all-to-all | bytes 1572864 | tf_op jit(solution)/shard_map/all_to_all | solution.py:227
  56.4 1.3 shard_map.97
  57.7 1.7 copy-done
  59.5 2.2 %shard_map.94 = (bf16[384,1024]{1,0:T(8,128)(2,1)S(1)}, bf16[384,1024]{1,0:T(8,128)(2,1)S(1)}) custom-call(s32[4]{0:T(128)S(1)} %pad_add_fusion.refs_0_, bf16[4,768,128]{2,1,0:T(8,128)(2,1)S(1)} %all-to-all-done.refs_1_, bf16[4,768,128]{2,1,0:T(8,128)(2,1)S(1)} %all_to_all.30.refs_2_, bf16[640,128]{1,0:T(8,128)(2,1)S(1)} %copy-done.5, ...), custom_call_target="tpu_custom_call" | custom-call | flops 1000000000 | bytes 5000000 | tf_op jit(solution)/shard_map/pallas_call | solution.py:75
  61.7 1.9 collective-permute-start.1
  63.6 2.3 %collective-permute-done.1.refs_2_ = bf16[384,1024]{1,0:T(8,128)(2,1)S(1)} collective-permute-done((bf16[384,1024]{1,0:T(8,128)(2,1)S(1)}, bf16[384,1024]{1,0:T(8,128)(2,1)S(1)}, u32[]{:S(2)}, u32[]{:S(2)}) %collective-permute-start.1) | collective-permute-done | bytes 786464 | tf_op jit(solution)/shard_map/ppermute | solution.py:43
  65.9 1.6 shard_map.95
  67.5 4.3 %all-to-all-start.2 = ((bf16[4,384,256]{2,1,0:T(8,128)(2,1)}), bf16[4,384,256]{2,1,0:T(8,128)(2,1)S(1)}, u32[]{:S(2)}, u32[]{:S(2)}) async-start(bf16[4,384,256]{2,1,0:T(8,128)(2,1)} %shard_map.95), calls=%async_computation.2 | async-start | bytes 1572864 | tf_op jit(solution)/shard_map/all_to_all | solution.py:259
  71.8 15.7 %all-to-all-done.2.refs_1_ = bf16[4,384,256]{2,1,0:T(8,128)(2,1)S(1)} async-done(((bf16[4,384,256]{2,1,0:T(8,128)(2,1)}), bf16[4,384,256]{2,1,0:T(8,128)(2,1)S(1)}, u32[]{:S(2)}, u32[]{:S(2)}) %all-to-all-start.2) | async-done | bytes 786464 | tf_op jit(solution)/shard_map/all_to_all | solution.py:259
  87.5 1.2 shard_map.96
  88.7 0.8 copy-done.6
  89.6 3.5 %all-to-all-start.3 = ((bf16[4,320,256]{2,1,0:T(8,128)(2,1)}), bf16[4,320,256]{2,1,0:T(8,128)(2,1)S(1)}, u32[]{:S(2)}, u32[]{:S(2)}) async-start(bf16[4,320,256]{2,1,0:T(8,128)(2,1)} %copy-done.6), calls=%async_computation.3 | async-start | bytes 1310720 | tf_op jit(solution)/shard_map/all_to_all | solution.py:267
  93.1 0.0 all-gather.9.cloned.1.call-start
  93.2 0.7 collective-permute-start.6
  93.9 2.9 %collective-permute-start.7 = (bf16[640,128]{1,0:T(8,128)(2,1)S(1)}, bf16[640,128]{1,0:T(8,128)(2,1)S(1)}, u32[]{:S(2)}, u32[]{:S(2)}) collective-permute-start(bf16[640,128]{1,0:T(8,128)(2,1)S(1)} %get-tuple-element.27), channel_id=1, source_target_pairs={{0,8},{1,24},{2,40},{3,56},{8,9},{9,25},{10,41},{11,57},{16,10},{1... | collective-permute-start | bytes 491528 | tf_op jit(solution)/shard_map/ppermute | solution.py:322
  96.8 1.0 collective-permute-done.7
  97.8 0.7 add.46
  98.5 0.0 all-gather.7.cloned.1.call-done.refs_2_
  98.5 3.3 %all-to-all-done.3.refs_1_ = bf16[4,320,256]{2,1,0:T(8,128)(2,1)S(1)} async-done(((bf16[4,320,256]{2,1,0:T(8,128)(2,1)}), bf16[4,320,256]{2,1,0:T(8,128)(2,1)S(1)}, u32[]{:S(2)}, u32[]{:S(2)}) %all-to-all-start.3) | async-done | bytes 655392 | tf_op jit(solution)/shard_map/all_to_all | solution.py:267
  101.8 1.7 copy-done.1
  103.6 1.6 copy-done.2
  105.2 2.8 %shard_map.98 = (bf16[320,1024]{1,0:T(8,128)(2,1)S(1)}, f32[320,128]{1,0:T(8,128)S(1)}, f32[320,128]{1,0:T(8,128)S(1)}) custom-call(s32[4]{0:T(128)S(1)} %pad_add_fusion.refs_0_, bf16[4,320,256]{2,1,0:T(8,128)(2,1)S(1)} %all-to-all-done.3.refs_1_, bf16[1024,1024]{1,0:T(8,128)(2,1)S(1)} %copy-done.2, bf16[8,2,640,128]{3,2,1,0:T(8,128)(2,1)S(1)} %copy-done.1), custom_call_target="tpu_custom_call" | custom-call | flops 1400000000 | bytes 6000000 | tf_op jit(solution)/shard_map/pallas_call | solution.py:75
  108.0 1.9 collective-permute-start.2
  109.9 2.1 %collective-permute-done.2.refs_3_ = bf16[320,1024]{1,0:T(8,128)(2,1)S(1)} collective-permute-done((bf16[320,1024]{1,0:T(8,128)(2,1)S(1)}, bf16[320,1024]{1,0:T(8,128)(2,1)S(1)}, u32[]{:S(2)}, u32[]{:S(2)}) %collective-permute-start.2) | collective-permute-done | bytes 655392 | tf_op jit(solution)/shard_map/ppermute | solution.py:43
  112.0 2.7 %shard_map.99 = (bf16[4,640,128]{2,1,0:T(8,128)(2,1)}, bf16[4,640,128]{2,1,0:T(8,128)(2,1)}) custom-call(s32[4]{0:T(128)S(1)} %pad_add_fusion.refs_0_, bf16[640,640]{1,0:T(8,128)(2,1)S(1)} %copy-done.4, bf16[320,1024]{1,0:T(8,128)(2,1)S(1)} %get-tuple-element.21.refs_2_, bf16[320,1024]{1,0:T(8,128)(2,1)S(1)} %collective-permute-done.2.refs_3_), custom_call_target="tpu_custom_call" | custom-call | flops 840000000 | bytes 4000000 | tf_op jit(solution)/shard_map/pallas_call | solution.py:75
  114.6 14.8 %all-to-all-start.4 = ((bf16[4,640,128]{2,1,0:T(8,128)(2,1)}), bf16[4,640,128]{2,1,0:T(8,128)(2,1)S(1)}, u32[]{:S(2)}, u32[]{:S(2)}) async-start(bf16[4,640,128]{2,1,0:T(8,128)(2,1)} %get-tuple-element.22), calls=%async_computation.4 | async-start | bytes 1310720 | tf_op jit(solution)/shard_map/all_to_all | solution.py:294
  129.5 1.9 collective-permute-start.5
  131.4 9.3 %all-to-all-done.4 = bf16[4,640,128]{2,1,0:T(8,128)(2,1)S(1)} async-done(((bf16[4,640,128]{2,1,0:T(8,128)(2,1)}), bf16[4,640,128]{2,1,0:T(8,128)(2,1)S(1)}, u32[]{:S(2)}, u32[]{:S(2)}) %all-to-all-start.4) | async-done | bytes 655392 | tf_op jit(solution)/shard_map/all_to_all | solution.py:294
  140.7 3.5 %all-to-all-start.5 = ((bf16[4,640,128]{2,1,0:T(8,128)(2,1)}), bf16[4,640,128]{2,1,0:T(8,128)(2,1)S(1)}, u32[]{:S(2)}, u32[]{:S(2)}) async-start(bf16[4,640,128]{2,1,0:T(8,128)(2,1)} %get-tuple-element.23), calls=%async_computation.5 | async-start | bytes 1310720 | tf_op jit(solution)/shard_map/all_to_all | solution.py:295
  144.2 2.0 %fusion = (f32[640,128]{1,0:T(8,128)}, f32[640,128]{1,0:T(8,128)}) fusion(f32[640,128]{1,0:T(8,128)} %param.9, f32[320,128]{1,0:T(8,128)S(1)} %get-tuple-element.24, f32[320,128]{1,0:T(8,128)S(1)} %collective-permute-done.5, pred[]{:T(512)S(6)} %eq.5, f32[640,128]{1,0:T(8,128)} %param.8), kind=kLoop, calls=%fused_computation.3 | loop fusion | flops 819200 | bytes 1638401 | tf_op jit(solution)/shard_map/add | solution.py:310
  146.2 0.1 convert_reduce_fusion.1
  146.3 23.7 %collective-permute-start.3 = (bf16[320,128]{1,0:T(8,128)(2,1)S(1)}, bf16[320,128]{1,0:T(8,128)(2,1)S(1)}, u32[]{:S(2)}, u32[]{:S(2)}) collective-permute-start(bf16[320,128]{1,0:T(8,128)(2,1)S(1)} %slice.51), channel_id=1, source_target_pairs={{0,4},{4,0},{1,5},{5,1},{2,6},{6,2},{3,7},{7,3},{8,12},{12,8},{9,1... | collective-permute-start | bytes 245768 | tf_op jit(solution)/shard_map/ppermute | solution.py:47
  170.0 0.1 convert_reduce_fusion
  170.2 8.3 %collective-permute-start.4 = (bf16[320,128]{1,0:T(8,128)(2,1)S(1)}, bf16[320,128]{1,0:T(8,128)(2,1)S(1)}, u32[]{:S(2)}, u32[]{:S(2)}) collective-permute-start(bf16[320,128]{1,0:T(8,128)(2,1)S(1)} %slice.50), channel_id=1, source_target_pairs={{0,4},{4,0},{1,5},{5,1},{2,6},{6,2},{3,7},{7,3},{8,12},{12,8},{9,1... | collective-permute-start | bytes 245768 | tf_op jit(solution)/shard_map/ppermute | solution.py:47
  178.5 0.0 all-gather.9.cloned.1.call-done
  178.5 1.3 copy-done.3
  179.9 3.1 %shard_map.100 = f32[640,640]{1,0:T(8,128)} custom-call(s32[4]{0:T(128)S(1)} %pad_add_fusion.refs_0_, bf16[4,768,128]{2,1,0:T(8,128)(2,1)S(1)} %all-to-all-done.refs_1_, bf16[4,768,128]{2,1,0:T(8,128)(2,1)S(1)} %all_to_all.30.refs_2_, bf16[8,640,128]{2,1,0:T(8,128)(2,1)S(1)} %bitcast.13, bf16[4,640,128]{2,1,0:T(8,128)(2,1)S(1)} %all-to-all-done.5.refs_4_), custom_call_target="tpu_custom_call" | custom-call | flops 840000000 | bytes 6000000 | tf_op jit(solution)/shard_map/pallas_call | solution.py:75
  183.0 6.4 %collective-permute-done.4 = bf16[320,128]{1,0:T(8,128)(2,1)S(1)} collective-permute-done((bf16[320,128]{1,0:T(8,128)(2,1)S(1)}, bf16[320,128]{1,0:T(8,128)(2,1)S(1)}, u32[]{:S(2)}, u32[]{:S(2)}) %collective-permute-start.4) | collective-permute-done | bytes 81952 | tf_op jit(solution)/shard_map/ppermute | solution.py:47
  189.5 0.7 pad_maximum_fusion.1
  (26 shorter events, 0.2 us)
Async XLA Ops:
  7.2 2.1 %copy-start.5 = (bf16[640,128]{1,0:T(8,128)(2,1)S(1)}, bf16[640,128]{1,0:T(8,128)(2,1)}, u32[]{:S(2)}) copy-start(bf16[640,128]{1,0:T(8,128)(2,1)} %refs_3_.1) | copy-start | bytes 491524
  7.2 2.1 %copy-start.7 = (bf16[1024,128]{1,0:T(8,128)(2,1)S(1)}, bf16[1024,128]{1,0:T(8,128)(2,1)}, u32[]{:S(2)}) copy-start(bf16[1024,128]{1,0:T(8,128)(2,1)} %refs_2_.1) | copy-start | bytes 786436
  7.2 50.5 %all-gather.5.cloned.1.call-start = ((), (), s32[]{:S(2)}) async-start(), calls=%async_computation.6 | async-start | bytes 2949120 | tf_op jit(solution)/shard_map/all_gather | solution.py:220
  10.8 29.7 %all-to-all-start = ((bf16[4,768,128]{2,1,0:T(8,128)(2,1)}), bf16[4,768,128]{2,1,0:T(8,128)(2,1)S(1)}, u32[]{:S(2)}, u32[]{:S(2)}) async-start(bf16[4,768,128]{2,1,0:T(8,128)(2,1)} %get-tuple-element.16), calls=%async_computation | async-start | bytes 1572864 | tf_op jit(solution)/shard_map/all_to_all | solution.py:218
  15.3 83.2 %all-gather.7.cloned.1.call-start = ((), (), s32[]{:S(2)}) async-start(), calls=%async_computation.7 | async-start | bytes 2359296 | tf_op jit(solution)/shard_map/all_gather | solution.py:236
  15.3 24.5 %collective-permute-start = (bf16[768,128]{1,0:T(8,128)(2,1)S(1)}, bf16[768,128]{1,0:T(8,128)(2,1)S(1)}, u32[]{:S(2)}, u32[]{:S(2)}) collective-permute-start(bf16[768,128]{1,0:T(8,128)(2,1)S(1)} %get-tuple-element.17), channel_id=1, source_target_pairs={{0,4},{4,0},{1,5},{5,1},{2,6},{6,2},{3,7},{7,3},{8,12},{12,8},{9,1... | collective-permute-start | bytes 589832 | tf_op jit(solution)/shard_map/ppermute | solution.py:47
  40.5 17.2 %copy-start.4 = (bf16[640,640]{1,0:T(8,128)(2,1)S(1)}, bf16[640,640]{1,0:T(8,128)(2,1)}, u32[]{:S(2)}) copy-start(bf16[640,640]{1,0:T(8,128)(2,1)} %refs_1_.3) | copy-start | bytes 2457604
  57.7 1.7 copy-start
  61.7 4.2 %collective-permute-start.1 = (bf16[384,1024]{1,0:T(8,128)(2,1)S(1)}, bf16[384,1024]{1,0:T(8,128)(2,1)S(1)}, u32[]{:S(2)}, u32[]{:S(2)}) collective-permute-start(bf16[384,1024]{1,0:T(8,128)(2,1)S(1)} %get-tuple-element.19), channel_id=1, source_target_pairs={{0,8},{8,0},{1,9},{9,1},{2,10},{10,2},{3,11},{11,3},{4,12},{12,4},... | collective-permute-start | bytes 2359304 | tf_op jit(solution)/shard_map/ppermute | solution.py:43
  67.5 20.0 %all-to-all-start.2 = ((bf16[4,384,256]{2,1,0:T(8,128)(2,1)}), bf16[4,384,256]{2,1,0:T(8,128)(2,1)S(1)}, u32[]{:S(2)}, u32[]{:S(2)}) async-start(bf16[4,384,256]{2,1,0:T(8,128)(2,1)} %shard_map.95), calls=%async_computation.2 | async-start | bytes 1572864 | tf_op jit(solution)/shard_map/all_to_all | solution.py:259
  88.7 0.8 copy-start.6
  89.6 12.3 %all-to-all-start.3 = ((bf16[4,320,256]{2,1,0:T(8,128)(2,1)}), bf16[4,320,256]{2,1,0:T(8,128)(2,1)S(1)}, u32[]{:S(2)}, u32[]{:S(2)}) async-start(bf16[4,320,256]{2,1,0:T(8,128)(2,1)} %copy-done.6), calls=%async_computation.3 | async-start | bytes 1310720 | tf_op jit(solution)/shard_map/all_to_all | solution.py:267
  93.1 85.4 %all-gather.9.cloned.1.call-start = ((), (), s32[]{:S(2)}) async-start(), calls=%async_computation.8 | async-start | bytes 1474560 | tf_op jit(solution)/shard_map/all_gather | solution.py:325
  93.2 3.6 %collective-permute-start.6 = (bf16[640,128]{1,0:T(8,128)(2,1)S(1)}, bf16[640,128]{1,0:T(8,128)(2,1)S(1)}, u32[]{:S(2)}, u32[]{:S(2)}) collective-permute-start(bf16[640,128]{1,0:T(8,128)(2,1)S(1)} %get-tuple-element.28), channel_id=1, source_target_pairs={{0,0},{1,16},{2,32},{3,48},{8,1},{9,17},{10,33},{11,49},{16,2},{17... | collective-permute-start | bytes 491528 | tf_op jit(solution)/shard_map/ppermute | solution.py:322
  93.9 3.9 %collective-permute-start.7 = (bf16[640,128]{1,0:T(8,128)(2,1)S(1)}, bf16[640,128]{1,0:T(8,128)(2,1)S(1)}, u32[]{:S(2)}, u32[]{:S(2)}) collective-permute-start(bf16[640,128]{1,0:T(8,128)(2,1)S(1)} %get-tuple-element.27), channel_id=1, source_target_pairs={{0,8},{1,24},{2,40},{3,56},{8,9},{9,25},{10,41},{11,57},{16,10},{1... | collective-permute-start | bytes 491528 | tf_op jit(solution)/shard_map/ppermute | solution.py:322
  101.8 1.7 copy-start.1
  103.6 1.6 copy-start.2
  108.0 4.0 %collective-permute-start.2 = (bf16[320,1024]{1,0:T(8,128)(2,1)S(1)}, bf16[320,1024]{1,0:T(8,128)(2,1)S(1)}, u32[]{:S(2)}, u32[]{:S(2)}) collective-permute-start(bf16[320,1024]{1,0:T(8,128)(2,1)S(1)} %get-tuple-element.21.refs_2_), channel_id=1, source_target_pairs={{0,8},{8,0},{1,9},{9,1},{2,10},{10,2},{3,11},{11,3},{4,12},{12,4},... | collective-permute-start | bytes 1966088 | tf_op jit(solution)/shard_map/ppermute | solution.py:43
  114.6 26.0 %all-to-all-start.4 = ((bf16[4,640,128]{2,1,0:T(8,128)(2,1)}), bf16[4,640,128]{2,1,0:T(8,128)(2,1)S(1)}, u32[]{:S(2)}, u32[]{:S(2)}) async-start(bf16[4,640,128]{2,1,0:T(8,128)(2,1)} %get-tuple-element.22), calls=%async_computation.4 | async-start | bytes 1310720 | tf_op jit(solution)/shard_map/all_to_all | solution.py:294
  129.5 14.7 %collective-permute-start.5 = (f32[320,128]{1,0:T(8,128)S(1)}, f32[320,128]{1,0:T(8,128)S(1)}, u32[]{:S(2)}, u32[]{:S(2)}) collective-permute-start(f32[320,128]{1,0:T(8,128)S(1)} %get-tuple-element.25), channel_id=1, source_target_pairs={{0,8},{8,0},{1,9},{9,1},{2,10},{10,2},{3,11},{11,3},{4,12},{12,4},... | collective-permute-start | bytes 491528 | tf_op jit(solution)/shard_map/ppermute | solution.py:43
  140.7 29.4 %all-to-all-start.5 = ((bf16[4,640,128]{2,1,0:T(8,128)(2,1)}), bf16[4,640,128]{2,1,0:T(8,128)(2,1)S(1)}, u32[]{:S(2)}, u32[]{:S(2)}) async-start(bf16[4,640,128]{2,1,0:T(8,128)(2,1)} %get-tuple-element.23), calls=%async_computation.5 | async-start | bytes 1310720 | tf_op jit(solution)/shard_map/all_to_all | solution.py:295
  146.3 36.7 %collective-permute-start.3 = (bf16[320,128]{1,0:T(8,128)(2,1)S(1)}, bf16[320,128]{1,0:T(8,128)(2,1)S(1)}, u32[]{:S(2)}, u32[]{:S(2)}) collective-permute-start(bf16[320,128]{1,0:T(8,128)(2,1)S(1)} %slice.51), channel_id=1, source_target_pairs={{0,4},{4,0},{1,5},{5,1},{2,6},{6,2},{3,7},{7,3},{8,12},{12,8},{9,1... | collective-permute-start | bytes 245768 | tf_op jit(solution)/shard_map/ppermute | solution.py:47
  170.2 19.3 %collective-permute-start.4 = (bf16[320,128]{1,0:T(8,128)(2,1)S(1)}, bf16[320,128]{1,0:T(8,128)(2,1)S(1)}, u32[]{:S(2)}, u32[]{:S(2)}) collective-permute-start(bf16[320,128]{1,0:T(8,128)(2,1)S(1)} %slice.50), channel_id=1, source_target_pairs={{0,4},{4,0},{1,5},{5,1},{2,6},{6,2},{3,7},{7,3},{8,12},{12,8},{9,1... | collective-permute-start | bytes 245768 | tf_op jit(solution)/shard_map/ppermute | solution.py:47
  178.5 1.3 copy-start.3
Sparse Core Ops, SparseCore 0:
  10.7 36.4 all-gather.4
  57.8 37.7 all-gather.6
  98.6 55.8 all-gather.8

commit v3 on v2

v3 whole, which is shorter than its diff:
```python
import itertools

import jax
import jax.numpy as jnp
from jax import lax
from jax.experimental import pallas as pl
from jax.experimental.pallas import tpu as pltpu
from jax.sharding import Mesh, PartitionSpec as P

M = 5120
C = 1024

first_beta = 0.9
second_beta = 0.95
epsilon = 1e-08

SIZES = {"x": 4, "core": 2, "zh": 2, "y": 4}
ROW = ("x", "core")
f32 = jnp.float32
bf16 = jnp.bfloat16


def pairs(axes, target):
    found = []
    for place in itertools.product(*[range(SIZES[a]) for a in axes]):
        there = target(*place)
        if there is None:
            continue
        src = dst = 0
        for a, s, d in zip(axes, place, there):
            src, dst = src * SIZES[a] + s, dst * SIZES[a] + d
        found.append((src, dst))
    return found


def dot(a, b, over_a, over_b):
    return lax.dot_general(
        a, b, (((over_a,), (over_b,)), ((), ())), preferred_element_type=f32
    )


def other_core(value):
    return lax.ppermute(value, "core", [(0, 1), (1, 0)])


def other_half(value):
    return lax.ppermute(value, "zh", [(0, 1), (1, 0)])


def spread(value, axis):
    return lax.all_to_all(
        jnp.broadcast_to(value[None], (4,) + value.shape), axis, 0, 0, tiled=True
    )


def left_source(core):
    def target(x, c, z, y):
        if x // 2 != z:
            return None
        return (y, core, z, 2 * (x % 2) + c)

    return pairs(("x", "core", "zh", "y"), target)


def shaped(shape, dtype):
    return jax.ShapeDtypeStruct(shape, dtype)


def call(
    kernel, outs, where, *operands, hbm=(), after=(), scratch=(), flops=0, moved=0, limit=40
):
    n = len(operands) + len(hbm)

    def inner(*refs):
        kernel(*refs[: n + 1], *refs[n + 1 + len(after) :])

    return pl.pallas_call(
        inner,
        out_shape=outs,
        in_specs=[pl.BlockSpec(memory_space=pltpu.SMEM)]
        + [pl.BlockSpec(memory_space=pltpu.VMEM)] * len(operands)
        + [pl.BlockSpec(memory_space=pl.ANY)] * (len(hbm) + len(after)),
        scratch_shapes=scratch,
        compiler_params=pltpu.CompilerParams(vmem_limit_bytes=limit * 1024 * 1024),
        cost_estimate=pl.CostEstimate(
            flops=flops, bytes_accessed=moved, transcendentals=0
        ),
    )(where, *operands, *hbm, *after)


def first_kernel(where, grad, right, first, second, mine, moments):
    mine[:640] = grad[...]
    mine[640:] = right[pl.ds(pl.multiple_of(where[0] * 128, 128), 128)]
    moments[0] = first[...].astype(bf16)
    moments[1] = second[...].astype(bf16)


def left_kernel(where, near, far, grad, left, keep, send, slabs, panel):
    core, z = where[1], where[2]
    for k in range(4):
        slabs[:, 128 * k : 128 * k + 128] = near[k, 640:]
        slabs[:, 512 + 128 * k : 640 + 128 * k] = far[k, 640:]
        panel[:, 128 * k : 128 * k + 128] = near[k, :640, :]
        panel[:, 512 + 128 * k : 640 + 128 * k] = far[k, :640, :]

    product = dot(left[...], panel[...], 0, 0).astype(bf16)
    gram = (dot(grad[...], panel[...], 0, 0) * (1.0 / M)).astype(bf16)

    def columns(t, flip):
        found = []
        for k in range(4):
            block = 2 * k + t
            if flip:
                block = (block + 4) % 8
            at = block * 128
            found += [gram[:64, at : at + 128], gram[64:, at : at + 128]]
        return jnp.concatenate(found, axis=1)

    for c in range(2):

        @pl.when(core == c)
        def _():
            keep[:320] = product[320 * c : 320 * c + 320]
            send[:320] = product[320 * (1 - c) : 320 * (1 - c) + 320]
            for half in range(2):

                @pl.when(z == half)
                def _():
                    keep[320:] = columns(c, half == 1)
                    send[320:] = columns(1 - c, half == 1)


def join_kernel(where, first, second, four):
    for k in range(4):
        at = slice(256 * k, 256 * k + 256)
        four[k] = (first[:, at].astype(f32) + second[:, at].astype(f32)).astype(bf16)


def sum_kernel(where, parts, rows, gram):
    total = (
        parts[0].astype(f32)
        + parts[1].astype(f32)
        + parts[2].astype(f32)
        + parts[3].astype(f32)
    )
    rows[...] = total[:320].astype(bf16)
    gram[:64] = total[320:, :128]
    gram[64:] = total[320:, 128:]


def turn_kernel(
    where, half, basis, moments, out, own, theirs, rows, rotated, right, old, sems
):
    row, core = where[0], where[1]
    copies = [
        pltpu.make_async_copy(
            basis.at[pl.ds(256 * c, 256)], right.at[pl.ds(256 * c, 256)], sems.at[c]
        )
        for c in range(4)
    ]
    at = pl.multiple_of(core * 320, 320)
    copies += [
        pltpu.make_async_copy(
            moments.at[pl.ds(4 * c, 4), :, pl.ds(at, 320)],
            old.at[pl.ds(4 * c, 4)],
            sems.at[4 + c],
        )
        for c in range(2)
    ]
    for copy in copies:
        copy.start()
    for k in range(4):
        rows[:, 256 * k : 256 * k + 256] = half[k]
    for c in range(4):
        copies[c].wait()
        rotated[:, 256 * c : 256 * c + 256] = dot(
            rows[...], right[256 * c : 256 * c + 256], 1, 1
        )
    copies[4].wait()
    copies[5].wait()
    for i in range(8):
        turned = rotated[:, 128 * i : 128 * i + 128]
        new = first_beta * old[i, 0].astype(f32) + (1.0 - first_beta) * turned
        new_sq = (
            second_beta * old[i, 1].astype(f32) + (1.0 - second_beta) * turned * turned
        )
        rows[:, 128 * i : 128 * i + 128] = (new / (jnp.sqrt(new_sq) + epsilon)).astype(bf16)
    out[...] = dot(rows[...], right[...], 1, 0).astype(bf16)
    own[...] = rotated[:, pl.ds(pl.multiple_of(row * 128, 128), 128)]
    next_row = row + 1 - 2 * core
    theirs[...] = rotated[:, pl.ds(pl.multiple_of(next_row * 128, 128), 128)]


def back_kernel(where, left, mine, other, top, bottom, joined):
    core = where[1]
    joined[pl.ds(pl.multiple_of(core * 320, 320), 320)] = mine[...]
    joined[pl.ds(pl.multiple_of(320 - core * 320, 320), 320)] = other[...]
    for out, at in ((top, 0), (bottom, 320)):
        product = dot(left[at : at + 320, :], joined[...], 1, 0).astype(bf16)
        for k in range(4):
            out[k, :320] = product[:, 128 * k : 128 * k + 128]
            out[k, 320:] = product[:, 512 + 128 * k : 640 + 128 * k]


def fold_kernel(where, parts, keep, send):
    total = (
        parts[0].astype(f32)
        + parts[1].astype(f32)
        + parts[2].astype(f32)
        + parts[3].astype(f32)
    )
    keep[...] = total[:320]
    send[...] = total[320:].astype(bf16)


def update_kernel(where, top, bottom, far_top, far_bottom, update):
    update[:320] = (top[...] + far_top[...].astype(f32)).astype(bf16)
    update[320:] = (bottom[...] + far_bottom[...].astype(f32)).astype(bf16)


def moments_kernel(where, own, theirs, first, second, first_new, second_new):
    core = where[1]
    for turned, at in ((own, core * 320), (theirs, 320 - core * 320)):
        rows = pl.ds(pl.multiple_of(at, 320), 320)
        value = turned[...]
        first_new[rows] = first_beta * first[rows] + (1.0 - first_beta) * value
        second_new[rows] = (
            second_beta * second[rows] + (1.0 - second_beta) * value * value
        )


def pair_kernel(where, first, second, out):
    out[...] = first[...] + second[...]


def gram_kernel(where, near, far, paired, out, corner, panel, other):
    for k in range(4):
        panel[:, 128 * k : 128 * k + 128] = near[k, :640, :]
        panel[:, 512 + 128 * k : 640 + 128 * k] = far[k, :640, :]
    for k in range(8):
        other[:, 128 * k : 128 * k + 128] = paired[k]
    out[...] = dot(panel[...], other[...], 1, 1) * (1.0 / C)
    corner[...] = out[:8, :128]


def body(grad, left_basis, right_rows, exp_avg, exp_avg_sq):
    x, core = lax.axis_index("x"), lax.axis_index("core")
    z, y = lax.axis_index("zh"), lax.axis_index("y")
    row = 2 * x + core
    where = jnp.stack([row, core, z, y]).astype(jnp.int32)

    mine, moments = call(
        first_kernel,
        [shaped((768, 128), bf16), shaped((2, 640, 128), bf16)],
        where,
        grad,
        right_rows,
        exp_avg,
        exp_avg_sq,
        moved=1_500_000,
    )
    far = other_half(mine)
    near_all = lax.all_gather(mine, "y", axis=0)

    moments = lax.all_gather(moments, ROW, axis=0)
    far_all = lax.all_gather(far, "y", axis=0)

    keep, send, slabs = call(
        left_kernel,
        [shaped((384, 1024), bf16)] * 2 + [shaped((128, 1024), bf16)],
        where,
        near_all,
        far_all,
        grad,
        left_basis,
        scratch=[pltpu.VMEM((640, 1024), bf16)],
        flops=1_000_000_000,
        moved=5_000_000,
    )
    basis = lax.all_gather(slabs, ROW, axis=0, tiled=True)
    summed = call(
        join_kernel,
        shaped((4, 384, 256), bf16),
        where,
        keep,
        other_core(send),
        after=(moments[:1, :1, :16],),
        moved=2_400_000,
    )
    summed = lax.all_to_all(summed, "x", 0, 0, tiled=True)
    rows, right_gram = call(
        sum_kernel,
        [shaped((320, 256), bf16), shaped((128, 128), f32)],
        where,
        summed,
        moved=1_500_000,
    )
    half = lax.all_gather(rows, "x", axis=0)

    axes = ("x", "core", "zh", "y")
    at = 2 * (y % 2)

    def piece(t):
        return jnp.where(
            y < 2,
            lax.dynamic_index_in_dim(near_all, at + t, 0, False)[:640],
            lax.dynamic_index_in_dim(far_all, at + t, 0, False)[:640],
        )

    pieces = [lax.ppermute(piece(t), axes, left_source(t)) for t in range(2)]

    turned, own, theirs = call(
        turn_kernel,
        [shaped((320, 1024), bf16), shaped((320, 128), f32), shaped((320, 128), f32)],
        where,
        half,
        hbm=(basis, moments),
        after=tuple(pieces),
        scratch=[
            pltpu.VMEM((320, 1024), bf16),
            pltpu.VMEM((320, 1024), f32),
            pltpu.VMEM((1024, 1024), bf16),
            pltpu.VMEM((8, 2, 320, 128), bf16),
            pltpu.SemaphoreType.DMA((6,)),
        ],
        limit=60,
        flops=1_400_000_000,
        moved=6_000_000,
    )
    top_parts, bottom_parts = call(
        back_kernel,
        [shaped((4, 640, 128), bf16)] * 2,
        where,
        left_basis,
        turned,
        other_core(turned),
        scratch=[pltpu.VMEM((640, 1024), bf16)],
        flops=840_000_000,
        moved=4_000_000,
    )
    top = lax.all_to_all(top_parts, "y", 0, 0, tiled=True)
    bottom = lax.all_to_all(bottom_parts, "y", 0, 0, tiled=True)
    kept, arrived = [], []
    for part in (top, bottom):
        keep, send = call(
            fold_kernel,
            [shaped((320, 128), f32), shaped((320, 128), bf16)],
            where,
            part,
            moved=1_000_000,
        )
        kept.append(keep)
        arrived.append(other_half(send))

    exp_avg_new, exp_avg_sq_new = call(
        moments_kernel,
        [shaped((640, 128), f32)] * 2,
        where,
        own,
        other_core(theirs),
        exp_avg,
        exp_avg_sq,
        after=(bottom,),
        moved=1_700_000,
    )

    pair = call(
        pair_kernel,
        shaped((640, 128), bf16),
        where,
        *pieces,
        after=(top_parts,),
        moved=500_000,
    )
    paired = lax.all_gather(pair, ROW, axis=0)
    left_gram, corner = call(
        gram_kernel,
        [shaped((640, 640), f32), shaped((8, 128), f32)],
        where,
        near_all,
        far_all,
        paired,
        after=(bottom,),
        scratch=[pltpu.VMEM((640, 1024), bf16), pltpu.VMEM((640, 1024), bf16)],
        flops=840_000_000,
        moved=6_000_000,
    )
    update = call(
        update_kernel,
        shaped((640, 128), bf16),
        where,
        *kept,
        *arrived,
        after=(corner,),
        moved=700_000,
    )
    return (update, exp_avg_new, exp_avg_sq_new, left_gram, right_gram)


def solution(mesh):
    wide = Mesh(
        mesh.devices.reshape(8, 4, 2, 2, 4), ("layer", "x", "core", "zh", "y")
    )
    row, col = ("x", "core"), ("zh", "y")
    return jax.shard_map(
        body,
        mesh=wide,
        in_specs=(
            P(("layer",) + row, col),
            P(("layer",) + row, col),
            P("layer", col),
            P(("layer",) + col, row),
            P(("layer",) + col, row),
        ),
        out_specs=(
            P(("layer",) + row, col),
            P(("layer",) + col, row),
            P(("layer",) + col, row),
            P(("layer",) + row, col),
            P(("layer",) + col, row),
        ),
        check_vma=False,
    )
```

time: 197 us -> 196 us (level)
  the two profiles are of different devices: /device:TPU:160 before, /device:TPU:105 now
where the time goes in v3:
time: 196 us; the launch traced here: 195 us
  starting transfers between devices  65.5 us (33%)
  blocking collectives  62.4 us (32%)
  Pallas kernels  26.3 us (13%)
  waiting for transfers between devices  16.3 us (8%)
  between operations  13.9 us (7%)
  local copies, waits for them, and re-layouts  10.7 us (5%)
    ppermute x3, starting transfers between devices, other_half(): return lax.ppermute(value, 'zh', [(0, 1), (1, 0)])  32.4 us
    pallas_call x12, Pallas kernels, call(): pl.pallas_call(inner, out_shape=outs, in_specs=[pl.BlockSpec(memory_space...  26.3 us
    all_to_all x1, blocking collectives, body(): bottom = lax.all_to_all(bottom_parts, 'y', 0, 0, tiled=True)  21.1 us
    all_gather x1, blocking collectives, body(): half = lax.all_gather(rows, 'x', axis=0)  17.2 us
    ppermute x3, starting transfers between devices, other_core(): return lax.ppermute(value, 'core', [(0, 1), (1, 0)])  16.4 us
    all_gather x1, blocking collectives, body(): far_all = lax.all_gather(far, 'y', axis=0)  12.5 us
    all_gather x1, blocking collectives, body(): near_all = lax.all_gather(mine, 'y', axis=0)  11.6 us
    unnamed x46, local copies, waits for them, and re-layouts  10.1 us
  transfers between devices with their start and end apart: 13, of which 4 were waited for; matrix products, arithmetic and copies ran while one was open for 0% of the time, Pallas kernels for 7%

profile of v3, /device:TPU:105, one launch (start us, length us, event | category | flops | bytes accessed | tf_op | source)
XLA Modules:
  0.0 195.2 jit_solution(5503518527146331981)
XLA Ops:
  7.2 0.0 all-gather.11.cloned.1.call-start
  7.2 0.1 pad_add_fusion.refs_0_
  7.3 1.0 copy-done.1
  8.3 1.0 copy-done.3
  9.2 0.9 copy-done.9
  10.2 0.9 copy-done.15
  11.1 1.3 shard_map.92
  12.5 0.0 all-gather.9.cloned.1.call-start
  12.5 12.7 %collective-permute-start = (bf16[768,128]{1,0:T(8,128)(2,1)S(1)}, bf16[768,128]{1,0:T(8,128)(2,1)S(1)}, u32[]{:S(2)}, u32[]{:S(2)}) collective-permute-start(bf16[768,128]{1,0:T(8,128)(2,1)S(1)} %get-tuple-element.25), channel_id=1, source_target_pairs={{0,4},{4,0},{1,5},{5,1},{2,6},{6,2},{3,7},{7,3},{8,12},{12,8},{9,1... | collective-permute-start | bytes 589832 | tf_op jit(solution)/shard_map/ppermute | solution.py:47
  25.3 11.6 %all-gather = bf16[3072,128]{1,0:T(8,128)(2,1)S(1)} all-gather(bf16[768,128]{1,0:T(8,128)(2,1)S(1)} %get-tuple-element.25), channel_id=2, replica_groups=mesh['layer'=8,'x'=4,'core'=2,'zh'=2,'y'=4] {'y'}, dimensions={0}, use_global_device_ids=true | all-gather | bytes 983040 | tf_op jit(solution)/shard_map/all_gather | solution.py:263
  36.9 12.5 %all-gather.1 = bf16[3072,128]{1,0:T(8,128)(2,1)S(1)} all-gather(bf16[768,128]{1,0:T(8,128)(2,1)S(1)} %collective-permute-done), channel_id=3, replica_groups=mesh['layer'=8,'x'=4,'core'=2,'zh'=2,'y'=4] {'y'}, dimensions={0}, use_global_device_ids=true | all-gather | bytes 983040 | tf_op jit(solution)/shard_map/all_gather | solution.py:266
  49.4 3.0 %shard_map.93 = (bf16[384,1024]{1,0:T(8,128)(2,1)S(1)}, bf16[384,1024]{1,0:T(8,128)(2,1)S(1)}, bf16[128,1024]{1,0:T(8,128)(2,1)}) custom-call(s32[4]{0:T(128)S(1)} %pad_add_fusion.refs_0_, bf16[4,768,128]{2,1,0:T(8,128)(2,1)S(1)} %bitcast.13, bf16[4,768,128]{2,1,0:T(8,128)(2,1)S(1)} %bitcast.16, bf16[640,128]{1,0:T(8,128)(2,1)S(1)} %copy-done.16, ...), custom_call_target="tpu_custom_call" | custom-call | flops 1000000000 | bytes 5000000 | tf_op jit(solution)/shard_map/pallas_call | solution.py:77
  52.4 0.9 copy-done.21
  53.3 6.5 %collective-permute-start.1 = (bf16[384,1024]{1,0:T(8,128)(2,1)}, bf16[384,1024]{1,0:T(8,128)(2,1)S(1)}, u32[]{:S(2)}, u32[]{:S(2)}) collective-permute-start(bf16[384,1024]{1,0:T(8,128)(2,1)} %copy-done.21), channel_id=1, source_target_pairs={{0,8},{8,0},{1,9},{9,1},{2,10},{10,2},{3,11},{11,3},{4,12},{12,4},... | collective-permute-start | bytes 2359304 | tf_op jit(solution)/shard_map/ppermute | solution.py:43
  59.8 0.0 all-gather.11.cloned.1.call-done
  59.8 0.7 slice.24.refs_3_
  60.5 1.4 collective-permute-done.1.refs_2_
  61.9 1.6 shard_map.94
  63.5 4.0 %all-to-all-start = ((bf16[4,384,256]{2,1,0:T(8,128)(2,1)}), bf16[4,384,256]{2,1,0:T(8,128)(2,1)S(1)}, u32[]{:S(2)}, u32[]{:S(2)}) async-start(bf16[4,384,256]{2,1,0:T(8,128)(2,1)} %shard_map.94), calls=%async_computation | async-start | bytes 1572864 | tf_op jit(solution)/shard_map/all_to_all | solution.py:290
  67.6 4.2 %collective-permute-start.2 = (bf16[640,128]{1,0:T(8,128)(2,1)S(1)}, bf16[640,128]{1,0:T(8,128)(2,1)S(1)}, u32[]{:S(2)}, u32[]{:S(2)}) collective-permute-start(bf16[640,128]{1,0:T(8,128)(2,1)S(1)} %get-tuple-element.46), channel_id=1, source_target_pairs={{0,0},{1,16},{2,32},{3,48},{8,1},{9,17},{10,33},{11,49},{16,2},{17... | collective-permute-start | bytes 491528 | tf_op jit(solution)/shard_map/ppermute | solution.py:310
  71.8 3.7 %collective-permute-start.3 = (bf16[640,128]{1,0:T(8,128)(2,1)S(1)}, bf16[640,128]{1,0:T(8,128)(2,1)S(1)}, u32[]{:S(2)}, u32[]{:S(2)}) collective-permute-start(bf16[640,128]{1,0:T(8,128)(2,1)S(1)} %get-tuple-element.45), channel_id=1, source_target_pairs={{0,8},{1,24},{2,40},{3,56},{8,9},{9,25},{10,41},{11,57},{16,10},{1... | collective-permute-start | bytes 491528 | tf_op jit(solution)/shard_map/ppermute | solution.py:310
  75.5 3.8 %all-to-all-done.refs_1_ = bf16[4,384,256]{2,1,0:T(8,128)(2,1)S(1)} async-done(((bf16[4,384,256]{2,1,0:T(8,128)(2,1)}), bf16[4,384,256]{2,1,0:T(8,128)(2,1)S(1)}, u32[]{:S(2)}, u32[]{:S(2)}) %all-to-all-start) | async-done | bytes 786464 | tf_op jit(solution)/shard_map/all_to_all | solution.py:290
  79.3 1.2 shard_map.95
  80.4 17.2 %all-gather.3 = bf16[1280,256]{1,0:T(8,128)(2,1)} all-gather(bf16[320,256]{1,0:T(8,128)(2,1)S(1)} %get-tuple-element.29), channel_id=5, replica_groups=mesh['layer'=8,'x'=4,'core'=2,'zh'=2,'y'=4] {'x'}, dimensions={0}, use_global_device_ids=true | all-gather | bytes 819200 | tf_op jit(solution)/shard_map/all_gather | solution.py:298
  97.7 0.0 all-gather.9.cloned.1.call-done.refs_2_
  97.7 0.6 copy-done.5
  98.3 0.1 copy-done.7
  98.4 6.8 %shard_map.96 = (bf16[320,1024]{1,0:T(8,128)(2,1)}, f32[320,128]{1,0:T(8,128)}, f32[320,128]{1,0:T(8,128)}) custom-call(s32[4]{0:T(128)} %copy-done.17, bf16[4,320,256]{2,1,0:T(8,128)(2,1)} %bitcast.22, bf16[1024,1024]{1,0:T(8,128)(2,1)} %all-gather.9.cloned.1.call-done.refs_2_, bf16[8,2,640,128]{3,2,1,0:T(8,128)(2,1)} %bitcast.21, ...), custom_call_target="tpu_custom_call" | custom-call | flops 1400000000 | bytes 6000000 | tf_op jit(solution)/shard_map/pallas_call | solution.py:77
  105.2 5.9 %collective-permute-start.4 = (bf16[320,1024]{1,0:T(8,128)(2,1)}, bf16[320,1024]{1,0:T(8,128)(2,1)S(1)}, u32[]{:S(2)}, u32[]{:S(2)}) collective-permute-start(bf16[320,1024]{1,0:T(8,128)(2,1)} %get-tuple-element.31.refs_2_), channel_id=1, source_target_pairs={{0,8},{8,0},{1,9},{9,1},{2,10},{10,2},{3,11},{11,3},{4,12},{12,4},... | collective-permute-start | bytes 1966088 | tf_op jit(solution)/shard_map/ppermute | solution.py:43
  111.1 1.9 collective-permute-done.4.refs_3_
  113.0 1.1 copy-done.22
  114.1 2.1 %shard_map.97 = (bf16[4,640,128]{2,1,0:T(8,128)(2,1)}, bf16[4,640,128]{2,1,0:T(8,128)(2,1)S(1)}) custom-call(s32[4]{0:T(128)S(1)} %copy-done.18, bf16[640,640]{1,0:T(8,128)(2,1)S(1)} %copy-done.20, bf16[320,1024]{1,0:T(8,128)(2,1)S(1)} %copy-done.22, bf16[320,1024]{1,0:T(8,128)(2,1)S(1)} %collective-permute-done.4.refs_3_), custom_call_target="tpu_custom_call" | custom-call | flops 840000000 | bytes 4000000 | tf_op jit(solution)/shard_map/pallas_call | solution.py:77
  116.3 1.2 shard_map.100
  117.5 21.1 %all_to_all.15.refs_1_.refs_4_.refs_5_ = bf16[4,640,128]{2,1,0:T(8,128)(2,1)S(1)} all-to-all(bf16[4,640,128]{2,1,0:T(8,128)(2,1)S(1)} %get-tuple-element.34), channel_id=1, replica_groups=mesh['layer'=8,'x'=4,'core'=2,'zh'=2,'y'=4] {'y'}, dimensions={0} | all-to-all | bytes 1310720 | tf_op jit(solution)/shard_map/all_to_all | solution.py:342
  138.6 4.6 %all-to-all-start.1 = ((bf16[4,640,128]{2,1,0:T(8,128)(2,1)}), bf16[4,640,128]{2,1,0:T(8,128)(2,1)S(1)}, u32[]{:S(2)}, u32[]{:S(2)}) async-start(bf16[4,640,128]{2,1,0:T(8,128)(2,1)} %get-tuple-element.32.refs_3_), calls=%async_computation.1 | async-start | bytes 1310720 | tf_op jit(solution)/shard_map/all_to_all | solution.py:341
  143.2 4.0 %collective-permute-start.7 = (f32[320,128]{1,0:T(8,128)}, f32[320,128]{1,0:T(8,128)}, u32[]{:S(2)}, u32[]{:S(2)}) collective-permute-start(f32[320,128]{1,0:T(8,128)} %get-tuple-element.40), channel_id=1, source_target_pairs={{0,8},{8,0},{1,9},{9,1},{2,10},{10,2},{3,11},{11,3},{4,12},{12,4},... | collective-permute-start | bytes 491528 | tf_op jit(solution)/shard_map/ppermute | solution.py:43
  147.2 1.2 shard_map.99
  148.5 0.7 copy-done.11
  149.1 16.4 %collective-permute-start.6 = (bf16[320,128]{1,0:T(8,128)(2,1)}, bf16[320,128]{1,0:T(8,128)(2,1)}, u32[]{:S(2)}, u32[]{:S(2)}) collective-permute-start(bf16[320,128]{1,0:T(8,128)(2,1)} %get-tuple-element.37), channel_id=1, source_target_pairs={{0,4},{4,0},{1,5},{5,1},{2,6},{6,2},{3,7},{7,3},{8,12},{12,8},{9,1... | collective-permute-start | bytes 245768 | tf_op jit(solution)/shard_map/ppermute | solution.py:47
  165.6 1.2 shard_map.98
  166.8 0.7 copy-done.13
  167.5 3.2 %collective-permute-start.5 = (bf16[320,128]{1,0:T(8,128)(2,1)}, bf16[320,128]{1,0:T(8,128)(2,1)S(1)}, u32[]{:S(2)}, u32[]{:S(2)}) collective-permute-start(bf16[320,128]{1,0:T(8,128)(2,1)} %get-tuple-element.36), channel_id=1, source_target_pairs={{0,4},{4,0},{1,5},{5,1},{2,6},{6,2},{3,7},{7,3},{8,12},{12,8},{9,1... | collective-permute-start | bytes 245768 | tf_op jit(solution)/shard_map/ppermute | solution.py:47
  170.8 0.9 copy-done.10
  171.7 1.9 shard_map.103
  173.6 1.3 copy-done
  174.9 3.1 %shard_map.101 = (f32[640,640]{1,0:T(8,128)}, f32[8,128]{1,0:T(8,128)S(1)}) custom-call(s32[4]{0:T(128)S(1)} %copy-done.18, bf16[4,768,128]{2,1,0:T(8,128)(2,1)S(1)} %bitcast.15, bf16[4,768,128]{2,1,0:T(8,128)(2,1)S(1)} %bitcast.18, bf16[8,640,128]{2,1,0:T(8,128)(2,1)S(1)} %bitcast.19, bf16[4,640,128]{2,1,0:T(8,128)(2,1)S(1)} %all_to_all.15.refs_1_.refs_4_.refs_5_), custom_call_target="tpu_custom_call" | custom-call | flops 840000000 | bytes 6000000 | tf_op jit(solution)/shard_map/pallas_call | solution.py:77
  178.0 9.1 %collective-permute-done.5.refs_3_ = bf16[320,128]{1,0:T(8,128)(2,1)S(1)} collective-permute-done((bf16[320,128]{1,0:T(8,128)(2,1)}, bf16[320,128]{1,0:T(8,128)(2,1)S(1)}, u32[]{:S(2)}, u32[]{:S(2)}) %collective-permute-start.5) | collective-permute-done | bytes 81952 | tf_op jit(solution)/shard_map/ppermute | solution.py:47
  187.1 1.6 shard_map.102
  (46 shorter events, 0.2 us)
Async XLA Ops:
  7.2 52.7 %all-gather.11.cloned.1.call-start = ((), (), s32[]{:S(2)}) async-start(), calls=%async_computation.4 | async-start | bytes 2949120 | tf_op jit(solution)/shard_map/all_gather | solution.py:265
  7.3 1.0 copy-start.1
  8.3 1.0 copy-start.3
  9.2 0.9 copy-start.9
  10.2 0.9 copy-start.15
  11.1 68.1 %copy-start.17 = (s32[4]{0:T(128)}, s32[4]{0:T(128)S(1)}, u32[]{:S(2)}) copy-start(s32[4]{0:T(128)S(1)} %pad_add_fusion.refs_0_) | copy-start | bytes 52
  11.1 38.3 %copy-start.16 = (bf16[640,128]{1,0:T(8,128)(2,1)S(1)}, bf16[640,128]{1,0:T(8,128)(2,1)}, u32[]{:S(2)}) copy-start(bf16[640,128]{1,0:T(8,128)(2,1)} %refs_3_.4) | copy-start | bytes 491524
  11.1 38.3 %copy-start.19 = (bf16[640,640]{1,0:T(8,128)(2,1)S(1)}, bf16[640,640]{1,0:T(8,128)(2,1)}, u32[]{:S(2)}) copy-start(bf16[640,640]{1,0:T(8,128)(2,1)} %refs_1_.3) | copy-start | bytes 2457604
  12.5 85.3 %all-gather.9.cloned.1.call-start = ((), (), s32[]{:S(2)}) async-start(), calls=%async_computation.3 | async-start | bytes 2359296 | tf_op jit(solution)/shard_map/all_gather | solution.py:280
  12.5 24.4 %collective-permute-start = (bf16[768,128]{1,0:T(8,128)(2,1)S(1)}, bf16[768,128]{1,0:T(8,128)(2,1)S(1)}, u32[]{:S(2)}, u32[]{:S(2)}) collective-permute-start(bf16[768,128]{1,0:T(8,128)(2,1)S(1)} %get-tuple-element.25), channel_id=1, source_target_pairs={{0,4},{4,0},{1,5},{5,1},{2,6},{6,2},{3,7},{7,3},{8,12},{12,8},{9,1... | collective-permute-start | bytes 589832 | tf_op jit(solution)/shard_map/ppermute | solution.py:47
  52.4 0.9 copy-start.21
  53.3 8.6 %collective-permute-start.1 = (bf16[384,1024]{1,0:T(8,128)(2,1)}, bf16[384,1024]{1,0:T(8,128)(2,1)S(1)}, u32[]{:S(2)}, u32[]{:S(2)}) collective-permute-start(bf16[384,1024]{1,0:T(8,128)(2,1)} %copy-done.21), channel_id=1, source_target_pairs={{0,8},{8,0},{1,9},{9,1},{2,10},{10,2},{3,11},{11,3},{4,12},{12,4},... | collective-permute-start | bytes 2359304 | tf_op jit(solution)/shard_map/ppermute | solution.py:43
  63.5 15.7 %all-to-all-start = ((bf16[4,384,256]{2,1,0:T(8,128)(2,1)}), bf16[4,384,256]{2,1,0:T(8,128)(2,1)S(1)}, u32[]{:S(2)}, u32[]{:S(2)}) async-start(bf16[4,384,256]{2,1,0:T(8,128)(2,1)} %shard_map.94), calls=%async_computation | async-start | bytes 1572864 | tf_op jit(solution)/shard_map/all_to_all | solution.py:290
  67.5 106.0 %all-gather.13.cloned.1.call-start = ((), (), s32[]{:S(2)}) async-start(), calls=%async_computation.5 | async-start | bytes 1474560 | tf_op jit(solution)/shard_map/all_gather | solution.py:375
  67.6 30.1 %collective-permute-start.2 = (bf16[640,128]{1,0:T(8,128)(2,1)S(1)}, bf16[640,128]{1,0:T(8,128)(2,1)S(1)}, u32[]{:S(2)}, u32[]{:S(2)}) collective-permute-start(bf16[640,128]{1,0:T(8,128)(2,1)S(1)} %get-tuple-element.46), channel_id=1, source_target_pairs={{0,0},{1,16},{2,32},{3,48},{8,1},{9,17},{10,33},{11,49},{16,2},{17... | collective-permute-start | bytes 491528 | tf_op jit(solution)/shard_map/ppermute | solution.py:310
  71.8 25.9 %collective-permute-start.3 = (bf16[640,128]{1,0:T(8,128)(2,1)S(1)}, bf16[640,128]{1,0:T(8,128)(2,1)S(1)}, u32[]{:S(2)}, u32[]{:S(2)}) collective-permute-start(bf16[640,128]{1,0:T(8,128)(2,1)S(1)} %get-tuple-element.45), channel_id=1, source_target_pairs={{0,8},{1,24},{2,40},{3,56},{8,9},{9,25},{10,41},{11,57},{16,10},{1... | collective-permute-start | bytes 491528 | tf_op jit(solution)/shard_map/ppermute | solution.py:310
  97.7 0.7 copy-start.5
  97.7 0.7 copy-start.7
  98.4 14.6 %copy-start.18 = (s32[4]{0:T(128)S(1)}, s32[4]{0:T(128)}, u32[]{:S(2)}) copy-start(s32[4]{0:T(128)} %copy-done.17) | copy-start | bytes 52
  98.4 14.6 %copy-start.20 = (bf16[640,640]{1,0:T(8,128)(2,1)S(1)}, bf16[640,640]{1,0:T(8,128)(2,1)}, u32[]{:S(2)}) copy-start(bf16[640,640]{1,0:T(8,128)(2,1)} %refs_1_.3) | copy-start | bytes 2457604
  105.2 11.1 %copy-start.6 = (bf16[640,128]{1,0:T(8,128)(2,1)S(1)}, bf16[640,128]{1,0:T(8,128)(2,1)}, u32[]{:S(2)}) copy-start(bf16[640,128]{1,0:T(8,128)(2,1)} %copy-done.5) | copy-start | bytes 491524
  105.2 11.1 %copy-start.8 = (bf16[640,128]{1,0:T(8,128)(2,1)S(1)}, bf16[640,128]{1,0:T(8,128)(2,1)}, u32[]{:S(2)}) copy-start(bf16[640,128]{1,0:T(8,128)(2,1)} %copy-done.7) | copy-start | bytes 491524
  105.2 7.8 %collective-permute-start.4 = (bf16[320,1024]{1,0:T(8,128)(2,1)}, bf16[320,1024]{1,0:T(8,128)(2,1)S(1)}, u32[]{:S(2)}, u32[]{:S(2)}) collective-permute-start(bf16[320,1024]{1,0:T(8,128)(2,1)} %get-tuple-element.31.refs_2_), channel_id=1, source_target_pairs={{0,8},{8,0},{1,9},{9,1},{2,10},{10,2},{3,11},{11,3},{4,12},{12,4},... | collective-permute-start | bytes 1966088 | tf_op jit(solution)/shard_map/ppermute | solution.py:43
  113.0 1.1 copy-start.22
  117.5 53.2 %copy-start.2 = (f32[640,128]{1,0:T(8,128)S(1)}, f32[640,128]{1,0:T(8,128)}, u32[]{:S(2)}) copy-start(f32[640,128]{1,0:T(8,128)} %refs_3_.5) | copy-start | bytes 983044
  117.5 53.3 %copy-start.4 = (f32[640,128]{1,0:T(8,128)S(1)}, f32[640,128]{1,0:T(8,128)}, u32[]{:S(2)}) copy-start(f32[640,128]{1,0:T(8,128)} %refs_4_.5) | copy-start | bytes 983044
  138.6 27.0 %all-to-all-start.1 = ((bf16[4,640,128]{2,1,0:T(8,128)(2,1)}), bf16[4,640,128]{2,1,0:T(8,128)(2,1)S(1)}, u32[]{:S(2)}, u32[]{:S(2)}) async-start(bf16[4,640,128]{2,1,0:T(8,128)(2,1)} %get-tuple-element.32.refs_3_), calls=%async_computation.1 | async-start | bytes 1310720 | tf_op jit(solution)/shard_map/all_to_all | solution.py:341
  143.2 27.5 %collective-permute-start.7 = (f32[320,128]{1,0:T(8,128)}, f32[320,128]{1,0:T(8,128)}, u32[]{:S(2)}, u32[]{:S(2)}) collective-permute-start(f32[320,128]{1,0:T(8,128)} %get-tuple-element.40), channel_id=1, source_target_pairs={{0,8},{8,0},{1,9},{9,1},{2,10},{10,2},{3,11},{11,3},{4,12},{12,4},... | collective-permute-start | bytes 491528 | tf_op jit(solution)/shard_map/ppermute | solution.py:43
  148.5 0.7 copy-start.11
  149.1 28.8 %collective-permute-start.6 = (bf16[320,128]{1,0:T(8,128)(2,1)}, bf16[320,128]{1,0:T(8,128)(2,1)}, u32[]{:S(2)}, u32[]{:S(2)}) collective-permute-start(bf16[320,128]{1,0:T(8,128)(2,1)} %get-tuple-element.37), channel_id=1, source_target_pairs={{0,4},{4,0},{1,5},{5,1},{2,6},{6,2},{3,7},{7,3},{8,12},{12,8},{9,1... | collective-permute-start | bytes 245768 | tf_op jit(solution)/shard_map/ppermute | solution.py:47
  166.8 0.7 copy-start.13
  167.5 19.6 %collective-permute-start.5 = (bf16[320,128]{1,0:T(8,128)(2,1)}, bf16[320,128]{1,0:T(8,128)(2,1)S(1)}, u32[]{:S(2)}, u32[]{:S(2)}) collective-permute-start(bf16[320,128]{1,0:T(8,128)(2,1)} %get-tuple-element.36), channel_id=1, source_target_pairs={{0,4},{4,0},{1,5},{5,1},{2,6},{6,2},{3,7},{7,3},{8,12},{12,8},{9,1... | collective-permute-start | bytes 245768 | tf_op jit(solution)/shard_map/ppermute | solution.py:47
  170.8 0.9 copy-start.10
  171.7 15.4 %copy-start.12 = (f32[320,128]{1,0:T(8,128)S(1)}, f32[320,128]{1,0:T(8,128)}, u32[]{:S(2)}) copy-start(f32[320,128]{1,0:T(8,128)} %copy-done.11) | copy-start | bytes 491524
  171.7 15.4 %copy-start.14 = (f32[320,128]{1,0:T(8,128)S(1)}, f32[320,128]{1,0:T(8,128)}, u32[]{:S(2)}) copy-start(f32[320,128]{1,0:T(8,128)} %copy-done.13) | copy-start | bytes 491524
  173.6 1.3 copy-start
Sparse Core Ops, SparseCore 0:
  12.6 37.4 all-gather.10
  53.4 43.6 all-gather.8
  117.6 43.2 all-gather.12

commit v4 on v3

v4 whole, which is shorter than its diff:
```python
import itertools

import jax
import jax.numpy as jnp
from jax import lax
from jax.experimental import pallas as pl
from jax.experimental.pallas import tpu as pltpu
from jax.sharding import Mesh, PartitionSpec as P

M = 5120
C = 1024

first_beta = 0.9
second_beta = 0.95
epsilon = 1e-08

SIZES = {"x": 4, "core": 2, "zh": 2, "y": 4}
ROW = ("x", "core")
f32 = jnp.float32
bf16 = jnp.bfloat16


def pairs(axes, target):
    found = []
    for place in itertools.product(*[range(SIZES[a]) for a in axes]):
        there = target(*place)
        if there is None:
            continue
        src = dst = 0
        for a, s, d in zip(axes, place, there):
            src, dst = src * SIZES[a] + s, dst * SIZES[a] + d
        found.append((src, dst))
    return found


def dot(a, b, over_a, over_b):
    return lax.dot_general(
        a, b, (((over_a,), (over_b,)), ((), ())), preferred_element_type=f32
    )


def other_core(value):
    return lax.ppermute(value, "core", [(0, 1), (1, 0)])


def other_half(value):
    return lax.ppermute(value, "zh", [(0, 1), (1, 0)])


def spread(value, axis):
    return lax.all_to_all(
        jnp.broadcast_to(value[None], (4,) + value.shape), axis, 0, 0, tiled=True
    )


def left_source(core):
    def target(x, c, z, y):
        if x // 2 != z:
            return None
        return (y, core, z, 2 * (x % 2) + c)

    return pairs(("x", "core", "zh", "y"), target)


def shaped(shape, dtype):
    return jax.ShapeDtypeStruct(shape, dtype)


def call(
    kernel, outs, where, *operands, hbm=(), after=(), to_hbm=(), scratch=(), flops=0, moved=0, limit=40
):
    n = len(operands) + len(hbm)

    def inner(*refs):
        kernel(*refs[: n + 1], *refs[n + 1 + len(after) :])

    spaces = [pltpu.HBM if k in to_hbm else pltpu.VMEM for k in range(len(outs))]
    return pl.pallas_call(
        inner,
        out_shape=outs,
        in_specs=[pl.BlockSpec(memory_space=pltpu.SMEM)]
        + [pl.BlockSpec(memory_space=pltpu.VMEM)] * len(operands)
        + [pl.BlockSpec(memory_space=pltpu.HBM)] * len(hbm)
        + [pl.BlockSpec(memory_space=pl.ANY)] * len(after),
        out_specs=[pl.BlockSpec(memory_space=space) for space in spaces],
        scratch_shapes=scratch,
        compiler_params=pltpu.CompilerParams(vmem_limit_bytes=limit * 1024 * 1024),
        cost_estimate=pl.CostEstimate(
            flops=flops, bytes_accessed=moved, transcendentals=0
        ),
    )(where, *operands, *hbm, *after)


def copies_of(pairs_of, sems):
    made = [
        pltpu.make_async_copy(src, dst, sems.at[k])
        for k, (src, dst) in enumerate(pairs_of)
    ]
    for copy in made:
        copy.start()
    return made


def first_kernel(
    where, grad, right, first, second, mine, moments, values, squares, rounded, sems
):
    rows = pl.ds(pl.multiple_of(where[0] * 128, 128), 128)
    copies = copies_of(
        [
            (first, values),
            (second, squares),
            (grad, mine.at[pl.ds(0, 640)]),
            (right.at[rows], mine.at[pl.ds(640, 128)]),
        ],
        sems,
    )
    copies[0].wait()
    rounded[0] = values[...].astype(bf16)
    copies[1].wait()
    rounded[1] = squares[...].astype(bf16)
    last = pltpu.make_async_copy(rounded, moments, sems.at[4])
    last.start()
    for copy in (copies[2], copies[3], last):
        copy.wait()


def basis_kernel(where, near, out):
    for k in range(4):
        out[:, 128 * k : 128 * k + 128] = near[k, 640:]


def left_kernel(where, near, far, grad, left, keep, send, slabs, panel, leave, sems):
    core, z = where[1], where[2]
    for k in range(4):
        slabs[:, 128 * k : 128 * k + 128] = far[k, 640:]
        panel[:, 128 * k : 128 * k + 128] = near[k, :640, :]
        panel[:, 512 + 128 * k : 640 + 128 * k] = far[k, :640, :]
    gram = (dot(grad[...], panel[...], 0, 0) * (1.0 / M)).astype(bf16)

    def columns(t, flip):
        found = []
        for k in range(4):
            at = (2 * k + t + 4 * flip) % 8 * 128
            found += [gram[:64, at : at + 128], gram[64:, at : at + 128]]
        return jnp.concatenate(found, axis=1)

    for c in range(2):
        for half in range(2):

            @pl.when(jnp.logical_and(core == c, z == half))
            def _():
                keep[320:] = columns(c, half)
                leave[320:] = columns(1 - c, half)

    tail = pl.ds(320, 64)
    copies = copies_of([(leave.at[tail], send.at[tail])], sems)
    for part in range(2):
        cols = slice(512 * part, 512 * part + 512)
        product = dot(left[...], panel[:, cols], 0, 0).astype(bf16)
        for c in range(2):

            @pl.when(core == c)
            def _():
                keep[:320, cols] = product[320 * c : 320 * c + 320]
                leave[:320, cols] = product[320 * (1 - c) : 320 * (1 - c) + 320]

        block = (pl.ds(0, 320), pl.ds(512 * part, 512))
        copies += copies_of([(leave.at[block], send.at[block])], sems.at[pl.ds(1 + part, 1)])
    for copy in copies:
        copy.wait()


def join_kernel(where, first, second, four):
    for k in range(4):
        at = slice(256 * k, 256 * k + 256)
        four[k] = (first[:, at].astype(f32) + second[:, at].astype(f32)).astype(bf16)


def sum_kernel(where, parts, rows, gram, mine, sems):
    def total(at):
        return (
            parts[0, at].astype(f32)
            + parts[1, at].astype(f32)
            + parts[2, at].astype(f32)
            + parts[3, at].astype(f32)
        )

    mine[...] = total(slice(0, 320)).astype(bf16)
    copies = copies_of([(mine, rows.at[k]) for k in range(4)], sems)
    last = total(slice(320, 384))
    gram[:64] = last[:, :128]
    gram[64:] = last[:, 128:]
    for copy in copies:
        copy.wait()


def turn_kernel(
    where, half, moments, near, far, out, blocks, rows, rotated, right, sems
):
    row, core = where[0], where[1]
    copies = copies_of(
        [
            (src.at[pl.ds(512 * k, 512)], right.at[n, pl.ds(512 * k, 512)])
            for n, src in ((0, near), (1, far))
            for k in range(2)
        ],
        sems,
    )
    for k in range(4):
        rows[:, 256 * k : 256 * k + 256] = half[k]
    for k in range(2):
        copies[k].wait()
        at = slice(512 * k, 512 * k + 512)
        rotated[:, at] = dot(rows[:, :512], right[0, at], 1, 1)
    for k in range(2):
        copies[2 + k].wait()
        at = slice(512 * k, 512 * k + 512)
        rotated[:, at] += dot(rows[:, 512:], right[1, at], 1, 1)
    next_row = row + 1 - 2 * core
    for k, at in ((0, row), (1, next_row)):
        blocks[k] = rotated[:, pl.ds(pl.multiple_of(at * 128, 128), 128)]
    for i in range(8):
        turned = rotated[:, 128 * i : 128 * i + 128]
        old, old_sq = moments[i, 0].astype(f32), moments[i, 1].astype(f32)
        new = first_beta * old + (1.0 - first_beta) * turned
        new_sq = second_beta * old_sq + (1.0 - second_beta) * turned * turned
        rows[:, 128 * i : 128 * i + 128] = (new / (jnp.sqrt(new_sq) + epsilon)).astype(bf16)
    out[:, :512] = dot(rows[...], right[0], 1, 0).astype(bf16)
    out[:, 512:] = dot(rows[...], right[1], 1, 0).astype(bf16)


def back_kernel(where, left, mine, other, top, bottom, joined):
    core = where[1]
    joined[pl.ds(pl.multiple_of(core * 320, 320), 320)] = mine[...]
    joined[pl.ds(pl.multiple_of(320 - core * 320, 320), 320)] = other[...]
    for out, at in ((top, 0), (bottom, 320)):
        product = dot(left[at : at + 320, :], joined[...], 1, 0).astype(bf16)
        for k in range(4):
            out[k, :320] = product[:, 128 * k : 128 * k + 128]
            out[k, 320:] = product[:, 512 + 128 * k : 640 + 128 * k]


def fold(parts, rows):
    return (
        parts[0, rows].astype(f32)
        + parts[1, rows].astype(f32)
        + parts[2, rows].astype(f32)
        + parts[3, rows].astype(f32)
    )


def fold_kernel(where, parts, send):
    send[...] = fold(parts, slice(320, 640)).astype(bf16)


def fold_last_kernel(where, parts, blocks, send, theirs):
    send[...] = fold(parts, slice(320, 640)).astype(bf16)
    theirs[...] = blocks[1]


def update_kernel(where, kept, far_top, far_bottom, update):
    update[:320] = (kept[:320] + far_top[...].astype(f32)).astype(bf16)
    update[320:] = (kept[320:] + far_bottom[...].astype(f32)).astype(bf16)


def moments_kernel(
    where, blocks, theirs, first, second, top, bottom, first_new, second_new, kept
):
    core = where[1]
    kept[:320] = fold(top, slice(0, 320))
    kept[320:] = fold(bottom, slice(0, 320))
    for turned, at in ((blocks.at[0], core * 320), (theirs, 320 - core * 320)):
        rows = pl.ds(pl.multiple_of(at, 320), 320)
        value = turned[...]
        first_new[rows] = first_beta * first[rows] + (1.0 - first_beta) * value
        second_new[rows] = (
            second_beta * second[rows] + (1.0 - second_beta) * value * value
        )


def pair_kernel(where, first, second, out, mark):
    out[...] = first[...] + second[...]
    mark[...] = jnp.zeros_like(mark)


def gram_kernel(where, near, far, paired, out, corner, panel, other):
    for k in range(4):
        panel[:, 128 * k : 128 * k + 128] = near[k, :640, :]
        panel[:, 512 + 128 * k : 640 + 128 * k] = far[k, :640, :]
    for k in range(8):
        other[:, 128 * k : 128 * k + 128] = paired[k]
    out[...] = dot(panel[...], other[...], 1, 1) * (1.0 / C)
    corner[...] = out[:8, :128]


def body(grad, left_basis, right_rows, exp_avg, exp_avg_sq):
    x, core = lax.axis_index("x"), lax.axis_index("core")
    z, y = lax.axis_index("zh"), lax.axis_index("y")
    row = 2 * x + core
    where = jnp.stack([row, core, z, y]).astype(jnp.int32)

    mine, moments = call(
        first_kernel,
        [shaped((768, 128), bf16), shaped((2, 640, 128), bf16)],
        where,
        hbm=(grad, right_rows, exp_avg, exp_avg_sq),
        to_hbm=(0, 1),
        scratch=[
            pltpu.VMEM((640, 128), f32),
            pltpu.VMEM((640, 128), f32),
            pltpu.VMEM((2, 640, 128), bf16),
            pltpu.SemaphoreType.DMA((5,)),
        ],
        moved=1_500_000,
        limit=60,
    )
    far = other_half(mine)
    near_all = lax.all_gather(mine, "y", axis=0)

    moments = lax.all_gather(moments, ROW, axis=0)
    (basis_near,) = call(
        basis_kernel,
        [shaped((128, 512), bf16)],
        where,
        near_all,
        after=(far,),
        moved=1_000_000,
    )
    basis_near = lax.all_gather(basis_near, ROW, axis=0, tiled=True)
    far_all = lax.all_gather(far, "y", axis=0)

    keep, send, slabs = call(
        left_kernel,
        [shaped((384, 1024), bf16)] * 2 + [shaped((128, 512), bf16)],
        where,
        near_all,
        far_all,
        grad,
        left_basis,
        to_hbm=(1,),
        scratch=[
            pltpu.VMEM((640, 1024), bf16),
            pltpu.VMEM((384, 1024), bf16),
            pltpu.SemaphoreType.DMA((3,)),
        ],
        flops=1_000_000_000,
        moved=5_000_000,
    )
    basis_far = lax.all_gather(slabs, ROW, axis=0, tiled=True)
    (summed,) = call(
        join_kernel,
        [shaped((4, 384, 256), bf16)],
        where,
        keep,
        other_core(send),
        after=(moments[:1, :1, :16],),
        moved=2_400_000,
    )
    moments = lax.dynamic_slice_in_dim(moments, core * 320, 320, 2)
    summed = lax.all_to_all(summed, "x", 0, 0, tiled=True)
    rows, right_gram = call(
        sum_kernel,
        [shaped((4, 320, 256), bf16), shaped((128, 128), f32)],
        where,
        summed,
        after=(moments, basis_near[:16, :128]),
        to_hbm=(0,),
        scratch=[pltpu.VMEM((320, 256), bf16), pltpu.SemaphoreType.DMA((4,))],
        moved=1_500_000,
    )
    half = lax.all_to_all(rows, "x", 0, 0, tiled=True)

    axes = ("x", "core", "zh", "y")
    at = 2 * (y % 2)

    def piece(t):
        return jnp.where(
            y < 2,
            lax.dynamic_index_in_dim(near_all, at + t, 0, False)[:640],
            lax.dynamic_index_in_dim(far_all, at + t, 0, False)[:640],
        )

    pair, paired_mark = call(
        pair_kernel,
        [shaped((640, 128), bf16), shaped((8, 128), f32)],
        where,
        *[lax.ppermute(piece(t), axes, left_source(t)) for t in range(2)],
        moved=500_000,
    )

    turned, blocks = call(
        turn_kernel,
        [shaped((320, 1024), bf16), shaped((2, 320, 128), f32)],
        where,
        half,
        moments,
        hbm=(basis_near, basis_far),
        after=(paired_mark,),
        scratch=[
            pltpu.VMEM((320, 1024), bf16),
            pltpu.VMEM((320, 1024), f32),
            pltpu.VMEM((2, 1024, 512), bf16),
            pltpu.SemaphoreType.DMA((4,)),
        ],
        flops=1_400_000_000,
        moved=6_000_000,
    )
    turned_far = other_core(turned)
    top_parts, bottom_parts = call(
        back_kernel,
        [shaped((4, 640, 128), bf16)] * 2,
        where,
        left_basis,
        turned,
        turned_far,
        scratch=[pltpu.VMEM((640, 1024), bf16)],
        flops=840_000_000,
        moved=4_000_000,
    )
    top = lax.all_to_all(top_parts, "y", 0, 0, tiled=True)
    bottom = lax.all_to_all(bottom_parts, "y", 0, 0, tiled=True)
    (send,) = call(fold_kernel, [shaped((320, 128), bf16)], where, top, moved=700_000)
    arrived = [other_half(send)]
    send, theirs = call(
        fold_last_kernel,
        [shaped((320, 128), bf16), shaped((320, 128), f32)],
        where,
        bottom,
        blocks,
        moved=700_000,
    )
    arrived.append(other_half(send))

    exp_avg_new, exp_avg_sq_new, kept = call(
        moments_kernel,
        [shaped((640, 128), f32)] * 3,
        where,
        blocks,
        other_core(theirs),
        exp_avg,
        exp_avg_sq,
        top,
        bottom,
        moved=1_700_000,
    )

    paired = lax.all_gather(pair, ROW, axis=0)
    left_gram, corner = call(
        gram_kernel,
        [shaped((640, 640), f32), shaped((8, 128), f32)],
        where,
        near_all,
        far_all,
        paired,
        after=(bottom,),
        scratch=[pltpu.VMEM((640, 1024), bf16), pltpu.VMEM((640, 1024), bf16)],
        flops=840_000_000,
        moved=6_000_000,
    )
    (update,) = call(
        update_kernel,
        [shaped((640, 128), bf16)],
        where,
        kept,
        *arrived,
        after=(corner,),
        moved=700_000,
    )
    return (update, exp_avg_new, exp_avg_sq_new, left_gram, right_gram)


def solution(mesh):
    wide = Mesh(
        mesh.devices.reshape(8, 4, 2, 2, 4), ("layer", "x", "core", "zh", "y")
    )
    row, col = ("x", "core"), ("zh", "y")
    return jax.shard_map(
        body,
        mesh=wide,
        in_specs=(
            P(("layer",) + row, col),
            P(("layer",) + row, col),
            P("layer", col),
            P(("layer",) + col, row),
            P(("layer",) + col, row),
        ),
        out_specs=(
            P(("layer",) + row, col),
            P(("layer",) + col, row),
            P(("layer",) + col, row),
            P(("layer",) + row, col),
            P(("layer",) + col, row),
        ),
        check_vma=False,
    )
```

time: 196 us -> 212 us (1.082)
  the two profiles are of different devices: /device:TPU:105 before, /device:TPU:32 now
where the time goes in v4:
time: 212 us; the launch traced here: 211 us
  waiting for transfers between devices  55.5 us (26%)
  starting transfers between devices  54 us (25%)
  blocking collectives  43.7 us (21%)
  Pallas kernels  32.4 us (15%)
  between operations  14 us (7%)
  local copies, waits for them, and re-layouts  10.3 us (5%)
    pallas_call x13, Pallas kernels, call(): pl.pallas_call(inner, out_shape=outs, in_specs=[pl.BlockSpec(memory_space...  32.4 us
    all_gather x1, waiting for transfers between devices, body(): basis_far = lax.all_gather(slabs, ROW, axis=0, tiled=True)  29.6 us
    ppermute x3, starting transfers between devices, other_half(): return lax.ppermute(value, 'zh', [(0, 1), (1, 0)])  29.5 us
    all_to_all x1, blocking collectives, body(): bottom = lax.all_to_all(bottom_parts, 'y', 0, 0, tiled=True)  15.5 us
    all_gather x1, blocking collectives, body(): far_all = lax.all_gather(far, 'y', axis=0)  14.1 us
    all_gather x1, blocking collectives, body(): near_all = lax.all_gather(mine, 'y', axis=0)  14 us
    ppermute x3, waiting for transfers between devices, other_half(): return lax.ppermute(value, 'zh', [(0, 1), (1, 0)])  10.5 us
    unnamed x32, local copies, waits for them, and re-layouts  7.51 us
  transfers between devices with their start and end apart: 15, of which 9 were waited for; matrix products, arithmetic and copies ran while one was open for 2% of the time, Pallas kernels for 11%

profile of v4, /device:TPU:32, one launch (start us, length us, event | category | flops | bytes accessed | tf_op | source)
XLA Modules:
  0.0 211.3 jit_solution(10538415299986407889)
XLA Ops:
  7.8 7.9 %shard_map.92 = (bf16[768,128]{1,0:T(8,128)(2,1)}, bf16[2,640,128]{2,1,0:T(8,128)(2,1)}) custom-call(s32[4]{0:T(128)} %pad_add_fusion.refs_0_, bf16[640,128]{1,0:T(8,128)(2,1)} %refs_3_.4, bf16[1024,128]{1,0:T(8,128)(2,1)} %refs_2_.1, f32[640,128]{1,0:T(8,128)} %refs_3_.5, f32[640,128]{1,0:T(8,128)} %refs_4_.5), custom_call_target="tpu_custom_call" | custom-call | bytes 1500000 | tf_op jit(solution)/shard_map/pallas_call | solution.py:78
  15.8 15.0 %collective-permute-start = (bf16[768,128]{1,0:T(8,128)(2,1)}, bf16[768,128]{1,0:T(8,128)(2,1)S(1)}, u32[]{:S(2)}, u32[]{:S(2)}) collective-permute-start(bf16[768,128]{1,0:T(8,128)(2,1)} %get-tuple-element.25), channel_id=1, source_target_pairs={{0,4},{4,0},{1,5},{5,1},{2,6},{6,2},{3,7},{7,3},{8,12},{12,8},{9,1... | collective-permute-start | bytes 589832 | tf_op jit(solution)/shard_map/ppermute | solution.py:47
  30.8 14.0 %all-gather = bf16[3072,128]{1,0:T(8,128)(2,1)S(1)} all-gather(bf16[768,128]{1,0:T(8,128)(2,1)} %get-tuple-element.25), channel_id=2, replica_groups=mesh['layer'=8,'x'=4,'core'=2,'zh'=2,'y'=4] {'y'}, dimensions={0}, use_global_device_ids=true | all-gather | bytes 983040 | tf_op jit(solution)/shard_map/all_gather | solution.py:318
  44.8 1.6 collective-permute-done.refs_2_
  46.5 1.2 shard_map.95
  47.7 14.1 %all-gather.1 = bf16[3072,128]{1,0:T(8,128)(2,1)S(1)} all-gather(bf16[768,128]{1,0:T(8,128)(2,1)S(1)} %collective-permute-done.refs_2_), channel_id=3, replica_groups=mesh['layer'=8,'x'=4,'core'=2,'zh'=2,'y'=4] {'y'}, dimensions={0}, use_global_device_ids=true | all-gather | bytes 983040 | tf_op jit(solution)/shard_map/all_gather | solution.py:330
  61.9 3.6 %shard_map.93 = (bf16[384,1024]{1,0:T(8,128)(2,1)S(1)}, bf16[384,1024]{1,0:T(8,128)(2,1)S(1)}, bf16[128,512]{1,0:T(8,128)(2,1)}) custom-call(s32[4]{0:T(128)S(1)} %copy-done.9, bf16[4,768,128]{2,1,0:T(8,128)(2,1)S(1)} %bitcast.13, bf16[4,768,128]{2,1,0:T(8,128)(2,1)S(1)} %bitcast.16, bf16[640,128]{1,0:T(8,128)(2,1)S(1)} %copy-done.8, ...), custom_call_target="tpu_custom_call" | custom-call | flops 1000000000 | bytes 5000000 | tf_op jit(solution)/shard_map/pallas_call | solution.py:78
  65.5 0.9 copy-done.14
  66.4 1.9 collective-permute-start.1
  68.4 0.7 slice.28.refs_3_
  69.0 1.9 collective-permute-done.1.refs_2_
  70.9 2.3 %shard_map.94 = bf16[4,384,256]{2,1,0:T(8,128)(2,1)} custom-call(s32[4]{0:T(128)S(1)} %copy-done.9, bf16[384,1024]{1,0:T(8,128)(2,1)S(1)} %get-tuple-element.26.refs_1_, bf16[384,1024]{1,0:T(8,128)(2,1)} %collective-permute-done.1.refs_2_, bf16[1,1,16,128]{3,2,1,0:T(8,128)(2,1)S(1)} %slice.28.refs_3_), custom_call_target="tpu_custom_call" | custom-call | bytes 2400000 | tf_op jit(solution)/shard_map/pallas_call | solution.py:78
  73.2 4.5 %all-to-all-start = ((bf16[4,384,256]{2,1,0:T(8,128)(2,1)}), bf16[4,384,256]{2,1,0:T(8,128)(2,1)}, u32[]{:S(2)}, u32[]{:S(2)}) async-start(bf16[4,384,256]{2,1,0:T(8,128)(2,1)} %shard_map.94), calls=%async_computation | async-start | bytes 1572864 | tf_op jit(solution)/shard_map/all_to_all | solution.py:360
  77.7 0.8 fusion
  78.5 2.9 %collective-permute-start.2 = (bf16[640,128]{1,0:T(8,128)(2,1)}, bf16[640,128]{1,0:T(8,128)(2,1)}, u32[]{:S(2)}, u32[]{:S(2)}) collective-permute-start(bf16[640,128]{1,0:T(8,128)(2,1)} %get-tuple-element.46), channel_id=1, source_target_pairs={{0,0},{1,16},{2,32},{3,48},{8,1},{9,17},{10,33},{11,49},{16,2},{17... | collective-permute-start | bytes 491528 | tf_op jit(solution)/shard_map/ppermute | solution.py:387
  81.4 4.0 %collective-permute-start.3 = (bf16[640,128]{1,0:T(8,128)(2,1)}, bf16[640,128]{1,0:T(8,128)(2,1)}, u32[]{:S(2)}, u32[]{:S(2)}) collective-permute-start(bf16[640,128]{1,0:T(8,128)(2,1)} %get-tuple-element.45), channel_id=1, source_target_pairs={{0,8},{1,24},{2,40},{3,56},{8,9},{9,25},{10,41},{11,57},{16,10},{1... | collective-permute-start | bytes 491528 | tf_op jit(solution)/shard_map/ppermute | solution.py:387
  85.4 4.0 %all-gather.9.cloned.1.call-done.refs_3_ = bf16[1024,512]{1,0:T(8,128)(2,1)} async-done(((bf16[128,512]{1,0:T(8,128)(2,1)}), bf16[1024,512]{1,0:T(8,128)(2,1)}) %all-gather.9.cloned.1.call-update) | async-done | bytes 1048592 | tf_op jit(solution)/shard_map/all_gather | solution.py:329
  89.4 0.7 slice.29.refs_3_
  90.0 1.4 constant_dynamic-slice_fusion.refs_2_
  91.5 0.9 all-to-all-done.refs_1_
  92.4 2.8 %shard_map.96 = (bf16[4,320,256]{2,1,0:T(8,128)(2,1)S(1)}, f32[128,128]{1,0:T(8,128)}) custom-call(s32[4]{0:T(128)S(1)} %copy-done.9, bf16[4,384,256]{2,1,0:T(8,128)(2,1)} %all-to-all-done.refs_1_, bf16[8,2,320,128]{3,2,1,0:T(8,128)(2,1)S(1)} %constant_dynamic-slice_fusion.refs_2_, bf16[16,128]{1,0:T(8,128)(2,1)S(1)} %slice.29.refs_3_), custom_call_target="tpu_custom_call" | custom-call | bytes 1500000 | tf_op jit(solution)/shard_map/pallas_call | solution.py:78
  95.2 0.8 copy-done.5
  96.0 3.5 %all-to-all-start.1 = ((bf16[4,320,256]{2,1,0:T(8,128)(2,1)}), bf16[4,320,256]{2,1,0:T(8,128)(2,1)S(1)}, u32[]{:S(2)}, u32[]{:S(2)}) async-start(bf16[4,320,256]{2,1,0:T(8,128)(2,1)} %copy-done.5), calls=%async_computation.1 | async-start | bytes 1310720 | tf_op jit(solution)/shard_map/all_to_all | solution.py:371
  99.6 1.0 shard_map.97
  100.6 0.7 copy-done.7
  101.3 29.6 %all-gather.11.cloned.1.call-done.refs_4_ = bf16[1024,512]{1,0:T(8,128)(2,1)} async-done(((bf16[128,512]{1,0:T(8,128)(2,1)}), bf16[1024,512]{1,0:T(8,128)(2,1)}) %all-gather.11.cloned.1.call-update) | async-done | bytes 1048592 | tf_op jit(solution)/shard_map/all_gather | solution.py:349
  131.0 1.2 copy-done.10
  132.2 1.2 copy-done.11
  133.4 3.5 %shard_map.98 = (bf16[320,1024]{1,0:T(8,128)(2,1)S(1)}, f32[2,320,128]{2,1,0:T(8,128)S(1)}) custom-call(s32[4]{0:T(128)S(1)} %copy-done.9, bf16[4,320,256]{2,1,0:T(8,128)(2,1)S(1)} %all-to-all-done.1.refs_1_, bf16[8,2,320,128]{3,2,1,0:T(8,128)(2,1)S(1)} %constant_dynamic-slice_fusion.refs_2_, bf16[1024,512]{1,0:T(8,128)(2,1)S(1)} %copy-done.10, ...), custom_call_target="tpu_custom_call" | custom-call | flops 1400000000 | bytes 6000000 | tf_op jit(solution)/shard_map/pallas_call | solution.py:78
  136.9 0.7 copy-done.1
  137.6 2.1 %collective-permute-start.4 = (bf16[320,1024]{1,0:T(8,128)(2,1)S(1)}, bf16[320,1024]{1,0:T(8,128)(2,1)S(1)}, u32[]{:S(2)}, u32[]{:S(2)}) collective-permute-start(bf16[320,1024]{1,0:T(8,128)(2,1)S(1)} %get-tuple-element.33.refs_2_), channel_id=1, source_target_pairs={{0,8},{8,0},{1,9},{9,1},{2,10},{10,2},{3,11},{11,3},{4,12},{12,4},... | collective-permute-start | bytes 1966088 | tf_op jit(solution)/shard_map/ppermute | solution.py:43
  139.8 1.8 collective-permute-done.4.refs_3_
  141.6 1.8 shard_map.99
  143.4 15.5 %all_to_all.20.refs_1_.refs_6_.refs_4_ = bf16[4,640,128]{2,1,0:T(8,128)(2,1)S(1)} all-to-all(bf16[4,640,128]{2,1,0:T(8,128)(2,1)S(1)} %get-tuple-element.34), channel_id=1, replica_groups=mesh['layer'=8,'x'=4,'core'=2,'zh'=2,'y'=4] {'y'}, dimensions={0} | all-to-all | bytes 1310720 | tf_op jit(solution)/shard_map/all_to_all | solution.py:421
  159.0 3.5 %all-to-all-start.3 = ((bf16[4,640,128]{2,1,0:T(8,128)(2,1)}), bf16[4,640,128]{2,1,0:T(8,128)(2,1)S(1)}, u32[]{:S(2)}, u32[]{:S(2)}) async-start(bf16[4,640,128]{2,1,0:T(8,128)(2,1)} %copy-done.6), calls=%async_computation.3 | async-start | bytes 1310720 | tf_op jit(solution)/shard_map/all_to_all | solution.py:420
  162.5 1.2 shard_map.100
  163.7 0.6 copy-done.15
  164.3 1.9 collective-permute-start.5
  166.3 6.6 %all-to-all-done.3.refs_5_.refs_1_ = bf16[4,640,128]{2,1,0:T(8,128)(2,1)S(1)} async-done(((bf16[4,640,128]{2,1,0:T(8,128)(2,1)}), bf16[4,640,128]{2,1,0:T(8,128)(2,1)S(1)}, u32[]{:S(2)}, u32[]{:S(2)}) %all-to-all-start.3) | async-done | bytes 655392 | tf_op jit(solution)/shard_map/all_to_all | solution.py:420
  172.9 1.2 shard_map.102
  174.1 11.9 %collective-permute-start.6 = (bf16[320,128]{1,0:T(8,128)(2,1)}, bf16[320,128]{1,0:T(8,128)(2,1)S(1)}, u32[]{:S(2)}, u32[]{:S(2)}) collective-permute-start(bf16[320,128]{1,0:T(8,128)(2,1)} %shard_map.102), channel_id=1, source_target_pairs={{0,4},{4,0},{1,5},{5,1},{2,6},{6,2},{3,7},{7,3},{8,12},{12,8},{9,1... | collective-permute-start | bytes 245768 | tf_op jit(solution)/shard_map/ppermute | solution.py:47
  186.0 2.6 %collective-permute-start.7 = (bf16[320,128]{1,0:T(8,128)(2,1)}, bf16[320,128]{1,0:T(8,128)(2,1)S(1)}, u32[]{:S(2)}, u32[]{:S(2)}) collective-permute-start(bf16[320,128]{1,0:T(8,128)(2,1)} %copy-done.15), channel_id=1, source_target_pairs={{0,4},{4,0},{1,5},{5,1},{2,6},{6,2},{3,7},{7,3},{8,12},{12,8},{9,1... | collective-permute-start | bytes 245768 | tf_op jit(solution)/shard_map/ppermute | solution.py:47
  188.7 1.3 copy-done
  190.0 3.1 %shard_map.103 = (f32[640,640]{1,0:T(8,128)}, f32[8,128]{1,0:T(8,128)S(1)}) custom-call(s32[4]{0:T(128)S(1)} %copy-done.9, bf16[4,768,128]{2,1,0:T(8,128)(2,1)S(1)} %bitcast.15, bf16[4,768,128]{2,1,0:T(8,128)(2,1)S(1)} %bitcast.18, bf16[8,640,128]{2,1,0:T(8,128)(2,1)S(1)} %bitcast.19, bf16[4,640,128]{2,1,0:T(8,128)(2,1)S(1)} %all_to_all.20.refs_1_.refs_6_.refs_4_), custom_call_target="tpu_custom_call" | custom-call | flops 840000000 | bytes 6000000 | tf_op jit(solution)/shard_map/pallas_call | solution.py:78
  193.2 1.5 shard_map.101
  194.6 2.0 collective-permute-done.6.refs_2_
  196.7 6.8 %collective-permute-done.7.refs_3_ = bf16[320,128]{1,0:T(8,128)(2,1)S(1)} collective-permute-done((bf16[320,128]{1,0:T(8,128)(2,1)}, bf16[320,128]{1,0:T(8,128)(2,1)S(1)}, u32[]{:S(2)}, u32[]{:S(2)}) %collective-permute-start.7) | collective-permute-done | bytes 81952 | tf_op jit(solution)/shard_map/ppermute | solution.py:47
  203.5 1.2 shard_map.104
  (39 shorter events, 0.9 us)
Async XLA Ops:
  7.2 61.2 %all-gather.13.cloned.1.call-start = ((), (), s32[]{:S(2)}) async-start(), calls=%async_computation.6 | async-start | bytes 2949120 | tf_op jit(solution)/shard_map/all_gather | solution.py:320
  7.8 38.6 %copy-start.9 = (s32[4]{0:T(128)S(1)}, s32[4]{0:T(128)}, u32[]{:S(2)}) copy-start(s32[4]{0:T(128)} %pad_add_fusion.refs_0_) | copy-start | bytes 52
  15.7 46.1 %copy-start.8 = (bf16[640,128]{1,0:T(8,128)(2,1)S(1)}, bf16[640,128]{1,0:T(8,128)(2,1)}, u32[]{:S(2)}) copy-start(bf16[640,128]{1,0:T(8,128)(2,1)} %refs_3_.4) | copy-start | bytes 491524
  15.8 46.1 %copy-start.12 = (bf16[640,640]{1,0:T(8,128)(2,1)S(1)}, bf16[640,640]{1,0:T(8,128)(2,1)}, u32[]{:S(2)}) copy-start(bf16[640,640]{1,0:T(8,128)(2,1)} %refs_1_.3) | copy-start | bytes 2457604
  15.8 73.6 %all-gather.9.cloned.1.call-start = ((), (), s32[]{:S(2)}) async-start(), calls=%async_computation.4 | async-start | bytes 1179648 | tf_op jit(solution)/shard_map/all_gather | solution.py:329
  15.8 30.6 %collective-permute-start = (bf16[768,128]{1,0:T(8,128)(2,1)}, bf16[768,128]{1,0:T(8,128)(2,1)S(1)}, u32[]{:S(2)}, u32[]{:S(2)}) collective-permute-start(bf16[768,128]{1,0:T(8,128)(2,1)} %get-tuple-element.25), channel_id=1, source_target_pairs={{0,4},{4,0},{1,5},{5,1},{2,6},{6,2},{3,7},{7,3},{8,12},{12,8},{9,1... | collective-permute-start | bytes 589832 | tf_op jit(solution)/shard_map/ppermute | solution.py:47
  47.7 83.3 %all-gather.11.cloned.1.call-start = ((), (), s32[]{:S(2)}) async-start(), calls=%async_computation.5 | async-start | bytes 1179648 | tf_op jit(solution)/shard_map/all_gather | solution.py:349
  65.5 0.9 copy-start.14
  66.4 4.5 %collective-permute-start.1 = (bf16[384,1024]{1,0:T(8,128)(2,1)}, bf16[384,1024]{1,0:T(8,128)(2,1)}, u32[]{:S(2)}, u32[]{:S(2)}) collective-permute-start(bf16[384,1024]{1,0:T(8,128)(2,1)} %copy-done.14), channel_id=1, source_target_pairs={{0,8},{8,0},{1,9},{9,1},{2,10},{10,2},{3,11},{11,3},{4,12},{12,4},... | collective-permute-start | bytes 2359304 | tf_op jit(solution)/shard_map/ppermute | solution.py:43
  73.2 19.2 %all-to-all-start = ((bf16[4,384,256]{2,1,0:T(8,128)(2,1)}), bf16[4,384,256]{2,1,0:T(8,128)(2,1)}, u32[]{:S(2)}, u32[]{:S(2)}) async-start(bf16[4,384,256]{2,1,0:T(8,128)(2,1)} %shard_map.94), calls=%async_computation | async-start | bytes 1572864 | tf_op jit(solution)/shard_map/all_to_all | solution.py:360
  78.5 21.1 %collective-permute-start.2 = (bf16[640,128]{1,0:T(8,128)(2,1)}, bf16[640,128]{1,0:T(8,128)(2,1)}, u32[]{:S(2)}, u32[]{:S(2)}) collective-permute-start(bf16[640,128]{1,0:T(8,128)(2,1)} %get-tuple-element.46), channel_id=1, source_target_pairs={{0,0},{1,16},{2,32},{3,48},{8,1},{9,17},{10,33},{11,49},{16,2},{17... | collective-permute-start | bytes 491528 | tf_op jit(solution)/shard_map/ppermute | solution.py:387
  81.4 18.2 %collective-permute-start.3 = (bf16[640,128]{1,0:T(8,128)(2,1)}, bf16[640,128]{1,0:T(8,128)(2,1)}, u32[]{:S(2)}, u32[]{:S(2)}) collective-permute-start(bf16[640,128]{1,0:T(8,128)(2,1)} %get-tuple-element.45), channel_id=1, source_target_pairs={{0,8},{1,24},{2,40},{3,56},{8,9},{9,25},{10,41},{11,57},{16,10},{1... | collective-permute-start | bytes 491528 | tf_op jit(solution)/shard_map/ppermute | solution.py:387
  95.2 0.8 copy-start.5
  96.0 34.9 %all-to-all-start.1 = ((bf16[4,320,256]{2,1,0:T(8,128)(2,1)}), bf16[4,320,256]{2,1,0:T(8,128)(2,1)S(1)}, u32[]{:S(2)}, u32[]{:S(2)}) async-start(bf16[4,320,256]{2,1,0:T(8,128)(2,1)} %copy-done.5), calls=%async_computation.1 | async-start | bytes 1310720 | tf_op jit(solution)/shard_map/all_to_all | solution.py:371
  99.5 89.2 %all-gather.15.cloned.1.call-start = ((), (), s32[]{:S(2)}) async-start(), calls=%async_computation.7 | async-start | bytes 1474560 | tf_op jit(solution)/shard_map/all_gather | solution.py:447
  100.6 0.7 copy-start.7
  131.0 1.2 copy-start.10
  132.2 1.2 copy-start.11
  133.4 8.2 %copy-start.13 = (bf16[640,640]{1,0:T(8,128)(2,1)S(1)}, bf16[640,640]{1,0:T(8,128)(2,1)}, u32[]{:S(2)}) copy-start(bf16[640,640]{1,0:T(8,128)(2,1)} %refs_1_.3) | copy-start | bytes 2457604
  136.9 0.7 copy-start.1
  137.6 4.0 %collective-permute-start.4 = (bf16[320,1024]{1,0:T(8,128)(2,1)S(1)}, bf16[320,1024]{1,0:T(8,128)(2,1)S(1)}, u32[]{:S(2)}, u32[]{:S(2)}) collective-permute-start(bf16[320,1024]{1,0:T(8,128)(2,1)S(1)} %get-tuple-element.33.refs_2_), channel_id=1, source_target_pairs={{0,8},{8,0},{1,9},{9,1},{2,10},{10,2},{3,11},{11,3},{4,12},{12,4},... | collective-permute-start | bytes 1966088 | tf_op jit(solution)/shard_map/ppermute | solution.py:43
  143.4 15.6 %copy-start.6 = (bf16[4,640,128]{2,1,0:T(8,128)(2,1)}, bf16[4,640,128]{2,1,0:T(8,128)(2,1)S(1)}, u32[]{:S(2)}) copy-start(bf16[4,640,128]{2,1,0:T(8,128)(2,1)S(1)} %get-tuple-element.36) | copy-start | bytes 1966084
  143.4 19.0 %copy-start.2 = (f32[2,320,128]{2,1,0:T(8,128)S(1)}, f32[2,320,128]{2,1,0:T(8,128)}, u32[]{:S(2)}) copy-start(f32[2,320,128]{2,1,0:T(8,128)} %copy-done.1) | copy-start | bytes 983044
  159.0 13.9 %all-to-all-start.3 = ((bf16[4,640,128]{2,1,0:T(8,128)(2,1)}), bf16[4,640,128]{2,1,0:T(8,128)(2,1)S(1)}, u32[]{:S(2)}, u32[]{:S(2)}) async-start(bf16[4,640,128]{2,1,0:T(8,128)(2,1)} %copy-done.6), calls=%async_computation.3 | async-start | bytes 1310720 | tf_op jit(solution)/shard_map/all_to_all | solution.py:420
  163.7 0.6 copy-start.15
  164.3 28.8 %collective-permute-start.5 = (f32[320,128]{1,0:T(8,128)}, f32[320,128]{1,0:T(8,128)S(1)}, u32[]{:S(2)}, u32[]{:S(2)}) collective-permute-start(f32[320,128]{1,0:T(8,128)} %get-tuple-element.35), channel_id=1, source_target_pairs={{0,8},{8,0},{1,9},{9,1},{2,10},{10,2},{3,11},{11,3},{4,12},{12,4},... | collective-permute-start | bytes 491528 | tf_op jit(solution)/shard_map/ppermute | solution.py:43
  174.1 22.5 %collective-permute-start.6 = (bf16[320,128]{1,0:T(8,128)(2,1)}, bf16[320,128]{1,0:T(8,128)(2,1)S(1)}, u32[]{:S(2)}, u32[]{:S(2)}) collective-permute-start(bf16[320,128]{1,0:T(8,128)(2,1)} %shard_map.102), channel_id=1, source_target_pairs={{0,4},{4,0},{1,5},{5,1},{2,6},{6,2},{3,7},{7,3},{8,12},{12,8},{9,1... | collective-permute-start | bytes 245768 | tf_op jit(solution)/shard_map/ppermute | solution.py:47
  186.0 17.5 %collective-permute-start.7 = (bf16[320,128]{1,0:T(8,128)(2,1)}, bf16[320,128]{1,0:T(8,128)(2,1)S(1)}, u32[]{:S(2)}, u32[]{:S(2)}) collective-permute-start(bf16[320,128]{1,0:T(8,128)(2,1)} %copy-done.15), channel_id=1, source_target_pairs={{0,4},{4,0},{1,5},{5,1},{2,6},{6,2},{3,7},{7,3},{8,12},{12,8},{9,1... | collective-permute-start | bytes 245768 | tf_op jit(solution)/shard_map/ppermute | solution.py:47
  188.7 1.3 copy-start
  190.0 3.1 %copy-start.3 = (f32[640,128]{1,0:T(8,128)S(1)}, f32[640,128]{1,0:T(8,128)}, u32[]{:S(2)}) copy-start(f32[640,128]{1,0:T(8,128)} %refs_3_.5) | copy-start | bytes 983044
  190.0 3.1 %copy-start.4 = (f32[640,128]{1,0:T(8,128)S(1)}, f32[640,128]{1,0:T(8,128)}, u32[]{:S(2)}) copy-start(f32[640,128]{1,0:T(8,128)} %refs_4_.5) | copy-start | bytes 983044
Sparse Core Ops, SparseCore 0:
  15.9 37.8 all-gather.12
  56.5 32.8 all-gather.8
  91.5 39.3 all-gather.10
  133.5 31.4 all-gather.14

commit v5 on v3

v5 whole, which is shorter than its diff:
```python
import itertools

import jax
import jax.numpy as jnp
from jax import lax
from jax.experimental import pallas as pl
from jax.experimental.pallas import tpu as pltpu
from jax.sharding import Mesh, PartitionSpec as P

M = 5120
C = 1024

first_beta = 0.9
second_beta = 0.95
epsilon = 1e-08

SIZES = {"x": 4, "core": 2, "zh": 2, "y": 4}
ROW = ("x", "core")
f32 = jnp.float32
bf16 = jnp.bfloat16


def pairs(axes, target):
    found = []
    for place in itertools.product(*[range(SIZES[a]) for a in axes]):
        there = target(*place)
        if there is None:
            continue
        src = dst = 0
        for a, s, d in zip(axes, place, there):
            src, dst = src * SIZES[a] + s, dst * SIZES[a] + d
        found.append((src, dst))
    return found


def dot(a, b, over_a, over_b):
    return lax.dot_general(
        a, b, (((over_a,), (over_b,)), ((), ())), preferred_element_type=f32
    )


def other_core(value):
    return lax.ppermute(value, "core", [(0, 1), (1, 0)])


def other_half(value):
    return lax.ppermute(value, "zh", [(0, 1), (1, 0)])


def spread(value, axis):
    return lax.all_to_all(
        jnp.broadcast_to(value[None], (4,) + value.shape), axis, 0, 0, tiled=True
    )


def left_source(core):
    def target(x, c, z, y):
        if x // 2 != z:
            return None
        return (y, core, z, 2 * (x % 2) + c)

    return pairs(("x", "core", "zh", "y"), target)


def shaped(shape, dtype):
    return jax.ShapeDtypeStruct(shape, dtype)


def call(
    kernel, outs, where, *operands, after=(), scratch=(), flops=0, moved=0, limit=24
):
    n = len(operands)

    def inner(*refs):
        kernel(*refs[: n + 1], *refs[n + 1 + len(after) :])

    return pl.pallas_call(
        inner,
        out_shape=outs,
        in_specs=[pl.BlockSpec(memory_space=pltpu.SMEM)]
        + [pl.BlockSpec(memory_space=pltpu.VMEM)] * n
        + [pl.BlockSpec(memory_space=pl.ANY)] * len(after),
        scratch_shapes=scratch,
        compiler_params=pltpu.CompilerParams(vmem_limit_bytes=limit * 1024 * 1024),
        cost_estimate=pl.CostEstimate(
            flops=flops, bytes_accessed=moved, transcendentals=0
        ),
    )(where, *operands, *after)


def first_kernel(where, grad, right, first, second, mine, moments):
    mine[:640] = grad[...]
    mine[640:] = right[pl.ds(pl.multiple_of(where[0] * 128, 128), 128)]
    moments[0] = first[...].astype(bf16)
    moments[1] = second[...].astype(bf16)


def left_kernel(where, near, far, grad, left, keep, send, slabs, panel):
    core, z = where[1], where[2]
    for k in range(4):
        slabs[:, 128 * k : 128 * k + 128] = near[k, 640:]
        slabs[:, 512 + 128 * k : 640 + 128 * k] = far[k, 640:]
        panel[:, 128 * k : 128 * k + 128] = near[k, :640, :]
        panel[:, 512 + 128 * k : 640 + 128 * k] = far[k, :640, :]

    product = dot(left[...], panel[...], 0, 0).astype(bf16)
    gram = (dot(grad[...], panel[...], 0, 0) * (1.0 / M)).astype(bf16)

    def columns(t, flip):
        found = []
        for k in range(4):
            block = 2 * k + t
            if flip:
                block = (block + 4) % 8
            at = block * 128
            found += [gram[:64, at : at + 128], gram[64:, at : at + 128]]
        return jnp.concatenate(found, axis=1)

    for c in range(2):

        @pl.when(core == c)
        def _():
            keep[:320] = product[320 * c : 320 * c + 320]
            send[:320] = product[320 * (1 - c) : 320 * (1 - c) + 320]
            for half in range(2):

                @pl.when(z == half)
                def _():
                    keep[320:] = columns(c, half == 1)
                    send[320:] = columns(1 - c, half == 1)


def join_kernel(where, first, second, four):
    for k in range(4):
        at = slice(256 * k, 256 * k + 256)
        four[k] = (first[:, at].astype(f32) + second[:, at].astype(f32)).astype(bf16)


def sum_kernel(where, parts, rows, gram):
    total = (
        parts[0].astype(f32)
        + parts[1].astype(f32)
        + parts[2].astype(f32)
        + parts[3].astype(f32)
    )
    mine = total[:320].astype(bf16)
    for k in range(4):
        rows[k] = mine
    gram[:64] = total[320:, :128]
    gram[64:] = total[320:, 128:]


def turn_kernel(where, half, moments, basis, out, own, rows, rotated):
    row, core = where[0], where[1]
    for k in range(4):
        rows[:, 256 * k : 256 * k + 256] = half[k]
    rotated[...] = dot(rows[...], basis[...], 1, 1)
    next_row = row + 1 - 2 * core
    own[...] = rotated[:, pl.ds(pl.multiple_of(row * 128, 128), 128)]
    theirs = rotated[:, pl.ds(pl.multiple_of(next_row * 128, 128), 128)]
    out[:, 1024:] = theirs.astype(bf16)
    for i in range(8):
        turned = rotated[:, 128 * i : 128 * i + 128]
        old, old_sq = moments[i, 0].astype(f32), moments[i, 1].astype(f32)
        new = first_beta * old + (1.0 - first_beta) * turned
        new_sq = second_beta * old_sq + (1.0 - second_beta) * turned * turned
        rows[:, 128 * i : 128 * i + 128] = (new / (jnp.sqrt(new_sq) + epsilon)).astype(bf16)
    out[:, :1024] = dot(rows[...], basis[...], 1, 0).astype(bf16)


def back_kernel(where, left, mine, other, out, joined):
    core = where[1]
    joined[pl.ds(pl.multiple_of(core * 320, 320), 320)] = mine[:, :1024]
    joined[pl.ds(pl.multiple_of(320 - core * 320, 320), 320)] = other[:, :1024]
    product = dot(left[...], joined[...], 1, 0).astype(bf16)
    for k in range(4):
        out[k, :640] = product[:, 128 * k : 128 * k + 128]
        out[k, 640:] = product[:, 512 + 128 * k : 640 + 128 * k]


def fold(parts, rows):
    return (
        parts[0, rows].astype(f32)
        + parts[1, rows].astype(f32)
        + parts[2, rows].astype(f32)
        + parts[3, rows].astype(f32)
    )


def fold_kernel(where, parts, send):
    send[...] = fold(parts, slice(640, 1280)).astype(bf16)


def update_kernel(where, kept, arrived, update):
    update[...] = (kept[...] + arrived[...].astype(f32)).astype(bf16)


def moments_kernel(
    where, own, other, first, second, parts, first_new, second_new, kept
):
    core = where[1]
    kept[...] = fold(parts, slice(0, 640))
    theirs = other[:, 1024:].astype(f32)
    for value, at in ((own[...], core * 320), (theirs, 320 - core * 320)):
        rows = pl.ds(pl.multiple_of(at, 320), 320)
        first_new[rows] = first_beta * first[rows] + (1.0 - first_beta) * value
        second_new[rows] = (
            second_beta * second[rows] + (1.0 - second_beta) * value * value
        )


def pair_kernel(where, first, second, out, mark):
    out[...] = first[...] + second[...]
    mark[...] = jnp.zeros_like(mark)


def gram_kernel(where, near, far, paired, out, panel, other):
    for k in range(4):
        panel[:, 128 * k : 128 * k + 128] = near[k, :640, :]
        panel[:, 512 + 128 * k : 640 + 128 * k] = far[k, :640, :]
    for k in range(8):
        other[:, 128 * k : 128 * k + 128] = paired[k]
    out[...] = dot(panel[...], other[...], 1, 1) * (1.0 / C)


def body(grad, left_basis, right_rows, exp_avg, exp_avg_sq):
    x, core = lax.axis_index("x"), lax.axis_index("core")
    z, y = lax.axis_index("zh"), lax.axis_index("y")
    row = 2 * x + core
    where = jnp.stack([row, core, z, y]).astype(jnp.int32)

    mine, moments = call(
        first_kernel,
        [shaped((768, 128), bf16), shaped((2, 640, 128), bf16)],
        where,
        grad,
        right_rows,
        exp_avg,
        exp_avg_sq,
        moved=1_500_000,
        limit=60,
    )
    far = other_half(mine)
    near_all = lax.all_gather(mine, "y", axis=0)

    moments = lax.all_gather(moments, ROW, axis=0)
    far_all = lax.all_gather(far, "y", axis=0)

    keep, send, slabs = call(
        left_kernel,
        [shaped((384, 1024), bf16)] * 2 + [shaped((128, 1024), bf16)],
        where,
        near_all,
        far_all,
        grad,
        left_basis,
        scratch=[pltpu.VMEM((640, 1024), bf16)],
        flops=1_000_000_000,
        moved=5_000_000,
    )
    basis = lax.all_gather(slabs, ROW, axis=0, tiled=True)
    (summed,) = call(
        join_kernel,
        [shaped((4, 384, 256), bf16)],
        where,
        keep,
        other_core(send),
        after=(moments[:1, :1, :16],),
        moved=2_400_000,
    )
    moments = lax.dynamic_slice_in_dim(moments, core * 320, 320, 2)
    summed = lax.all_to_all(summed, "x", 0, 0, tiled=True)

    axes = ("x", "core", "zh", "y")
    at = 2 * (y % 2)

    def piece(t):
        return jnp.where(
            y < 2,
            lax.dynamic_index_in_dim(near_all, at + t, 0, False)[:640],
            lax.dynamic_index_in_dim(far_all, at + t, 0, False)[:640],
        )

    pair, paired_mark = call(
        pair_kernel,
        [shaped((640, 128), bf16), shaped((8, 128), f32)],
        where,
        *[lax.ppermute(piece(t), axes, left_source(t)) for t in range(2)],
        moved=500_000,
    )

    rows, right_gram = call(
        sum_kernel,
        [shaped((4, 320, 256), bf16), shaped((128, 128), f32)],
        where,
        summed,
        after=(moments[:1, :1, :16], paired_mark),
        moved=1_500_000,
    )
    half = lax.all_to_all(rows, "x", 0, 0, tiled=True)

    turned, own = call(
        turn_kernel,
        [shaped((320, 1152), bf16), shaped((320, 128), f32)],
        where,
        half,
        moments,
        basis,
        scratch=[pltpu.VMEM((320, 1024), bf16), pltpu.VMEM((320, 1024), f32)],
        flops=1_400_000_000,
        moved=6_000_000,
    )
    turned_far = other_core(turned)
    (parts,) = call(
        back_kernel,
        [shaped((4, 1280, 128), bf16)],
        where,
        left_basis,
        turned,
        turned_far,
        scratch=[pltpu.VMEM((640, 1024), bf16)],
        flops=840_000_000,
        moved=4_000_000,
    )
    parts = lax.all_to_all(parts, "y", 0, 0, tiled=True)
    (send,) = call(
        fold_kernel, [shaped((640, 128), bf16)], where, parts, moved=1_400_000
    )
    arrived = other_half(send)

    paired = lax.all_gather(pair, ROW, axis=0)
    (left_gram,) = call(
        gram_kernel,
        [shaped((640, 640), f32)],
        where,
        near_all,
        far_all,
        paired,
        after=(send,),
        scratch=[pltpu.VMEM((640, 1024), bf16), pltpu.VMEM((640, 1024), bf16)],
        flops=10_000,
        moved=10_000,
    )
    exp_avg_new, exp_avg_sq_new, kept = call(
        moments_kernel,
        [shaped((640, 128), f32)] * 3,
        where,
        own,
        turned_far,
        exp_avg,
        exp_avg_sq,
        parts,
        moved=10_000,
    )

    (update,) = call(
        update_kernel,
        [shaped((640, 128), bf16)],
        where,
        kept,
        arrived,
        moved=700_000,
    )
    return (update, exp_avg_new, exp_avg_sq_new, left_gram, right_gram)


def solution(mesh):
    wide = Mesh(
        mesh.devices.reshape(8, 4, 2, 2, 4), ("layer", "x", "core", "zh", "y")
    )
    row, col = ("x", "core"), ("zh", "y")
    return jax.shard_map(
        body,
        mesh=wide,
        in_specs=(
            P(("layer",) + row, col),
            P(("layer",) + row, col),
            P("layer", col),
            P(("layer",) + col, row),
            P(("layer",) + col, row),
        ),
        out_specs=(
            P(("layer",) + row, col),
            P(("layer",) + col, row),
            P(("layer",) + col, row),
            P(("layer",) + row, col),
            P(("layer",) + col, row),
        ),
        check_vma=False,
    )
```

time: 196 us -> 185 us (0.944)
  the two profiles are of different devices: /device:TPU:105 before, /device:TPU:32 now
where the time goes in v5:
time: 185 us; the launch traced here: 184 us
  starting transfers between devices  62.9 us (34%)
  blocking collectives  51.7 us (28%)
  waiting for transfers between devices  28.2 us (15%)
  Pallas kernels  20.6 us (11%)
  between operations  13.9 us (8%)
  local copies, waits for them, and re-layouts  6.01 us (3%)
    ppermute x2, starting transfers between devices, other_half(): return lax.ppermute(value, 'zh', [(0, 1), (1, 0)])  26.5 us
    all_to_all x1, blocking collectives, body(): parts = lax.all_to_all(parts, 'y', 0, 0, tiled=True)  23.5 us
    pallas_call x11, Pallas kernels, call(): pl.pallas_call(inner, out_shape=outs, in_specs=[pl.BlockSpec(memory_space...  20.6 us
    all_to_all x1, starting transfers between devices, body(): half = lax.all_to_all(rows, 'x', 0, 0, tiled=True)  15.4 us
    all_gather x1, blocking collectives, body(): far_all = lax.all_gather(far, 'y', axis=0)  14.2 us
    all_gather x1, blocking collectives, body(): near_all = lax.all_gather(mine, 'y', axis=0)  14 us
    ppermute x2, starting transfers between devices, other_core(): return lax.ppermute(value, 'core', [(0, 1), (1, 0)])  11.1 us
    ppermute x2, waiting for transfers between devices, other_half(): return lax.ppermute(value, 'zh', [(0, 1), (1, 0)])  9.94 us
  transfers between devices with their start and end apart: 11, of which 7 were waited for; matrix products, arithmetic and copies ran while one was open for 1% of the time, Pallas kernels for 9%

profile of v5, /device:TPU:32, one launch (start us, length us, event | category | flops | bytes accessed | tf_op | source)
XLA Modules:
  0.0 183.9 jit_solution(17452605406334857137)
XLA Ops:
  7.2 0.0 all-gather.10.cloned.1.call-start
  7.2 0.6 pad_add_fusion.refs_0_
  7.8 2.1 %shard_map.92 = (bf16[768,128]{1,0:T(8,128)(2,1)}, bf16[2,640,128]{2,1,0:T(8,128)(2,1)}) custom-call(s32[4]{0:T(128)} %pad_add_fusion.refs_0_, bf16[640,128]{1,0:T(8,128)(2,1)} %refs_3_.4, bf16[1024,128]{1,0:T(8,128)(2,1)} %refs_2_.1, f32[640,128]{1,0:T(8,128)} %refs_3_.5, f32[640,128]{1,0:T(8,128)} %refs_4_.5), custom_call_target="tpu_custom_call" | custom-call | bytes 1500000 | tf_op jit(solution)/shard_map/pallas_call | solution.py:77
  9.9 0.0 all-gather.10.cloned.1.call-update
  10.0 0.0 all-gather.8.cloned.1.call-start
  10.0 14.8 %collective-permute-start = (bf16[768,128]{1,0:T(8,128)(2,1)}, bf16[768,128]{1,0:T(8,128)(2,1)S(1)}, u32[]{:S(2)}, u32[]{:S(2)}) collective-permute-start(bf16[768,128]{1,0:T(8,128)(2,1)} %get-tuple-element.19), channel_id=1, source_target_pairs={{0,4},{4,0},{1,5},{5,1},{2,6},{6,2},{3,7},{7,3},{8,12},{12,8},{9,1... | collective-permute-start | bytes 589832 | tf_op jit(solution)/shard_map/ppermute | solution.py:47
  24.8 14.0 %all-gather = bf16[3072,128]{1,0:T(8,128)(2,1)S(1)} all-gather(bf16[768,128]{1,0:T(8,128)(2,1)} %get-tuple-element.19), channel_id=2, replica_groups=mesh['layer'=8,'x'=4,'core'=2,'zh'=2,'y'=4] {'y'}, dimensions={0}, use_global_device_ids=true | all-gather | bytes 983040 | tf_op jit(solution)/shard_map/all_gather | solution.py:244
  38.9 1.6 collective-permute-done
  40.5 14.2 %all-gather.1 = bf16[3072,128]{1,0:T(8,128)(2,1)S(1)} all-gather(bf16[768,128]{1,0:T(8,128)(2,1)S(1)} %collective-permute-done), channel_id=3, replica_groups=mesh['layer'=8,'x'=4,'core'=2,'zh'=2,'y'=4] {'y'}, dimensions={0}, use_global_device_ids=true | all-gather | bytes 983040 | tf_op jit(solution)/shard_map/all_gather | solution.py:247
  54.7 0.0 copy-done.9
  54.7 3.0 %shard_map.93 = (bf16[384,1024]{1,0:T(8,128)(2,1)S(1)}, bf16[384,1024]{1,0:T(8,128)(2,1)S(1)}, bf16[128,1024]{1,0:T(8,128)(2,1)}) custom-call(s32[4]{0:T(128)S(1)} %copy-done.10, bf16[4,768,128]{2,1,0:T(8,128)(2,1)S(1)} %bitcast.12, bf16[4,768,128]{2,1,0:T(8,128)(2,1)S(1)} %bitcast.15, bf16[640,128]{1,0:T(8,128)(2,1)S(1)} %copy-done.9, ...), custom_call_target="tpu_custom_call" | custom-call | flops 1000000000 | bytes 5000000 | tf_op jit(solution)/shard_map/pallas_call | solution.py:77
  57.8 0.9 copy-done.12
  58.6 0.0 all-gather.8.cloned.1.call-update
  58.7 1.9 %collective-permute-start.1 = (bf16[384,1024]{1,0:T(8,128)(2,1)}, bf16[384,1024]{1,0:T(8,128)(2,1)S(1)}, u32[]{:S(2)}, u32[]{:S(2)}) collective-permute-start(bf16[384,1024]{1,0:T(8,128)(2,1)} %copy-done.12), channel_id=1, source_target_pairs={{0,8},{8,0},{1,9},{9,1},{2,10},{10,2},{3,11},{11,3},{4,12},{12,4},... | collective-permute-start | bytes 2359304 | tf_op jit(solution)/shard_map/ppermute | solution.py:43
  60.6 0.0 all-gather.10.cloned.1.call-done
  60.6 0.7 constant_dynamic-slice_fusion
  61.4 1.7 collective-permute-done.1.refs_2_
  63.1 1.6 shard_map.94
  64.7 4.5 %all-to-all-start = ((bf16[4,384,256]{2,1,0:T(8,128)(2,1)}), bf16[4,384,256]{2,1,0:T(8,128)(2,1)S(1)}, u32[]{:S(2)}, u32[]{:S(2)}) async-start(bf16[4,384,256]{2,1,0:T(8,128)(2,1)} %shard_map.94), calls=%async_computation | async-start | bytes 1572864 | tf_op jit(solution)/shard_map/all_to_all | solution.py:272
  69.2 0.7 collective-permute-start.2
  69.8 4.8 %collective-permute-start.3 = (bf16[640,128]{1,0:T(8,128)(2,1)S(1)}, bf16[640,128]{1,0:T(8,128)(2,1)S(1)}, u32[]{:S(2)}, u32[]{:S(2)}) collective-permute-start(bf16[640,128]{1,0:T(8,128)(2,1)S(1)} %get-tuple-element.35), channel_id=1, source_target_pairs={{0,8},{1,24},{2,40},{3,56},{8,9},{9,25},{10,41},{11,57},{16,10},{1... | collective-permute-start | bytes 491528 | tf_op jit(solution)/shard_map/ppermute | solution.py:288
  74.6 0.0 collective-permute-done.2.refs_1_
  74.6 1.0 collective-permute-done.3.refs_2_
  75.6 1.2 shard_map.95
  76.9 6.3 %all-to-all-done.refs_1_ = bf16[4,384,256]{2,1,0:T(8,128)(2,1)S(1)} async-done(((bf16[4,384,256]{2,1,0:T(8,128)(2,1)}), bf16[4,384,256]{2,1,0:T(8,128)(2,1)S(1)}, u32[]{:S(2)}, u32[]{:S(2)}) %all-to-all-start) | async-done | bytes 786464 | tf_op jit(solution)/shard_map/all_to_all | solution.py:272
  83.2 1.5 shard_map.96
  84.6 15.4 %all-to-all-start.1 = ((bf16[4,320,256]{2,1,0:T(8,128)(2,1)}), bf16[4,320,256]{2,1,0:T(8,128)(2,1)S(1)}, u32[]{:S(2)}, u32[]{:S(2)}) async-start(bf16[4,320,256]{2,1,0:T(8,128)(2,1)} %get-tuple-element.24), calls=%async_computation.1 | async-start | bytes 1310720 | tf_op jit(solution)/shard_map/all_to_all | solution.py:300
  100.0 0.7 all-gather.12.cloned.1.call-update
  100.7 1.4 constant_dynamic-slice_fusion.1.refs_2_
  102.2 0.0 all-gather.8.cloned.1.call-done.refs_3_
  102.2 6.6 %all-to-all-done.1.refs_1_ = bf16[4,320,256]{2,1,0:T(8,128)(2,1)S(1)} async-done(((bf16[4,320,256]{2,1,0:T(8,128)(2,1)}), bf16[4,320,256]{2,1,0:T(8,128)(2,1)S(1)}, u32[]{:S(2)}, u32[]{:S(2)}) %all-to-all-start.1) | async-done | bytes 655392 | tf_op jit(solution)/shard_map/all_to_all | solution.py:300
  108.8 1.6 copy-done.11
  110.4 2.8 %shard_map.97 = (bf16[320,1152]{1,0:T(8,128)(2,1)S(1)}, f32[320,128]{1,0:T(8,128)S(1)}) custom-call(s32[4]{0:T(128)S(1)} %copy-done.10, bf16[4,320,256]{2,1,0:T(8,128)(2,1)S(1)} %all-to-all-done.1.refs_1_, bf16[8,2,320,128]{3,2,1,0:T(8,128)(2,1)S(1)} %constant_dynamic-slice_fusion.1.refs_2_, bf16[1024,1024]{1,0:T(8,128)(2,1)S(1)} %copy-done.11), custom_call_target="tpu_custom_call" | custom-call | flops 1400000000 | bytes 6000000 | tf_op jit(solution)/shard_map/pallas_call | solution.py:77
  113.2 0.0 copy-start.7
  113.2 9.1 %collective-permute-start.4 = (bf16[320,1152]{1,0:T(8,128)(2,1)S(1)}, bf16[320,1152]{1,0:T(8,128)(2,1)S(1)}, u32[]{:S(2)}, u32[]{:S(2)}) collective-permute-start(bf16[320,1152]{1,0:T(8,128)(2,1)S(1)} %get-tuple-element.27.refs_2_), channel_id=1, source_target_pairs={{0,8},{8,0},{1,9},{9,1},{2,10},{10,2},{3,11},{11,3},{4,12},{12,4},... | collective-permute-start | bytes 2211848 | tf_op jit(solution)/shard_map/ppermute | solution.py:43
  122.4 1.8 collective-permute-done.4.refs_3_.refs_2_
  124.2 1.8 shard_map.98
  126.0 23.5 %all_to_all.15.refs_5_.refs_1_ = bf16[4,1280,128]{2,1,0:T(8,128)(2,1)S(1)} all-to-all(bf16[4,1280,128]{2,1,0:T(8,128)(2,1)S(1)} %shard_map.98), channel_id=1, replica_groups=mesh['layer'=8,'x'=4,'core'=2,'zh'=2,'y'=4] {'y'}, dimensions={0} | all-to-all | bytes 2621440 | tf_op jit(solution)/shard_map/all_to_all | solution.py:325
  149.5 0.6 shard_map.100.refs_4_
  150.2 11.7 %collective-permute-start.5 = (bf16[640,128]{1,0:T(8,128)(2,1)S(1)}, bf16[640,128]{1,0:T(8,128)(2,1)S(1)}, u32[]{:S(2)}, u32[]{:S(2)}) collective-permute-start(bf16[640,128]{1,0:T(8,128)(2,1)S(1)} %shard_map.100.refs_4_), channel_id=1, source_target_pairs={{0,4},{4,0},{1,5},{5,1},{2,6},{6,2},{3,7},{7,3},{8,12},{12,8},{9,1... | collective-permute-start | bytes 491528 | tf_op jit(solution)/shard_map/ppermute | solution.py:47
  161.9 0.0 all-gather.12.cloned.1.call-done
  161.9 1.3 copy-done.2
  163.2 3.1 %shard_map.102 = f32[640,640]{1,0:T(8,128)} custom-call(s32[4]{0:T(128)S(1)} %copy-done.10, bf16[4,768,128]{2,1,0:T(8,128)(2,1)S(1)} %bitcast.14, bf16[4,768,128]{2,1,0:T(8,128)(2,1)S(1)} %bitcast.17, bf16[8,640,128]{2,1,0:T(8,128)(2,1)S(1)} %bitcast.18, bf16[640,128]{1,0:T(8,128)(2,1)S(1)} %shard_map.100.refs_4_), custom_call_target="tpu_custom_call" | custom-call | flops 10000 | bytes 10000 | tf_op jit(solution)/shard_map/pallas_call | solution.py:77
  166.4 0.0 copy-done.1
  166.4 0.0 copy-done.4
  166.4 1.5 shard_map.99
  167.9 8.3 %collective-permute-done.5.refs_2_ = bf16[640,128]{1,0:T(8,128)(2,1)S(1)} collective-permute-done((bf16[640,128]{1,0:T(8,128)(2,1)S(1)}, bf16[640,128]{1,0:T(8,128)(2,1)S(1)}, u32[]{:S(2)}, u32[]{:S(2)}) %collective-permute-start.5) | collective-permute-done | bytes 163872 | tf_op jit(solution)/shard_map/ppermute | solution.py:47
  176.2 1.2 shard_map.101
  (21 shorter events, 0.1 us)
Async XLA Ops:
  7.2 53.5 %all-gather.10.cloned.1.call-start = ((), (), s32[]{:S(2)}) async-start(), calls=%async_computation.4 | async-start | bytes 2949120 | tf_op jit(solution)/shard_map/all_gather | solution.py:246
  7.8 46.9 %copy-start.5 = (bf16[640,640]{1,0:T(8,128)(2,1)S(1)}, bf16[640,640]{1,0:T(8,128)(2,1)}, u32[]{:S(2)}) copy-start(bf16[640,640]{1,0:T(8,128)(2,1)} %refs_1_.3) | copy-start | bytes 2457604
  7.8 46.9 %copy-start.9 = (bf16[640,128]{1,0:T(8,128)(2,1)S(1)}, bf16[640,128]{1,0:T(8,128)(2,1)}, u32[]{:S(2)}) copy-start(bf16[640,128]{1,0:T(8,128)(2,1)} %refs_3_.4) | copy-start | bytes 491524
  7.8 46.9 %copy-start.10 = (s32[4]{0:T(128)S(1)}, s32[4]{0:T(128)}, u32[]{:S(2)}) copy-start(s32[4]{0:T(128)} %pad_add_fusion.refs_0_) | copy-start | bytes 52
  10.0 92.2 %all-gather.8.cloned.1.call-start = ((), (), s32[]{:S(2)}) async-start(), calls=%async_computation.3 | async-start | bytes 2359296 | tf_op jit(solution)/shard_map/all_gather | solution.py:261
  10.0 30.5 %collective-permute-start = (bf16[768,128]{1,0:T(8,128)(2,1)}, bf16[768,128]{1,0:T(8,128)(2,1)S(1)}, u32[]{:S(2)}, u32[]{:S(2)}) collective-permute-start(bf16[768,128]{1,0:T(8,128)(2,1)} %get-tuple-element.19), channel_id=1, source_target_pairs={{0,4},{4,0},{1,5},{5,1},{2,6},{6,2},{3,7},{7,3},{8,12},{12,8},{9,1... | collective-permute-start | bytes 589832 | tf_op jit(solution)/shard_map/ppermute | solution.py:47
  57.8 0.9 copy-start.12
  58.7 4.4 %collective-permute-start.1 = (bf16[384,1024]{1,0:T(8,128)(2,1)}, bf16[384,1024]{1,0:T(8,128)(2,1)S(1)}, u32[]{:S(2)}, u32[]{:S(2)}) collective-permute-start(bf16[384,1024]{1,0:T(8,128)(2,1)} %copy-done.12), channel_id=1, source_target_pairs={{0,8},{8,0},{1,9},{9,1},{2,10},{10,2},{3,11},{11,3},{4,12},{12,4},... | collective-permute-start | bytes 2359304 | tf_op jit(solution)/shard_map/ppermute | solution.py:43
  64.7 18.5 %all-to-all-start = ((bf16[4,384,256]{2,1,0:T(8,128)(2,1)}), bf16[4,384,256]{2,1,0:T(8,128)(2,1)S(1)}, u32[]{:S(2)}, u32[]{:S(2)}) async-start(bf16[4,384,256]{2,1,0:T(8,128)(2,1)} %shard_map.94), calls=%async_computation | async-start | bytes 1572864 | tf_op jit(solution)/shard_map/all_to_all | solution.py:272
  69.2 5.5 %collective-permute-start.2 = (bf16[640,128]{1,0:T(8,128)(2,1)S(1)}, bf16[640,128]{1,0:T(8,128)(2,1)S(1)}, u32[]{:S(2)}, u32[]{:S(2)}) collective-permute-start(bf16[640,128]{1,0:T(8,128)(2,1)S(1)} %get-tuple-element.36), channel_id=1, source_target_pairs={{0,0},{1,16},{2,32},{3,48},{8,1},{9,17},{10,33},{11,49},{16,2},{17... | collective-permute-start | bytes 491528 | tf_op jit(solution)/shard_map/ppermute | solution.py:288
  69.8 5.8 %collective-permute-start.3 = (bf16[640,128]{1,0:T(8,128)(2,1)S(1)}, bf16[640,128]{1,0:T(8,128)(2,1)S(1)}, u32[]{:S(2)}, u32[]{:S(2)}) collective-permute-start(bf16[640,128]{1,0:T(8,128)(2,1)S(1)} %get-tuple-element.35), channel_id=1, source_target_pairs={{0,8},{1,24},{2,40},{3,56},{8,9},{9,25},{10,41},{11,57},{16,10},{1... | collective-permute-start | bytes 491528 | tf_op jit(solution)/shard_map/ppermute | solution.py:288
  84.6 24.1 %all-to-all-start.1 = ((bf16[4,320,256]{2,1,0:T(8,128)(2,1)}), bf16[4,320,256]{2,1,0:T(8,128)(2,1)S(1)}, u32[]{:S(2)}, u32[]{:S(2)}) async-start(bf16[4,320,256]{2,1,0:T(8,128)(2,1)} %get-tuple-element.24), calls=%async_computation.1 | async-start | bytes 1310720 | tf_op jit(solution)/shard_map/all_to_all | solution.py:300
  100.0 61.9 %all-gather.12.cloned.1.call-start = ((), (), s32[]{:S(2)}) async-start(), calls=%async_computation.5 | async-start | bytes 1474560 | tf_op jit(solution)/shard_map/all_gather | solution.py:331
  108.8 1.6 copy-start.11
  110.4 13.8 %copy-start.6 = (bf16[640,640]{1,0:T(8,128)(2,1)S(1)}, bf16[640,640]{1,0:T(8,128)(2,1)}, u32[]{:S(2)}) copy-start(bf16[640,640]{1,0:T(8,128)(2,1)} %refs_1_.3) | copy-start | bytes 2457604
  113.2 12.8 %copy-start.7 = (f32[320,128]{1,0:T(8,128)}, f32[320,128]{1,0:T(8,128)S(1)}, u32[]{:S(2)}) copy-start(f32[320,128]{1,0:T(8,128)S(1)} %get-tuple-element.26.refs_1_) | copy-start | bytes 491524
  113.2 11.0 %collective-permute-start.4 = (bf16[320,1152]{1,0:T(8,128)(2,1)S(1)}, bf16[320,1152]{1,0:T(8,128)(2,1)S(1)}, u32[]{:S(2)}, u32[]{:S(2)}) collective-permute-start(bf16[320,1152]{1,0:T(8,128)(2,1)S(1)} %get-tuple-element.27.refs_2_), channel_id=1, source_target_pairs={{0,8},{8,0},{1,9},{9,1},{2,10},{10,2},{3,11},{11,3},{4,12},{12,4},... | collective-permute-start | bytes 2211848 | tf_op jit(solution)/shard_map/ppermute | solution.py:43
  124.2 1.8 %copy-start = (bf16[320,1152]{1,0:T(8,128)(2,1)}, bf16[320,1152]{1,0:T(8,128)(2,1)S(1)}, u32[]{:S(2)}) copy-start(bf16[320,1152]{1,0:T(8,128)(2,1)S(1)} %collective-permute-done.4.refs_3_.refs_2_) | copy-start | bytes 2211844
  150.2 26.0 %collective-permute-start.5 = (bf16[640,128]{1,0:T(8,128)(2,1)S(1)}, bf16[640,128]{1,0:T(8,128)(2,1)S(1)}, u32[]{:S(2)}, u32[]{:S(2)}) collective-permute-start(bf16[640,128]{1,0:T(8,128)(2,1)S(1)} %shard_map.100.refs_4_), channel_id=1, source_target_pairs={{0,4},{4,0},{1,5},{5,1},{2,6},{6,2},{3,7},{7,3},{8,12},{12,8},{9,1... | collective-permute-start | bytes 491528 | tf_op jit(solution)/shard_map/ppermute | solution.py:47
  161.9 1.3 copy-start.2
  163.2 3.1 %copy-start.1 = (bf16[320,1152]{1,0:T(8,128)(2,1)S(1)}, bf16[320,1152]{1,0:T(8,128)(2,1)}, u32[]{:S(2)}) copy-start(bf16[320,1152]{1,0:T(8,128)(2,1)} %copy-done) | copy-start | bytes 2211844
  163.2 3.1 %copy-start.3 = (f32[640,128]{1,0:T(8,128)S(1)}, f32[640,128]{1,0:T(8,128)}, u32[]{:S(2)}) copy-start(f32[640,128]{1,0:T(8,128)} %refs_3_.5) | copy-start | bytes 983044
  163.2 3.1 %copy-start.4 = (f32[640,128]{1,0:T(8,128)S(1)}, f32[640,128]{1,0:T(8,128)}, u32[]{:S(2)}) copy-start(f32[640,128]{1,0:T(8,128)} %refs_4_.5) | copy-start | bytes 983044
  163.2 3.1 %copy-start.8 = (f32[320,128]{1,0:T(8,128)S(1)}, f32[320,128]{1,0:T(8,128)}, u32[]{:S(2)}) copy-start(f32[320,128]{1,0:T(8,128)} %copy-done.7) | copy-start | bytes 491524
Sparse Core Ops, SparseCore 0:
  10.7 37.8 all-gather.9
  58.8 38.2 all-gather.7
  103.5 40.8 all-gather.11

commit v6 on v5

--- a/solution.py
+++ b/solution.py
@@ -44,7 +44,14 @@
 
 
 def other_half(value):
-    return lax.ppermute(value, "zh", [(0, 1), (1, 0)])
+    axes = ("core", "zh", "y")
+    return lax.ppermute(
+        value, axes, pairs(axes, lambda c, z, y: (c, 1 - z, (y + 2 * c) % 4))
+    )
+
+
+def shifted(k, core):
+    return lax.rem(k + 2 * core, 4)
 
 
 def spread(value, axis):
@@ -57,7 +64,8 @@
     def target(x, c, z, y):
         if x // 2 != z:
             return None
-        return (y, core, z, 2 * (x % 2) + c)
+        there = 2 * (x % 2) + c
+        return ((y - there) % 4, core, z, there)
 
     return pairs(("x", "core", "zh", "y"), target)
 
@@ -98,10 +106,11 @@
 def left_kernel(where, near, far, grad, left, keep, send, slabs, panel):
     core, z = where[1], where[2]
     for k in range(4):
+        place = shifted(k, core)
         slabs[:, 128 * k : 128 * k + 128] = near[k, 640:]
-        slabs[:, 512 + 128 * k : 640 + 128 * k] = far[k, 640:]
-        panel[:, 128 * k : 128 * k + 128] = near[k, :640, :]
-        panel[:, 512 + 128 * k : 640 + 128 * k] = far[k, :640, :]
+        slabs[:, 512 + 128 * k : 640 + 128 * k] = far[place, 640:]
+        panel[:, 128 * k : 128 * k + 128] = near[k, :640]
+        panel[:, 512 + 128 * k : 640 + 128 * k] = far[place, :640]
 
     product = dot(left[...], panel[...], 0, 0).astype(bf16)
     gram = (dot(grad[...], panel[...], 0, 0) * (1.0 / M)).astype(bf16)
@@ -175,7 +184,13 @@
     product = dot(left[...], joined[...], 1, 0).astype(bf16)
     for k in range(4):
         out[k, :640] = product[:, 128 * k : 128 * k + 128]
-        out[k, 640:] = product[:, 512 + 128 * k : 640 + 128 * k]
+    for c in range(2):
+
+        @pl.when(core == c)
+        def _():
+            for k in range(4):
+                at = 512 + 128 * ((k + 2 * c) % 4)
+                out[k, 640:] = product[:, at : at + 128]
 
 
 def fold(parts, rows):
@@ -216,8 +231,8 @@
 
 def gram_kernel(where, near, far, paired, out, panel, other):
     for k in range(4):
-        panel[:, 128 * k : 128 * k + 128] = near[k, :640, :]
-        panel[:, 512 + 128 * k : 640 + 128 * k] = far[k, :640, :]
+        panel[:, 128 * k : 128 * k + 128] = near[k, :640]
+        panel[:, 512 + 128 * k : 640 + 128 * k] = far[shifted(k, where[1]), :640]
     for k in range(8):
         other[:, 128 * k : 128 * k + 128] = paired[k]
     out[...] = dot(panel[...], other[...], 1, 1) * (1.0 / C)
@@ -272,13 +287,14 @@
     summed = lax.all_to_all(summed, "x", 0, 0, tiled=True)
 
     axes = ("x", "core", "zh", "y")
-    at = 2 * (y % 2)
+    to_x = (y + 8 - 2 * (x % 2) - core) % 4
+    at = 2 * (to_x % 2)
 
     def piece(t):
         return jnp.where(
-            y < 2,
+            to_x < 2,
             lax.dynamic_index_in_dim(near_all, at + t, 0, False)[:640],
-            lax.dynamic_index_in_dim(far_all, at + t, 0, False)[:640],
+            lax.dynamic_index_in_dim(far_all, shifted(at + t, core), 0, False)[:640],
         )
 
     pair, paired_mark = call(

time: 185 us -> 181 us (0.978)
  waiting for transfers between devices: 28.2 us -> 24.4 us
  blocking collectives: 51.7 us -> 54.7 us
  starting transfers between devices: 62.9 us -> 60.3 us
    all_to_all x1, starting transfers between devices: 15.4 us -> 10.2 us  [body(): half = lax.all_to_all(rows, 'x', 0, 0, tiled=True)]
    ppermute x2, starting transfers between devices: 26.5 us -> 30.8 us  [other_half(): lax.ppermute(value, axes, pairs(axes, lambda c, z, y: (c, 1 - z, (y + 2 *...]
    ppermute x2, starting transfers between devices: 11.1 us -> 8.32 us  [other_core(): return lax.ppermute(value, 'core', [(0, 1), (1, 0)])]
    all_to_all x1, waiting for transfers between devices: 6.32 us -> 3.71 us  [body(): summed = lax.all_to_all(summed, 'x', 0, 0, tiled=True)]
  transfers between devices with their start and end apart: 11 -> 11, of which waited for: 7 -> 7; matrix products, arithmetic and copies ran while one was open for 1% -> 1% of each run, Pallas kernels for 9% -> 10%
where the time goes in v6:
time: 181 us
  starting transfers between devices  60.3 us (33%)
  blocking collectives  54.7 us (30%)
  waiting for transfers between devices  24.4 us (13%)
  Pallas kernels  20.6 us (11%)
  between operations  13.9 us (8%)
  local copies, waits for them, and re-layouts  6.01 us (3%)
    ppermute x2, starting transfers between devices, other_half(): lax.ppermute(value, axes, pairs(axes, lambda c, z, y: (c, 1 - z, (y + 2 *...  30.8 us
    all_to_all x1, blocking collectives, body(): parts = lax.all_to_all(parts, 'y', 0, 0, tiled=True)  23.2 us
    pallas_call x11, Pallas kernels, call(): pl.pallas_call(inner, out_shape=outs, in_specs=[pl.BlockSpec(memory_space...  20.6 us
    all_gather x1, blocking collectives, body(): far_all = lax.all_gather(far, 'y', axis=0)  15.9 us
    all_gather x1, blocking collectives, body(): near_all = lax.all_gather(mine, 'y', axis=0)  15.6 us
    all_to_all x1, starting transfers between devices, body(): half = lax.all_to_all(rows, 'x', 0, 0, tiled=True)  10.2 us
    ppermute x2, waiting for transfers between devices, other_half(): lax.ppermute(value, axes, pairs(axes, lambda c, z, y: (c, 1 - z, (y + 2 *...  8.77 us
    ppermute x2, starting transfers between devices, other_core(): return lax.ppermute(value, 'core', [(0, 1), (1, 0)])  8.32 us
  transfers between devices with their start and end apart: 11, of which 7 were waited for; matrix products, arithmetic and copies ran while one was open for 1% of the time, Pallas kernels for 10%

profile of v6, /device:TPU:32, one launch (start us, length us, event | category | flops | bytes accessed | tf_op | source)
XLA Modules:
  0.0 180.6 jit_solution(7288426832102456046)
XLA Ops:
  7.2 0.0 all-gather.10.cloned.1.call-start
  7.2 0.6 pad_add_fusion.refs_0_
  7.8 2.1 %shard_map.92 = (bf16[768,128]{1,0:T(8,128)(2,1)}, bf16[2,640,128]{2,1,0:T(8,128)(2,1)}) custom-call(s32[4]{0:T(128)} %pad_add_fusion.refs_0_, bf16[640,128]{1,0:T(8,128)(2,1)} %refs_3_.4, bf16[1024,128]{1,0:T(8,128)(2,1)} %refs_2_.1, f32[640,128]{1,0:T(8,128)} %refs_3_.5, f32[640,128]{1,0:T(8,128)} %refs_4_.5), custom_call_target="tpu_custom_call" | custom-call | bytes 1500000 | tf_op jit(solution)/shard_map/pallas_call | solution.py:85
  9.9 0.0 all-gather.10.cloned.1.call-update
  10.0 0.0 all-gather.8.cloned.1.call-start
  10.0 14.8 %collective-permute-start = (bf16[768,128]{1,0:T(8,128)(2,1)}, bf16[768,128]{1,0:T(8,128)(2,1)S(1)}, u32[]{:S(2)}, u32[]{:S(2)}) collective-permute-start(bf16[768,128]{1,0:T(8,128)(2,1)} %get-tuple-element.19), channel_id=1, source_target_pairs={{0,4},{1,5},{2,6},{3,7},{4,0},{5,1},{6,2},{7,3},{8,14},{9,15},{10,... | collective-permute-start | bytes 589832 | tf_op jit(solution)/shard_map/ppermute | solution.py:48
  24.8 15.6 %all-gather = bf16[3072,128]{1,0:T(8,128)(2,1)S(1)} all-gather(bf16[768,128]{1,0:T(8,128)(2,1)} %get-tuple-element.19), channel_id=2, replica_groups=mesh['layer'=8,'x'=4,'core'=2,'zh'=2,'y'=4] {'y'}, dimensions={0}, use_global_device_ids=true | all-gather | bytes 983040 | tf_op jit(solution)/shard_map/all_gather | solution.py:259
  40.5 0.2 collective-permute-done
  40.7 15.9 %all-gather.1 = bf16[3072,128]{1,0:T(8,128)(2,1)S(1)} all-gather(bf16[768,128]{1,0:T(8,128)(2,1)S(1)} %collective-permute-done), channel_id=3, replica_groups=mesh['layer'=8,'x'=4,'core'=2,'zh'=2,'y'=4] {'y'}, dimensions={0}, use_global_device_ids=true | all-gather | bytes 983040 | tf_op jit(solution)/shard_map/all_gather | solution.py:262
  56.6 0.0 copy-done.5
  56.6 0.0 copy-done.9
  56.6 3.0 %shard_map.93 = (bf16[384,1024]{1,0:T(8,128)(2,1)S(1)}, bf16[384,1024]{1,0:T(8,128)(2,1)S(1)}, bf16[128,1024]{1,0:T(8,128)(2,1)}) custom-call(s32[4]{0:T(128)S(1)} %copy-done.10, bf16[4,768,128]{2,1,0:T(8,128)(2,1)S(1)} %bitcast.12, bf16[4,768,128]{2,1,0:T(8,128)(2,1)S(1)} %bitcast.15, bf16[640,128]{1,0:T(8,128)(2,1)S(1)} %copy-done.9, ...), custom_call_target="tpu_custom_call" | custom-call | flops 1000000000 | bytes 5000000 | tf_op jit(solution)/shard_map/pallas_call | solution.py:85
  59.6 0.9 copy-done.12
  60.5 0.0 all-gather.8.cloned.1.call-update
  60.5 1.9 %collective-permute-start.1 = (bf16[384,1024]{1,0:T(8,128)(2,1)}, bf16[384,1024]{1,0:T(8,128)(2,1)S(1)}, u32[]{:S(2)}, u32[]{:S(2)}) collective-permute-start(bf16[384,1024]{1,0:T(8,128)(2,1)} %copy-done.12), channel_id=1, source_target_pairs={{0,8},{8,0},{1,9},{9,1},{2,10},{10,2},{3,11},{11,3},{4,12},{12,4},... | collective-permute-start | bytes 2359304 | tf_op jit(solution)/shard_map/ppermute | solution.py:43
  62.4 0.0 all-gather.10.cloned.1.call-done
  62.5 0.7 constant_dynamic-slice_fusion
  63.2 1.7 collective-permute-done.1.refs_2_
  64.9 1.6 shard_map.94
  66.5 4.3 %all-to-all-start = ((bf16[4,384,256]{2,1,0:T(8,128)(2,1)}), bf16[4,384,256]{2,1,0:T(8,128)(2,1)S(1)}, u32[]{:S(2)}, u32[]{:S(2)}) async-start(bf16[4,384,256]{2,1,0:T(8,128)(2,1)} %shard_map.94), calls=%async_computation | async-start | bytes 1572864 | tf_op jit(solution)/shard_map/all_to_all | solution.py:287
  70.8 0.7 collective-permute-start.2
  71.5 5.9 %collective-permute-start.3 = (bf16[640,128]{1,0:T(8,128)(2,1)S(1)}, bf16[640,128]{1,0:T(8,128)(2,1)S(1)}, u32[]{:S(2)}, u32[]{:S(2)}) collective-permute-start(bf16[640,128]{1,0:T(8,128)(2,1)S(1)} %get-tuple-element.35), channel_id=1, source_target_pairs={{0,8},{1,24},{2,40},{3,56},{8,57},{9,9},{10,25},{11,41},{16,42},{1... | collective-permute-start | bytes 491528 | tf_op jit(solution)/shard_map/ppermute | solution.py:304
  77.4 0.0 collective-permute-done.2.refs_1_
  77.4 1.0 collective-permute-done.3.refs_2_
  78.4 1.2 shard_map.95
  79.7 3.7 %all-to-all-done.refs_1_ = bf16[4,384,256]{2,1,0:T(8,128)(2,1)S(1)} async-done(((bf16[4,384,256]{2,1,0:T(8,128)(2,1)}), bf16[4,384,256]{2,1,0:T(8,128)(2,1)S(1)}, u32[]{:S(2)}, u32[]{:S(2)}) %all-to-all-start) | async-done | bytes 786464 | tf_op jit(solution)/shard_map/all_to_all | solution.py:287
  83.4 1.5 shard_map.96
  84.8 10.2 %all-to-all-start.1 = ((bf16[4,320,256]{2,1,0:T(8,128)(2,1)}), bf16[4,320,256]{2,1,0:T(8,128)(2,1)S(1)}, u32[]{:S(2)}, u32[]{:S(2)}) async-start(bf16[4,320,256]{2,1,0:T(8,128)(2,1)} %get-tuple-element.24), calls=%async_computation.1 | async-start | bytes 1310720 | tf_op jit(solution)/shard_map/all_to_all | solution.py:316
  95.1 0.7 all-gather.12.cloned.1.call-update
  95.8 1.4 constant_dynamic-slice_fusion.1.refs_2_
  97.3 0.0 all-gather.8.cloned.1.call-done.refs_3_
  97.3 6.6 %all-to-all-done.1.refs_1_ = bf16[4,320,256]{2,1,0:T(8,128)(2,1)S(1)} async-done(((bf16[4,320,256]{2,1,0:T(8,128)(2,1)}), bf16[4,320,256]{2,1,0:T(8,128)(2,1)S(1)}, u32[]{:S(2)}, u32[]{:S(2)}) %all-to-all-start.1) | async-done | bytes 655392 | tf_op jit(solution)/shard_map/all_to_all | solution.py:316
  103.9 1.6 copy-done.11
  105.5 2.8 %shard_map.97 = (bf16[320,1152]{1,0:T(8,128)(2,1)S(1)}, f32[320,128]{1,0:T(8,128)S(1)}) custom-call(s32[4]{0:T(128)S(1)} %copy-done.10, bf16[4,320,256]{2,1,0:T(8,128)(2,1)S(1)} %all-to-all-done.1.refs_1_, bf16[8,2,320,128]{3,2,1,0:T(8,128)(2,1)S(1)} %constant_dynamic-slice_fusion.1.refs_2_, bf16[1024,1024]{1,0:T(8,128)(2,1)S(1)} %copy-done.11), custom_call_target="tpu_custom_call" | custom-call | flops 1400000000 | bytes 6000000 | tf_op jit(solution)/shard_map/pallas_call | solution.py:85
  108.3 0.0 copy-start.7
  108.3 6.4 %collective-permute-start.4 = (bf16[320,1152]{1,0:T(8,128)(2,1)S(1)}, bf16[320,1152]{1,0:T(8,128)(2,1)S(1)}, u32[]{:S(2)}, u32[]{:S(2)}) collective-permute-start(bf16[320,1152]{1,0:T(8,128)(2,1)S(1)} %get-tuple-element.27.refs_2_), channel_id=1, source_target_pairs={{0,8},{8,0},{1,9},{9,1},{2,10},{10,2},{3,11},{11,3},{4,12},{12,4},... | collective-permute-start | bytes 2211848 | tf_op jit(solution)/shard_map/ppermute | solution.py:43
  114.7 1.8 %collective-permute-done.4.refs_3_.refs_2_ = bf16[320,1152]{1,0:T(8,128)(2,1)S(1)} collective-permute-done((bf16[320,1152]{1,0:T(8,128)(2,1)S(1)}, bf16[320,1152]{1,0:T(8,128)(2,1)S(1)}, u32[]{:S(2)}, u32[]{:S(2)}) %collective-permute-start.4) | collective-permute-done | bytes 737312 | tf_op jit(solution)/shard_map/ppermute | solution.py:43
  116.5 1.9 %shard_map.98 = bf16[4,1280,128]{2,1,0:T(8,128)(2,1)S(1)} custom-call(s32[4]{0:T(128)S(1)} %copy-done.10, bf16[640,640]{1,0:T(8,128)(2,1)S(1)} %copy-done.6, bf16[320,1152]{1,0:T(8,128)(2,1)S(1)} %get-tuple-element.27.refs_2_, bf16[320,1152]{1,0:T(8,128)(2,1)S(1)} %collective-permute-done.4.refs_3_.refs_2_), custom_call_target="tpu_custom_call" | custom-call | flops 840000000 | bytes 4000000 | tf_op jit(solution)/shard_map/pallas_call | solution.py:85
  118.5 23.2 %all_to_all.15.refs_5_.refs_1_ = bf16[4,1280,128]{2,1,0:T(8,128)(2,1)S(1)} all-to-all(bf16[4,1280,128]{2,1,0:T(8,128)(2,1)S(1)} %shard_map.98), channel_id=1, replica_groups=mesh['layer'=8,'x'=4,'core'=2,'zh'=2,'y'=4] {'y'}, dimensions={0} | all-to-all | bytes 2621440 | tf_op jit(solution)/shard_map/all_to_all | solution.py:341
  141.7 0.6 shard_map.100.refs_4_
  142.3 16.0 %collective-permute-start.5 = (bf16[640,128]{1,0:T(8,128)(2,1)S(1)}, bf16[640,128]{1,0:T(8,128)(2,1)S(1)}, u32[]{:S(2)}, u32[]{:S(2)}) collective-permute-start(bf16[640,128]{1,0:T(8,128)(2,1)S(1)} %shard_map.100.refs_4_), channel_id=1, source_target_pairs={{0,4},{1,5},{2,6},{3,7},{4,0},{5,1},{6,2},{7,3},{8,14},{9,15},{10,... | collective-permute-start | bytes 491528 | tf_op jit(solution)/shard_map/ppermute | solution.py:48
  158.3 0.0 all-gather.12.cloned.1.call-done
  158.3 1.3 copy-done.2
  159.7 3.1 %shard_map.102 = f32[640,640]{1,0:T(8,128)} custom-call(s32[4]{0:T(128)S(1)} %copy-done.10, bf16[4,768,128]{2,1,0:T(8,128)(2,1)S(1)} %bitcast.14, bf16[4,768,128]{2,1,0:T(8,128)(2,1)S(1)} %bitcast.17, bf16[8,640,128]{2,1,0:T(8,128)(2,1)S(1)} %bitcast.18, bf16[640,128]{1,0:T(8,128)(2,1)S(1)} %shard_map.100.refs_4_), custom_call_target="tpu_custom_call" | custom-call | flops 10000 | bytes 10000 | tf_op jit(solution)/shard_map/pallas_call | solution.py:85
  162.8 0.0 copy-done.1
  162.8 1.5 shard_map.99
  164.3 8.6 %collective-permute-done.5.refs_2_ = bf16[640,128]{1,0:T(8,128)(2,1)S(1)} collective-permute-done((bf16[640,128]{1,0:T(8,128)(2,1)S(1)}, bf16[640,128]{1,0:T(8,128)(2,1)S(1)}, u32[]{:S(2)}, u32[]{:S(2)}) %collective-permute-start.5) | collective-permute-done | bytes 163872 | tf_op jit(solution)/shard_map/ppermute | solution.py:48
  172.9 1.2 shard_map.101
  (21 shorter events, 0.1 us)
Async XLA Ops:
  7.2 55.3 %all-gather.10.cloned.1.call-start = ((), (), s32[]{:S(2)}) async-start(), calls=%async_computation.4 | async-start | bytes 2949120 | tf_op jit(solution)/shard_map/all_gather | solution.py:261
  7.8 48.8 %copy-start.5 = (bf16[640,640]{1,0:T(8,128)(2,1)S(1)}, bf16[640,640]{1,0:T(8,128)(2,1)}, u32[]{:S(2)}) copy-start(bf16[640,640]{1,0:T(8,128)(2,1)} %refs_1_.3) | copy-start | bytes 2457604
  7.8 48.8 %copy-start.9 = (bf16[640,128]{1,0:T(8,128)(2,1)S(1)}, bf16[640,128]{1,0:T(8,128)(2,1)}, u32[]{:S(2)}) copy-start(bf16[640,128]{1,0:T(8,128)(2,1)} %refs_3_.4) | copy-start | bytes 491524
  7.8 48.8 %copy-start.10 = (s32[4]{0:T(128)S(1)}, s32[4]{0:T(128)}, u32[]{:S(2)}) copy-start(s32[4]{0:T(128)} %pad_add_fusion.refs_0_) | copy-start | bytes 52
  10.0 87.3 %all-gather.8.cloned.1.call-start = ((), (), s32[]{:S(2)}) async-start(), calls=%async_computation.3 | async-start | bytes 2359296 | tf_op jit(solution)/shard_map/all_gather | solution.py:276
  10.0 30.7 %collective-permute-start = (bf16[768,128]{1,0:T(8,128)(2,1)}, bf16[768,128]{1,0:T(8,128)(2,1)S(1)}, u32[]{:S(2)}, u32[]{:S(2)}) collective-permute-start(bf16[768,128]{1,0:T(8,128)(2,1)} %get-tuple-element.19), channel_id=1, source_target_pairs={{0,4},{1,5},{2,6},{3,7},{4,0},{5,1},{6,2},{7,3},{8,14},{9,15},{10,... | collective-permute-start | bytes 589832 | tf_op jit(solution)/shard_map/ppermute | solution.py:48
  59.6 0.9 copy-start.12
  60.5 4.4 %collective-permute-start.1 = (bf16[384,1024]{1,0:T(8,128)(2,1)}, bf16[384,1024]{1,0:T(8,128)(2,1)S(1)}, u32[]{:S(2)}, u32[]{:S(2)}) collective-permute-start(bf16[384,1024]{1,0:T(8,128)(2,1)} %copy-done.12), channel_id=1, source_target_pairs={{0,8},{8,0},{1,9},{9,1},{2,10},{10,2},{3,11},{11,3},{4,12},{12,4},... | collective-permute-start | bytes 2359304 | tf_op jit(solution)/shard_map/ppermute | solution.py:43
  66.5 16.9 %all-to-all-start = ((bf16[4,384,256]{2,1,0:T(8,128)(2,1)}), bf16[4,384,256]{2,1,0:T(8,128)(2,1)S(1)}, u32[]{:S(2)}, u32[]{:S(2)}) async-start(bf16[4,384,256]{2,1,0:T(8,128)(2,1)} %shard_map.94), calls=%async_computation | async-start | bytes 1572864 | tf_op jit(solution)/shard_map/all_to_all | solution.py:287
  70.8 6.6 %collective-permute-start.2 = (bf16[640,128]{1,0:T(8,128)(2,1)S(1)}, bf16[640,128]{1,0:T(8,128)(2,1)S(1)}, u32[]{:S(2)}, u32[]{:S(2)}) collective-permute-start(bf16[640,128]{1,0:T(8,128)(2,1)S(1)} %get-tuple-element.36), channel_id=1, source_target_pairs={{0,0},{1,16},{2,32},{3,48},{8,49},{9,1},{10,17},{11,33},{16,34},{1... | collective-permute-start | bytes 491528 | tf_op jit(solution)/shard_map/ppermute | solution.py:304
  71.5 6.9 %collective-permute-start.3 = (bf16[640,128]{1,0:T(8,128)(2,1)S(1)}, bf16[640,128]{1,0:T(8,128)(2,1)S(1)}, u32[]{:S(2)}, u32[]{:S(2)}) collective-permute-start(bf16[640,128]{1,0:T(8,128)(2,1)S(1)} %get-tuple-element.35), channel_id=1, source_target_pairs={{0,8},{1,24},{2,40},{3,56},{8,57},{9,9},{10,25},{11,41},{16,42},{1... | collective-permute-start | bytes 491528 | tf_op jit(solution)/shard_map/ppermute | solution.py:304
  84.8 19.0 %all-to-all-start.1 = ((bf16[4,320,256]{2,1,0:T(8,128)(2,1)}), bf16[4,320,256]{2,1,0:T(8,128)(2,1)S(1)}, u32[]{:S(2)}, u32[]{:S(2)}) async-start(bf16[4,320,256]{2,1,0:T(8,128)(2,1)} %get-tuple-element.24), calls=%async_computation.1 | async-start | bytes 1310720 | tf_op jit(solution)/shard_map/all_to_all | solution.py:316
  95.1 63.2 %all-gather.12.cloned.1.call-start = ((), (), s32[]{:S(2)}) async-start(), calls=%async_computation.5 | async-start | bytes 1474560 | tf_op jit(solution)/shard_map/all_gather | solution.py:347
  103.9 1.6 copy-start.11
  105.5 11.0 %copy-start.6 = (bf16[640,640]{1,0:T(8,128)(2,1)S(1)}, bf16[640,640]{1,0:T(8,128)(2,1)}, u32[]{:S(2)}) copy-start(bf16[640,640]{1,0:T(8,128)(2,1)} %refs_1_.3) | copy-start | bytes 2457604
  108.3 10.2 %copy-start.7 = (f32[320,128]{1,0:T(8,128)}, f32[320,128]{1,0:T(8,128)S(1)}, u32[]{:S(2)}) copy-start(f32[320,128]{1,0:T(8,128)S(1)} %get-tuple-element.26.refs_1_) | copy-start | bytes 491524
  108.3 8.2 %collective-permute-start.4 = (bf16[320,1152]{1,0:T(8,128)(2,1)S(1)}, bf16[320,1152]{1,0:T(8,128)(2,1)S(1)}, u32[]{:S(2)}, u32[]{:S(2)}) collective-permute-start(bf16[320,1152]{1,0:T(8,128)(2,1)S(1)} %get-tuple-element.27.refs_2_), channel_id=1, source_target_pairs={{0,8},{8,0},{1,9},{9,1},{2,10},{10,2},{3,11},{11,3},{4,12},{12,4},... | collective-permute-start | bytes 2211848 | tf_op jit(solution)/shard_map/ppermute | solution.py:43
  116.5 1.9 %copy-start = (bf16[320,1152]{1,0:T(8,128)(2,1)}, bf16[320,1152]{1,0:T(8,128)(2,1)S(1)}, u32[]{:S(2)}) copy-start(bf16[320,1152]{1,0:T(8,128)(2,1)S(1)} %collective-permute-done.4.refs_3_.refs_2_) | copy-start | bytes 2211844
  142.3 30.6 %collective-permute-start.5 = (bf16[640,128]{1,0:T(8,128)(2,1)S(1)}, bf16[640,128]{1,0:T(8,128)(2,1)S(1)}, u32[]{:S(2)}, u32[]{:S(2)}) collective-permute-start(bf16[640,128]{1,0:T(8,128)(2,1)S(1)} %shard_map.100.refs_4_), channel_id=1, source_target_pairs={{0,4},{1,5},{2,6},{3,7},{4,0},{5,1},{6,2},{7,3},{8,14},{9,15},{10,... | collective-permute-start | bytes 491528 | tf_op jit(solution)/shard_map/ppermute | solution.py:48
  158.3 1.3 copy-start.2
  159.7 3.1 %copy-start.1 = (bf16[320,1152]{1,0:T(8,128)(2,1)S(1)}, bf16[320,1152]{1,0:T(8,128)(2,1)}, u32[]{:S(2)}) copy-start(bf16[320,1152]{1,0:T(8,128)(2,1)} %copy-done) | copy-start | bytes 2211844
  159.7 3.1 %copy-start.3 = (f32[640,128]{1,0:T(8,128)S(1)}, f32[640,128]{1,0:T(8,128)}, u32[]{:S(2)}) copy-start(f32[640,128]{1,0:T(8,128)} %refs_3_.5) | copy-start | bytes 983044
  159.7 3.1 %copy-start.4 = (f32[640,128]{1,0:T(8,128)S(1)}, f32[640,128]{1,0:T(8,128)}, u32[]{:S(2)}) copy-start(f32[640,128]{1,0:T(8,128)} %refs_4_.5) | copy-start | bytes 983044
  159.7 3.1 %copy-start.8 = (f32[320,128]{1,0:T(8,128)S(1)}, f32[320,128]{1,0:T(8,128)}, u32[]{:S(2)}) copy-start(f32[320,128]{1,0:T(8,128)} %copy-done.7) | copy-start | bytes 491524
Sparse Core Ops, SparseCore 0:
  10.7 37.8 all-gather.9
  60.6 35.4 all-gather.7
  98.8 40.8 all-gather.11

commit v7 on v5

--- a/solution.py
+++ b/solution.py
@@ -57,7 +57,8 @@
     def target(x, c, z, y):
         if x // 2 != z:
             return None
-        return (y, core, z, 2 * (x % 2) + c)
+        there = 2 * (x % 2) + c
+        return ((y - there) % 4, core, z, there)
 
     return pairs(("x", "core", "zh", "y"), target)
 
@@ -67,7 +68,7 @@
 
 
 def call(
-    kernel, outs, where, *operands, after=(), scratch=(), flops=0, moved=0, limit=24
+    kernel, outs, where, *operands, after=(), scratch=(), flops=0, moved=0, limit=16
 ):
     n = len(operands)
 
@@ -100,8 +101,8 @@
     for k in range(4):
         slabs[:, 128 * k : 128 * k + 128] = near[k, 640:]
         slabs[:, 512 + 128 * k : 640 + 128 * k] = far[k, 640:]
-        panel[:, 128 * k : 128 * k + 128] = near[k, :640, :]
-        panel[:, 512 + 128 * k : 640 + 128 * k] = far[k, :640, :]
+        panel[:, 128 * k : 128 * k + 128] = near[k, :640]
+        panel[:, 512 + 128 * k : 640 + 128 * k] = far[k, :640]
 
     product = dot(left[...], panel[...], 0, 0).astype(bf16)
     gram = (dot(grad[...], panel[...], 0, 0) * (1.0 / M)).astype(bf16)
@@ -191,10 +192,6 @@
     send[...] = fold(parts, slice(640, 1280)).astype(bf16)
 
 
-def update_kernel(where, kept, arrived, update):
-    update[...] = (kept[...] + arrived[...].astype(f32)).astype(bf16)
-
-
 def moments_kernel(
     where, own, other, first, second, parts, first_new, second_new, kept
 ):
@@ -216,8 +213,8 @@
 
 def gram_kernel(where, near, far, paired, out, panel, other):
     for k in range(4):
-        panel[:, 128 * k : 128 * k + 128] = near[k, :640, :]
-        panel[:, 512 + 128 * k : 640 + 128 * k] = far[k, :640, :]
+        panel[:, 128 * k : 128 * k + 128] = near[k, :640]
+        panel[:, 512 + 128 * k : 640 + 128 * k] = far[k, :640]
     for k in range(8):
         other[:, 128 * k : 128 * k + 128] = paired[k]
     out[...] = dot(panel[...], other[...], 1, 1) * (1.0 / C)
@@ -272,11 +269,12 @@
     summed = lax.all_to_all(summed, "x", 0, 0, tiled=True)
 
     axes = ("x", "core", "zh", "y")
-    at = 2 * (y % 2)
+    to_x = (y + 8 - 2 * (x % 2) - core) % 4
+    at = 2 * (to_x % 2)
 
     def piece(t):
         return jnp.where(
-            y < 2,
+            to_x < 2,
             lax.dynamic_index_in_dim(near_all, at + t, 0, False)[:640],
             lax.dynamic_index_in_dim(far_all, at + t, 0, False)[:640],
         )
@@ -294,7 +292,7 @@
         [shaped((4, 320, 256), bf16), shaped((128, 128), f32)],
         where,
         summed,
-        after=(moments[:1, :1, :16], paired_mark),
+        after=(moments[:1, :1, :16],),
         moved=1_500_000,
     )
     half = lax.all_to_all(rows, "x", 0, 0, tiled=True)
@@ -306,6 +304,7 @@
         half,
         moments,
         basis,
+        after=(paired_mark,),
         scratch=[pltpu.VMEM((320, 1024), bf16), pltpu.VMEM((320, 1024), f32)],
         flops=1_400_000_000,
         moved=6_000_000,
@@ -353,14 +352,7 @@
         moved=10_000,
     )
 
-    (update,) = call(
-        update_kernel,
-        [shaped((640, 128), bf16)],
-        where,
-        kept,
-        arrived,
-        moved=700_000,
-    )
+    update = (kept + arrived.astype(f32)).astype(bf16)
     return (update, exp_avg_new, exp_avg_sq_new, left_gram, right_gram)
 
 

time: 185 us -> 175 us (0.946)
  the two profiles are of different devices: /device:TPU:32 before, /device:TPU:36 now
where the time goes in v7:
time: 175 us; the launch traced here: 174 us
  blocking collectives  64.3 us (37%)
  starting transfers between devices  42.3 us (24%)
  waiting for transfers between devices  26.2 us (15%)
  Pallas kernels  18.4 us (11%)
  between operations  13.9 us (8%)
  local copies, waits for them, and re-layouts  7.8 us (4%)
    ppermute x2, starting transfers between devices, other_half(): return lax.ppermute(value, 'zh', [(0, 1), (1, 0)])  26.7 us
    all_to_all x1, blocking collectives, body(): parts = lax.all_to_all(parts, 'y', 0, 0, tiled=True)  21.2 us
    pallas_call x10, Pallas kernels, call(): pl.pallas_call(inner, out_shape=outs, in_specs=[pl.BlockSpec(memory_space...  18.4 us
    all_to_all x1, blocking collectives, body(): summed = lax.all_to_all(summed, 'x', 0, 0, tiled=True)  14.7 us
    all_gather x1, blocking collectives, body(): far_all = lax.all_gather(far, 'y', axis=0)  14.4 us
    all_gather x1, blocking collectives, body(): near_all = lax.all_gather(mine, 'y', axis=0)  14 us
    ppermute x2, waiting for transfers between devices, body(): lax.ppermute(piece(t), axes, left_source(t))  12.4 us
    ppermute x2, waiting for transfers between devices, other_half(): return lax.ppermute(value, 'zh', [(0, 1), (1, 0)])  10.4 us
  transfers between devices with their start and end apart: 10, of which 5 were waited for; matrix products, arithmetic and copies ran while one was open for 1% of the time, Pallas kernels for 9%

profile of v7, /device:TPU:36, one launch (start us, length us, event | category | flops | bytes accessed | tf_op | source)
XLA Modules:
  0.0 174.3 jit_solution(3638456495746301775)
XLA Ops:
  7.2 0.0 all-gather.10.cloned.1.call-start
  7.2 0.6 pad_add_fusion.refs_0_
  7.8 2.1 %shard_map.92 = (bf16[768,128]{1,0:T(8,128)(2,1)}, bf16[2,640,128]{2,1,0:T(8,128)(2,1)}) custom-call(s32[4]{0:T(128)} %pad_add_fusion.refs_0_, bf16[640,128]{1,0:T(8,128)(2,1)} %refs_3_.4, bf16[1024,128]{1,0:T(8,128)(2,1)} %refs_2_.1, f32[640,128]{1,0:T(8,128)} %refs_3_.5, f32[640,128]{1,0:T(8,128)} %refs_4_.5), custom_call_target="tpu_custom_call" | custom-call | bytes 1500000 | tf_op jit(solution)/shard_map/pallas_call | solution.py:78
  9.9 0.0 all-gather.10.cloned.1.call-update
  10.0 0.0 all-gather.8.cloned.1.call-start
  10.0 14.8 %collective-permute-start = (bf16[768,128]{1,0:T(8,128)(2,1)}, bf16[768,128]{1,0:T(8,128)(2,1)S(1)}, u32[]{:S(2)}, u32[]{:S(2)}) collective-permute-start(bf16[768,128]{1,0:T(8,128)(2,1)} %get-tuple-element.19), channel_id=1, source_target_pairs={{0,4},{4,0},{1,5},{5,1},{2,6},{6,2},{3,7},{7,3},{8,12},{12,8},{9,1... | collective-permute-start | bytes 589832 | tf_op jit(solution)/shard_map/ppermute | solution.py:47
  24.8 14.0 %all-gather = bf16[3072,128]{1,0:T(8,128)(2,1)S(1)} all-gather(bf16[768,128]{1,0:T(8,128)(2,1)} %get-tuple-element.19), channel_id=2, replica_groups=mesh['layer'=8,'x'=4,'core'=2,'zh'=2,'y'=4] {'y'}, dimensions={0}, use_global_device_ids=true | all-gather | bytes 983040 | tf_op jit(solution)/shard_map/all_gather | solution.py:241
  38.9 1.6 collective-permute-done
  40.5 14.4 %all-gather.1 = bf16[3072,128]{1,0:T(8,128)(2,1)S(1)} all-gather(bf16[768,128]{1,0:T(8,128)(2,1)S(1)} %collective-permute-done), channel_id=3, replica_groups=mesh['layer'=8,'x'=4,'core'=2,'zh'=2,'y'=4] {'y'}, dimensions={0}, use_global_device_ids=true | all-gather | bytes 983040 | tf_op jit(solution)/shard_map/all_gather | solution.py:244
  54.9 0.0 copy-done.12
  54.9 3.0 %shard_map.93 = (bf16[384,1024]{1,0:T(8,128)(2,1)S(1)}, bf16[384,1024]{1,0:T(8,128)(2,1)S(1)}, bf16[128,1024]{1,0:T(8,128)(2,1)}) custom-call(s32[4]{0:T(128)S(1)} %copy-done.12, bf16[4,768,128]{2,1,0:T(8,128)(2,1)S(1)} %bitcast.12, bf16[4,768,128]{2,1,0:T(8,128)(2,1)S(1)} %bitcast.15, bf16[640,128]{1,0:T(8,128)(2,1)S(1)} %copy-done.11, ...), custom_call_target="tpu_custom_call" | custom-call | flops 1000000000 | bytes 5000000 | tf_op jit(solution)/shard_map/pallas_call | solution.py:78
  57.9 0.9 copy-done.7
  58.8 0.0 all-gather.8.cloned.1.call-update
  58.8 1.9 %collective-permute-start.1 = (bf16[384,1024]{1,0:T(8,128)(2,1)S(1)}, bf16[384,1024]{1,0:T(8,128)(2,1)S(1)}, u32[]{:S(2)}, u32[]{:S(2)}) collective-permute-start(bf16[384,1024]{1,0:T(8,128)(2,1)S(1)} %get-tuple-element.21), channel_id=1, source_target_pairs={{0,8},{8,0},{1,9},{9,1},{2,10},{10,2},{3,11},{11,3},{4,12},{12,4},... | collective-permute-start | bytes 2359304 | tf_op jit(solution)/shard_map/ppermute | solution.py:43
  60.8 0.0 all-gather.10.cloned.1.call-done
  60.8 0.8 constant_dynamic-slice_fusion
  61.5 1.5 collective-permute-done.1.refs_2_
  63.0 1.1 copy-done.8
  64.1 0.7 shard_map.94
  64.9 14.7 %all_to_all.15.refs_1_ = bf16[4,384,256]{2,1,0:T(8,128)(2,1)S(1)} all-to-all(bf16[4,384,256]{2,1,0:T(8,128)(2,1)S(1)} %shard_map.94), channel_id=1, replica_groups=mesh['layer'=8,'x'=4,'core'=2,'zh'=2,'y'=4] {'x'}, dimensions={0} | all-to-all | bytes 1572864 | tf_op jit(solution)/shard_map/all_to_all | solution.py:269
  79.6 1.5 shard_map.95
  81.0 7.1 %all-to-all-start.1 = ((bf16[4,320,256]{2,1,0:T(8,128)(2,1)}), bf16[4,320,256]{2,1,0:T(8,128)(2,1)S(1)}, u32[]{:S(2)}, u32[]{:S(2)}) async-start(bf16[4,320,256]{2,1,0:T(8,128)(2,1)} %get-tuple-element.23), calls=%async_computation.1 | async-start | bytes 1310720 | tf_op jit(solution)/shard_map/all_to_all | solution.py:298
  88.2 1.3 collective-permute-start.2
  89.5 0.7 collective-permute-start.3
  90.2 12.4 %collective-permute-done.2.refs_1_ = bf16[640,128]{1,0:T(8,128)(2,1)S(1)} collective-permute-done((bf16[640,128]{1,0:T(8,128)(2,1)S(1)}, bf16[640,128]{1,0:T(8,128)(2,1)S(1)}, u32[]{:S(2)}, u32[]{:S(2)}) %collective-permute-start.2) | collective-permute-done | bytes 163872 | tf_op jit(solution)/shard_map/ppermute | solution.py:286
  102.6 0.0 collective-permute-done.3.refs_2_
  102.6 1.2 shard_map.96
  103.8 0.0 all-gather.12.cloned.1.call-update
  103.9 1.4 constant_dynamic-slice_fusion.1.refs_2_
  105.3 0.0 all-gather.8.cloned.1.call-done.refs_3_
  105.3 0.0 all-to-all-done.1.refs_1_
  105.4 1.6 copy-done.13
  106.9 2.8 %shard_map.97 = (bf16[320,1152]{1,0:T(8,128)(2,1)S(1)}, f32[320,128]{1,0:T(8,128)S(1)}) custom-call(s32[4]{0:T(128)S(1)} %copy-done.12, bf16[4,320,256]{2,1,0:T(8,128)(2,1)S(1)} %all-to-all-done.1.refs_1_, bf16[8,2,320,128]{3,2,1,0:T(8,128)(2,1)S(1)} %constant_dynamic-slice_fusion.1.refs_2_, bf16[1024,1024]{1,0:T(8,128)(2,1)S(1)} %copy-done.13, ...), custom_call_target="tpu_custom_call" | custom-call | flops 1400000000 | bytes 6000000 | tf_op jit(solution)/shard_map/pallas_call | solution.py:78
  109.7 0.0 copy-start.9
  109.8 0.7 copy-done.9
  110.4 4.5 %collective-permute-start.4 = (bf16[320,1152]{1,0:T(8,128)(2,1)S(1)}, bf16[320,1152]{1,0:T(8,128)(2,1)S(1)}, u32[]{:S(2)}, u32[]{:S(2)}) collective-permute-start(bf16[320,1152]{1,0:T(8,128)(2,1)S(1)} %get-tuple-element.27.refs_2_), channel_id=1, source_target_pairs={{0,8},{8,0},{1,9},{9,1},{2,10},{10,2},{3,11},{11,3},{4,12},{12,4},... | collective-permute-start | bytes 2211848 | tf_op jit(solution)/shard_map/ppermute | solution.py:43
  114.9 1.8 %collective-permute-done.4.refs_3_.refs_2_ = bf16[320,1152]{1,0:T(8,128)(2,1)S(1)} collective-permute-done((bf16[320,1152]{1,0:T(8,128)(2,1)S(1)}, bf16[320,1152]{1,0:T(8,128)(2,1)S(1)}, u32[]{:S(2)}, u32[]{:S(2)}) %collective-permute-start.4) | collective-permute-done | bytes 737312 | tf_op jit(solution)/shard_map/ppermute | solution.py:43
  116.8 1.8 %shard_map.98 = bf16[4,1280,128]{2,1,0:T(8,128)(2,1)S(1)} custom-call(s32[4]{0:T(128)S(1)} %copy-done.12, bf16[640,640]{1,0:T(8,128)(2,1)S(1)} %copy-done.6, bf16[320,1152]{1,0:T(8,128)(2,1)S(1)} %get-tuple-element.27.refs_2_, bf16[320,1152]{1,0:T(8,128)(2,1)S(1)} %collective-permute-done.4.refs_3_.refs_2_), custom_call_target="tpu_custom_call" | custom-call | flops 840000000 | bytes 4000000 | tf_op jit(solution)/shard_map/pallas_call | solution.py:78
  118.6 0.0 copy-done
  118.6 21.2 %all_to_all.16.refs_5_.refs_1_ = bf16[4,1280,128]{2,1,0:T(8,128)(2,1)S(1)} all-to-all(bf16[4,1280,128]{2,1,0:T(8,128)(2,1)S(1)} %shard_map.98), channel_id=1, replica_groups=mesh['layer'=8,'x'=4,'core'=2,'zh'=2,'y'=4] {'y'}, dimensions={0} | all-to-all | bytes 2621440 | tf_op jit(solution)/shard_map/all_to_all | solution.py:324
  139.7 0.6 shard_map.100.refs_4_
  140.4 11.9 %collective-permute-start.5 = (bf16[640,128]{1,0:T(8,128)(2,1)S(1)}, bf16[640,128]{1,0:T(8,128)(2,1)S(1)}, u32[]{:S(2)}, u32[]{:S(2)}) collective-permute-start(bf16[640,128]{1,0:T(8,128)(2,1)S(1)} %shard_map.100.refs_4_), channel_id=1, source_target_pairs={{0,4},{4,0},{1,5},{5,1},{2,6},{6,2},{3,7},{7,3},{8,12},{12,8},{9,1... | collective-permute-start | bytes 491528 | tf_op jit(solution)/shard_map/ppermute | solution.py:47
  152.2 0.0 all-gather.12.cloned.1.call-done
  152.3 1.3 copy-done.2
  153.6 3.1 %shard_map.101 = f32[640,640]{1,0:T(8,128)} custom-call(s32[4]{0:T(128)S(1)} %copy-done.12, bf16[4,768,128]{2,1,0:T(8,128)(2,1)S(1)} %bitcast.14, bf16[4,768,128]{2,1,0:T(8,128)(2,1)S(1)} %bitcast.17, bf16[8,640,128]{2,1,0:T(8,128)(2,1)S(1)} %bitcast.18, bf16[640,128]{1,0:T(8,128)(2,1)S(1)} %shard_map.100.refs_4_), custom_call_target="tpu_custom_call" | custom-call | flops 10000 | bytes 10000 | tf_op jit(solution)/shard_map/pallas_call | solution.py:78
  156.7 1.5 shard_map.99
  158.2 8.8 %collective-permute-done.5 = bf16[640,128]{1,0:T(8,128)(2,1)S(1)} collective-permute-done((bf16[640,128]{1,0:T(8,128)(2,1)S(1)}, bf16[640,128]{1,0:T(8,128)(2,1)S(1)}, u32[]{:S(2)}, u32[]{:S(2)}) %collective-permute-start.5) | collective-permute-done | bytes 163872 | tf_op jit(solution)/shard_map/ppermute | solution.py:47
  167.0 0.7 add_convert_fusion
  (22 shorter events, 0.1 us)
Async XLA Ops:
  7.2 53.6 %all-gather.10.cloned.1.call-start = ((), (), s32[]{:S(2)}) async-start(), calls=%async_computation.4 | async-start | bytes 2949120 | tf_op jit(solution)/shard_map/all_gather | solution.py:243
  7.8 47.1 %copy-start.5 = (bf16[640,640]{1,0:T(8,128)(2,1)S(1)}, bf16[640,640]{1,0:T(8,128)(2,1)}, u32[]{:S(2)}) copy-start(bf16[640,640]{1,0:T(8,128)(2,1)} %refs_1_.3) | copy-start | bytes 2457604
  7.8 47.1 %copy-start.11 = (bf16[640,128]{1,0:T(8,128)(2,1)S(1)}, bf16[640,128]{1,0:T(8,128)(2,1)}, u32[]{:S(2)}) copy-start(bf16[640,128]{1,0:T(8,128)(2,1)} %refs_3_.4) | copy-start | bytes 491524
  7.8 47.1 %copy-start.12 = (s32[4]{0:T(128)S(1)}, s32[4]{0:T(128)}, u32[]{:S(2)}) copy-start(s32[4]{0:T(128)} %pad_add_fusion.refs_0_) | copy-start | bytes 52
  10.0 95.4 %all-gather.8.cloned.1.call-start = ((), (), s32[]{:S(2)}) async-start(), calls=%async_computation.3 | async-start | bytes 2359296 | tf_op jit(solution)/shard_map/all_gather | solution.py:258
  10.0 30.5 %collective-permute-start = (bf16[768,128]{1,0:T(8,128)(2,1)}, bf16[768,128]{1,0:T(8,128)(2,1)S(1)}, u32[]{:S(2)}, u32[]{:S(2)}) collective-permute-start(bf16[768,128]{1,0:T(8,128)(2,1)} %get-tuple-element.19), channel_id=1, source_target_pairs={{0,4},{4,0},{1,5},{5,1},{2,6},{6,2},{3,7},{7,3},{8,12},{12,8},{9,1... | collective-permute-start | bytes 589832 | tf_op jit(solution)/shard_map/ppermute | solution.py:47
  57.9 0.9 copy-start.7
  58.8 4.2 %collective-permute-start.1 = (bf16[384,1024]{1,0:T(8,128)(2,1)S(1)}, bf16[384,1024]{1,0:T(8,128)(2,1)S(1)}, u32[]{:S(2)}, u32[]{:S(2)}) collective-permute-start(bf16[384,1024]{1,0:T(8,128)(2,1)S(1)} %get-tuple-element.21), channel_id=1, source_target_pairs={{0,8},{8,0},{1,9},{9,1},{2,10},{10,2},{3,11},{11,3},{4,12},{12,4},... | collective-permute-start | bytes 2359304 | tf_op jit(solution)/shard_map/ppermute | solution.py:43
  63.0 1.1 copy-start.8
  81.0 24.3 %all-to-all-start.1 = ((bf16[4,320,256]{2,1,0:T(8,128)(2,1)}), bf16[4,320,256]{2,1,0:T(8,128)(2,1)S(1)}, u32[]{:S(2)}, u32[]{:S(2)}) async-start(bf16[4,320,256]{2,1,0:T(8,128)(2,1)} %get-tuple-element.23), calls=%async_computation.1 | async-start | bytes 1310720 | tf_op jit(solution)/shard_map/all_to_all | solution.py:298
  88.2 64.1 %all-gather.12.cloned.1.call-start = ((), (), s32[]{:S(2)}) async-start(), calls=%async_computation.5 | async-start | bytes 1474560 | tf_op jit(solution)/shard_map/all_gather | solution.py:330
  88.2 14.4 %collective-permute-start.2 = (bf16[640,128]{1,0:T(8,128)(2,1)S(1)}, bf16[640,128]{1,0:T(8,128)(2,1)S(1)}, u32[]{:S(2)}, u32[]{:S(2)}) collective-permute-start(bf16[640,128]{1,0:T(8,128)(2,1)S(1)} %get-tuple-element.36), channel_id=1, source_target_pairs={{0,0},{1,16},{2,32},{3,48},{8,49},{9,1},{10,17},{11,33},{16,34},{1... | collective-permute-start | bytes 491528 | tf_op jit(solution)/shard_map/ppermute | solution.py:286
  89.5 13.1 %collective-permute-start.3 = (bf16[640,128]{1,0:T(8,128)(2,1)S(1)}, bf16[640,128]{1,0:T(8,128)(2,1)S(1)}, u32[]{:S(2)}, u32[]{:S(2)}) collective-permute-start(bf16[640,128]{1,0:T(8,128)(2,1)S(1)} %get-tuple-element.35), channel_id=1, source_target_pairs={{0,8},{1,24},{2,40},{3,56},{8,57},{9,9},{10,25},{11,41},{16,42},{1... | collective-permute-start | bytes 491528 | tf_op jit(solution)/shard_map/ppermute | solution.py:286
  105.3 1.6 copy-start.13
  106.9 9.8 %copy-start.6 = (bf16[640,640]{1,0:T(8,128)(2,1)S(1)}, bf16[640,640]{1,0:T(8,128)(2,1)}, u32[]{:S(2)}) copy-start(bf16[640,640]{1,0:T(8,128)(2,1)} %refs_1_.3) | copy-start | bytes 2457604
  109.7 0.7 copy-start.9
  110.4 6.3 %collective-permute-start.4 = (bf16[320,1152]{1,0:T(8,128)(2,1)S(1)}, bf16[320,1152]{1,0:T(8,128)(2,1)S(1)}, u32[]{:S(2)}, u32[]{:S(2)}) collective-permute-start(bf16[320,1152]{1,0:T(8,128)(2,1)S(1)} %get-tuple-element.27.refs_2_), channel_id=1, source_target_pairs={{0,8},{8,0},{1,9},{9,1},{2,10},{10,2},{3,11},{11,3},{4,12},{12,4},... | collective-permute-start | bytes 2211848 | tf_op jit(solution)/shard_map/ppermute | solution.py:43
  116.7 1.8 %copy-start = (bf16[320,1152]{1,0:T(8,128)(2,1)}, bf16[320,1152]{1,0:T(8,128)(2,1)S(1)}, u32[]{:S(2)}) copy-start(bf16[320,1152]{1,0:T(8,128)(2,1)S(1)} %collective-permute-done.4.refs_3_.refs_2_) | copy-start | bytes 2211844
  140.4 26.7 %collective-permute-start.5 = (bf16[640,128]{1,0:T(8,128)(2,1)S(1)}, bf16[640,128]{1,0:T(8,128)(2,1)S(1)}, u32[]{:S(2)}, u32[]{:S(2)}) collective-permute-start(bf16[640,128]{1,0:T(8,128)(2,1)S(1)} %shard_map.100.refs_4_), channel_id=1, source_target_pairs={{0,4},{4,0},{1,5},{5,1},{2,6},{6,2},{3,7},{7,3},{8,12},{12,8},{9,1... | collective-permute-start | bytes 491528 | tf_op jit(solution)/shard_map/ppermute | solution.py:47
  152.3 1.3 copy-start.2
  153.6 3.1 %copy-start.1 = (bf16[320,1152]{1,0:T(8,128)(2,1)S(1)}, bf16[320,1152]{1,0:T(8,128)(2,1)}, u32[]{:S(2)}) copy-start(bf16[320,1152]{1,0:T(8,128)(2,1)} %copy-done) | copy-start | bytes 2211844
  153.6 3.1 %copy-start.3 = (f32[640,128]{1,0:T(8,128)S(1)}, f32[640,128]{1,0:T(8,128)}, u32[]{:S(2)}) copy-start(f32[640,128]{1,0:T(8,128)} %refs_3_.5) | copy-start | bytes 983044
  153.6 3.1 %copy-start.4 = (f32[640,128]{1,0:T(8,128)S(1)}, f32[640,128]{1,0:T(8,128)}, u32[]{:S(2)}) copy-start(f32[640,128]{1,0:T(8,128)} %refs_4_.5) | copy-start | bytes 983044
  153.6 3.1 %copy-start.10 = (f32[320,128]{1,0:T(8,128)S(1)}, f32[320,128]{1,0:T(8,128)}, u32[]{:S(2)}) copy-start(f32[320,128]{1,0:T(8,128)} %copy-done.9) | copy-start | bytes 491524
Sparse Core Ops, SparseCore 0:
  10.7 37.1 all-gather.9
  58.9 33.8 all-gather.7
  104.0 32.9 all-gather.11

commit v8 on v7

--- a/solution.py
+++ b/solution.py
@@ -256,16 +256,16 @@
         moved=5_000_000,
     )
     basis = lax.all_gather(slabs, ROW, axis=0, tiled=True)
+    moments = lax.dynamic_slice_in_dim(moments, core * 320, 320, 2)
     (summed,) = call(
         join_kernel,
         [shaped((4, 384, 256), bf16)],
         where,
         keep,
         other_core(send),
-        after=(moments[:1, :1, :16],),
+        after=(moments,),
         moved=2_400_000,
     )
-    moments = lax.dynamic_slice_in_dim(moments, core * 320, 320, 2)
     summed = lax.all_to_all(summed, "x", 0, 0, tiled=True)
 
     axes = ("x", "core", "zh", "y")
@@ -292,7 +292,6 @@
         [shaped((4, 320, 256), bf16), shaped((128, 128), f32)],
         where,
         summed,
-        after=(moments[:1, :1, :16],),
         moved=1_500_000,
     )
     half = lax.all_to_all(rows, "x", 0, 0, tiled=True)

time: 175 us -> 173 us (0.989)
  the two profiles are of different devices: /device:TPU:36 before, /device:TPU:34 now
where the time goes in v8:
time: 173 us; the launch traced here: 172 us
  blocking collectives  67.9 us (39%)
  starting transfers between devices  45 us (26%)
  waiting for transfers between devices  19 us (11%)
  Pallas kernels  18.3 us (11%)
  between operations  14 us (8%)
  local copies, waits for them, and re-layouts  6.86 us (4%)
    ppermute x2, starting transfers between devices, other_half(): return lax.ppermute(value, 'zh', [(0, 1), (1, 0)])  29.6 us
    all_to_all x1, blocking collectives, body(): parts = lax.all_to_all(parts, 'y', 0, 0, tiled=True)  23.2 us
    pallas_call x10, Pallas kernels, call(): pl.pallas_call(inner, out_shape=outs, in_specs=[pl.BlockSpec(memory_space...  18.3 us
    all_to_all x1, blocking collectives, body(): summed = lax.all_to_all(summed, 'x', 0, 0, tiled=True)  16.3 us
    all_gather x1, blocking collectives, body(): far_all = lax.all_gather(far, 'y', axis=0)  14.4 us
    all_gather x1, blocking collectives, body(): near_all = lax.all_gather(mine, 'y', axis=0)  14 us
    ppermute x2, waiting for transfers between devices, other_half(): return lax.ppermute(value, 'zh', [(0, 1), (1, 0)])  9.85 us
    ppermute x2, waiting for transfers between devices, body(): lax.ppermute(piece(t), axes, left_source(t))  6.23 us
  transfers between devices with their start and end apart: 10, of which 5 were waited for; matrix products, arithmetic and copies ran while one was open for 1% of the time, Pallas kernels for 9%

profile of v8, /device:TPU:34, one launch (start us, length us, event | category | flops | bytes accessed | tf_op | source)
XLA Modules:
  0.0 172.4 jit_solution(5200573752035768271)
XLA Ops:
  7.2 0.0 all-gather.10.cloned.1.call-start
  7.2 0.6 pad_add_fusion.refs_0_
  7.8 2.0 %shard_map.92 = (bf16[768,128]{1,0:T(8,128)(2,1)}, bf16[2,640,128]{2,1,0:T(8,128)(2,1)}) custom-call(s32[4]{0:T(128)} %pad_add_fusion.refs_0_, bf16[640,128]{1,0:T(8,128)(2,1)} %refs_3_.4, bf16[1024,128]{1,0:T(8,128)(2,1)} %refs_2_.1, f32[640,128]{1,0:T(8,128)} %refs_3_.5, f32[640,128]{1,0:T(8,128)} %refs_4_.5), custom_call_target="tpu_custom_call" | custom-call | bytes 1500000 | tf_op jit(solution)/shard_map/pallas_call | solution.py:78
  9.9 0.0 all-gather.10.cloned.1.call-update
  9.9 0.0 all-gather.8.cloned.1.call-start
  9.9 15.0 %collective-permute-start = (bf16[768,128]{1,0:T(8,128)(2,1)}, bf16[768,128]{1,0:T(8,128)(2,1)S(1)}, u32[]{:S(2)}, u32[]{:S(2)}) collective-permute-start(bf16[768,128]{1,0:T(8,128)(2,1)} %get-tuple-element.19), channel_id=1, source_target_pairs={{0,4},{4,0},{1,5},{5,1},{2,6},{6,2},{3,7},{7,3},{8,12},{12,8},{9,1... | collective-permute-start | bytes 589832 | tf_op jit(solution)/shard_map/ppermute | solution.py:47
  24.9 14.0 %all-gather = bf16[3072,128]{1,0:T(8,128)(2,1)S(1)} all-gather(bf16[768,128]{1,0:T(8,128)(2,1)} %get-tuple-element.19), channel_id=2, replica_groups=mesh['layer'=8,'x'=4,'core'=2,'zh'=2,'y'=4] {'y'}, dimensions={0}, use_global_device_ids=true | all-gather | bytes 983040 | tf_op jit(solution)/shard_map/all_gather | solution.py:241
  38.9 1.6 collective-permute-done
  40.6 14.4 %all-gather.1 = bf16[3072,128]{1,0:T(8,128)(2,1)S(1)} all-gather(bf16[768,128]{1,0:T(8,128)(2,1)S(1)} %collective-permute-done), channel_id=3, replica_groups=mesh['layer'=8,'x'=4,'core'=2,'zh'=2,'y'=4] {'y'}, dimensions={0}, use_global_device_ids=true | all-gather | bytes 983040 | tf_op jit(solution)/shard_map/all_gather | solution.py:244
  54.9 0.0 copy-done.14
  54.9 3.3 %shard_map.93 = (bf16[384,1024]{1,0:T(8,128)(2,1)S(1)}, bf16[384,1024]{1,0:T(8,128)(2,1)}, bf16[128,1024]{1,0:T(8,128)(2,1)}) custom-call(s32[4]{0:T(128)S(1)} %copy-done.14, bf16[4,768,128]{2,1,0:T(8,128)(2,1)S(1)} %bitcast.12, bf16[4,768,128]{2,1,0:T(8,128)(2,1)S(1)} %bitcast.15, bf16[640,128]{1,0:T(8,128)(2,1)S(1)} %copy-done.13, ...), custom_call_target="tpu_custom_call" | custom-call | flops 1000000000 | bytes 5000000 | tf_op jit(solution)/shard_map/pallas_call | solution.py:78
  58.2 0.9 copy-done.7
  59.1 0.0 all-gather.8.cloned.1.call-update
  59.2 1.9 %collective-permute-start.1 = (bf16[384,1024]{1,0:T(8,128)(2,1)}, bf16[384,1024]{1,0:T(8,128)(2,1)}, u32[]{:S(2)}, u32[]{:S(2)}) collective-permute-start(bf16[384,1024]{1,0:T(8,128)(2,1)} %get-tuple-element.21), channel_id=1, source_target_pairs={{0,8},{8,0},{1,9},{9,1},{2,10},{10,2},{3,11},{11,3},{4,12},{12,4},... | collective-permute-start | bytes 2359304 | tf_op jit(solution)/shard_map/ppermute | solution.py:43
  61.1 0.0 all-gather.10.cloned.1.call-done
  61.1 1.5 constant_dynamic-slice_fusion.refs_3_.refs_2_
  62.7 1.0 collective-permute-done.1.refs_2_
  63.7 1.3 shard_map.94
  65.0 16.3 %all_to_all.15.refs_1_ = bf16[4,384,256]{2,1,0:T(8,128)(2,1)S(1)} all-to-all(bf16[4,384,256]{2,1,0:T(8,128)(2,1)S(1)} %shard_map.94), channel_id=1, replica_groups=mesh['layer'=8,'x'=4,'core'=2,'zh'=2,'y'=4] {'x'}, dimensions={0} | all-to-all | bytes 1572864 | tf_op jit(solution)/shard_map/all_to_all | solution.py:269
  81.3 1.2 shard_map.95
  82.5 0.8 copy-done.9
  83.3 5.2 %all-to-all-start.1 = ((bf16[4,320,256]{2,1,0:T(8,128)(2,1)}), bf16[4,320,256]{2,1,0:T(8,128)(2,1)S(1)}, u32[]{:S(2)}, u32[]{:S(2)}) async-start(bf16[4,320,256]{2,1,0:T(8,128)(2,1)} %copy-done.9), calls=%async_computation.1 | async-start | bytes 1310720 | tf_op jit(solution)/shard_map/all_to_all | solution.py:297
  88.6 3.5 %collective-permute-start.2 = (bf16[640,128]{1,0:T(8,128)(2,1)S(1)}, bf16[640,128]{1,0:T(8,128)(2,1)S(1)}, u32[]{:S(2)}, u32[]{:S(2)}) collective-permute-start(bf16[640,128]{1,0:T(8,128)(2,1)S(1)} %get-tuple-element.34), channel_id=1, source_target_pairs={{0,0},{1,16},{2,32},{3,48},{8,49},{9,1},{10,17},{11,33},{16,34},{1... | collective-permute-start | bytes 491528 | tf_op jit(solution)/shard_map/ppermute | solution.py:286
  92.0 1.3 collective-permute-start.3
  93.3 6.2 %collective-permute-done.2.refs_1_ = bf16[640,128]{1,0:T(8,128)(2,1)S(1)} collective-permute-done((bf16[640,128]{1,0:T(8,128)(2,1)S(1)}, bf16[640,128]{1,0:T(8,128)(2,1)S(1)}, u32[]{:S(2)}, u32[]{:S(2)}) %collective-permute-start.2) | collective-permute-done | bytes 163872 | tf_op jit(solution)/shard_map/ppermute | solution.py:286
  99.6 0.0 collective-permute-done.3.refs_2_
  99.6 0.6 shard_map.96
  100.2 0.0 copy-start.12
  100.2 0.7 copy-done.12
  100.8 0.0 all-gather.12.cloned.1.call-update
  100.9 0.0 all-gather.8.cloned.1.call-done.refs_3_
  100.9 0.0 all-to-all-done.1.refs_1_
  100.9 1.6 copy-done.15
  102.5 2.8 %shard_map.97 = (bf16[320,1152]{1,0:T(8,128)(2,1)S(1)}, f32[320,128]{1,0:T(8,128)S(1)}) custom-call(s32[4]{0:T(128)S(1)} %copy-done.14, bf16[4,320,256]{2,1,0:T(8,128)(2,1)S(1)} %all-to-all-done.1.refs_1_, bf16[8,2,320,128]{3,2,1,0:T(8,128)(2,1)S(1)} %constant_dynamic-slice_fusion.refs_3_.refs_2_, bf16[1024,1024]{1,0:T(8,128)(2,1)S(1)} %copy-done.15, ...), custom_call_target="tpu_custom_call" | custom-call | flops 1400000000 | bytes 6000000 | tf_op jit(solution)/shard_map/pallas_call | solution.py:78
  105.3 0.0 copy-start.10
  105.3 3.5 %collective-permute-start.4 = (bf16[320,1152]{1,0:T(8,128)(2,1)S(1)}, bf16[320,1152]{1,0:T(8,128)(2,1)S(1)}, u32[]{:S(2)}, u32[]{:S(2)}) collective-permute-start(bf16[320,1152]{1,0:T(8,128)(2,1)S(1)} %get-tuple-element.27.refs_2_), channel_id=1, source_target_pairs={{0,8},{8,0},{1,9},{9,1},{2,10},{10,2},{3,11},{11,3},{4,12},{12,4},... | collective-permute-start | bytes 2211848 | tf_op jit(solution)/shard_map/ppermute | solution.py:43
  108.8 1.8 %collective-permute-done.4.refs_3_.refs_2_ = bf16[320,1152]{1,0:T(8,128)(2,1)S(1)} collective-permute-done((bf16[320,1152]{1,0:T(8,128)(2,1)S(1)}, bf16[320,1152]{1,0:T(8,128)(2,1)S(1)}, u32[]{:S(2)}, u32[]{:S(2)}) %collective-permute-start.4) | collective-permute-done | bytes 737312 | tf_op jit(solution)/shard_map/ppermute | solution.py:43
  110.6 1.8 %shard_map.98 = bf16[4,1280,128]{2,1,0:T(8,128)(2,1)S(1)} custom-call(s32[4]{0:T(128)S(1)} %copy-done.14, bf16[640,640]{1,0:T(8,128)(2,1)S(1)} %copy-done.6, bf16[320,1152]{1,0:T(8,128)(2,1)S(1)} %get-tuple-element.27.refs_2_, bf16[320,1152]{1,0:T(8,128)(2,1)S(1)} %collective-permute-done.4.refs_3_.refs_2_), custom_call_target="tpu_custom_call" | custom-call | flops 840000000 | bytes 4000000 | tf_op jit(solution)/shard_map/pallas_call | solution.py:78
  112.5 23.2 %all_to_all.16.refs_5_.refs_1_ = bf16[4,1280,128]{2,1,0:T(8,128)(2,1)S(1)} all-to-all(bf16[4,1280,128]{2,1,0:T(8,128)(2,1)S(1)} %shard_map.98), channel_id=1, replica_groups=mesh['layer'=8,'x'=4,'core'=2,'zh'=2,'y'=4] {'y'}, dimensions={0} | all-to-all | bytes 2621440 | tf_op jit(solution)/shard_map/all_to_all | solution.py:323
  135.7 0.6 shard_map.100.refs_4_
  136.3 14.6 %collective-permute-start.5 = (bf16[640,128]{1,0:T(8,128)(2,1)S(1)}, bf16[640,128]{1,0:T(8,128)(2,1)S(1)}, u32[]{:S(2)}, u32[]{:S(2)}) collective-permute-start(bf16[640,128]{1,0:T(8,128)(2,1)S(1)} %shard_map.100.refs_4_), channel_id=1, source_target_pairs={{0,4},{4,0},{1,5},{5,1},{2,6},{6,2},{3,7},{7,3},{8,12},{12,8},{9,1... | collective-permute-start | bytes 491528 | tf_op jit(solution)/shard_map/ppermute | solution.py:47
  150.9 0.0 all-gather.12.cloned.1.call-done
  151.0 1.3 copy-done.2
  152.3 3.1 %shard_map.101 = f32[640,640]{1,0:T(8,128)} custom-call(s32[4]{0:T(128)S(1)} %copy-done.14, bf16[4,768,128]{2,1,0:T(8,128)(2,1)S(1)} %bitcast.14, bf16[4,768,128]{2,1,0:T(8,128)(2,1)S(1)} %bitcast.17, bf16[8,640,128]{2,1,0:T(8,128)(2,1)S(1)} %bitcast.18, bf16[640,128]{1,0:T(8,128)(2,1)S(1)} %shard_map.100.refs_4_), custom_call_target="tpu_custom_call" | custom-call | flops 10000 | bytes 10000 | tf_op jit(solution)/shard_map/pallas_call | solution.py:78
  155.4 0.0 copy-done.3
  155.4 1.5 shard_map.99
  156.9 8.2 %collective-permute-done.5 = bf16[640,128]{1,0:T(8,128)(2,1)S(1)} collective-permute-done((bf16[640,128]{1,0:T(8,128)(2,1)S(1)}, bf16[640,128]{1,0:T(8,128)(2,1)S(1)}, u32[]{:S(2)}, u32[]{:S(2)}) %collective-permute-start.5) | collective-permute-done | bytes 163872 | tf_op jit(solution)/shard_map/ppermute | solution.py:47
  165.1 0.7 add_convert_fusion
  (25 shorter events, 0.1 us)
Async XLA Ops:
  7.2 54.0 %all-gather.10.cloned.1.call-start = ((), (), s32[]{:S(2)}) async-start(), calls=%async_computation.4 | async-start | bytes 2949120 | tf_op jit(solution)/shard_map/all_gather | solution.py:243
  9.9 45.1 %copy-start.5 = (bf16[640,640]{1,0:T(8,128)(2,1)S(1)}, bf16[640,640]{1,0:T(8,128)(2,1)}, u32[]{:S(2)}) copy-start(bf16[640,640]{1,0:T(8,128)(2,1)} %refs_1_.3) | copy-start | bytes 2457604
  9.9 45.1 %copy-start.13 = (bf16[640,128]{1,0:T(8,128)(2,1)S(1)}, bf16[640,128]{1,0:T(8,128)(2,1)}, u32[]{:S(2)}) copy-start(bf16[640,128]{1,0:T(8,128)(2,1)} %refs_3_.4) | copy-start | bytes 491524
  9.9 45.1 %copy-start.14 = (s32[4]{0:T(128)S(1)}, s32[4]{0:T(128)}, u32[]{:S(2)}) copy-start(s32[4]{0:T(128)} %pad_add_fusion.refs_0_) | copy-start | bytes 52
  9.9 91.0 %all-gather.8.cloned.1.call-start = ((), (), s32[]{:S(2)}) async-start(), calls=%async_computation.3 | async-start | bytes 2359296 | tf_op jit(solution)/shard_map/all_gather | solution.py:258
  9.9 30.6 %collective-permute-start = (bf16[768,128]{1,0:T(8,128)(2,1)}, bf16[768,128]{1,0:T(8,128)(2,1)S(1)}, u32[]{:S(2)}, u32[]{:S(2)}) collective-permute-start(bf16[768,128]{1,0:T(8,128)(2,1)} %get-tuple-element.19), channel_id=1, source_target_pairs={{0,4},{4,0},{1,5},{5,1},{2,6},{6,2},{3,7},{7,3},{8,12},{12,8},{9,1... | collective-permute-start | bytes 589832 | tf_op jit(solution)/shard_map/ppermute | solution.py:47
  58.2 0.9 copy-start.7
  59.2 4.5 %collective-permute-start.1 = (bf16[384,1024]{1,0:T(8,128)(2,1)}, bf16[384,1024]{1,0:T(8,128)(2,1)}, u32[]{:S(2)}, u32[]{:S(2)}) collective-permute-start(bf16[384,1024]{1,0:T(8,128)(2,1)} %get-tuple-element.21), channel_id=1, source_target_pairs={{0,8},{8,0},{1,9},{9,1},{2,10},{10,2},{3,11},{11,3},{4,12},{12,4},... | collective-permute-start | bytes 2359304 | tf_op jit(solution)/shard_map/ppermute | solution.py:43
  61.1 2.6 %copy-start.8 = (bf16[384,1024]{1,0:T(8,128)(2,1)S(1)}, bf16[384,1024]{1,0:T(8,128)(2,1)}, u32[]{:S(2)}) copy-start(bf16[384,1024]{1,0:T(8,128)(2,1)} %copy-done.7) | copy-start | bytes 2359300
  82.5 0.8 copy-start.9
  83.3 17.6 %all-to-all-start.1 = ((bf16[4,320,256]{2,1,0:T(8,128)(2,1)}), bf16[4,320,256]{2,1,0:T(8,128)(2,1)S(1)}, u32[]{:S(2)}, u32[]{:S(2)}) async-start(bf16[4,320,256]{2,1,0:T(8,128)(2,1)} %copy-done.9), calls=%async_computation.1 | async-start | bytes 1310720 | tf_op jit(solution)/shard_map/all_to_all | solution.py:297
  88.5 62.4 %all-gather.12.cloned.1.call-start = ((), (), s32[]{:S(2)}) async-start(), calls=%async_computation.5 | async-start | bytes 1474560 | tf_op jit(solution)/shard_map/all_gather | solution.py:329
  88.6 11.0 %collective-permute-start.2 = (bf16[640,128]{1,0:T(8,128)(2,1)S(1)}, bf16[640,128]{1,0:T(8,128)(2,1)S(1)}, u32[]{:S(2)}, u32[]{:S(2)}) collective-permute-start(bf16[640,128]{1,0:T(8,128)(2,1)S(1)} %get-tuple-element.34), channel_id=1, source_target_pairs={{0,0},{1,16},{2,32},{3,48},{8,49},{9,1},{10,17},{11,33},{16,34},{1... | collective-permute-start | bytes 491528 | tf_op jit(solution)/shard_map/ppermute | solution.py:286
  92.0 7.5 %collective-permute-start.3 = (bf16[640,128]{1,0:T(8,128)(2,1)S(1)}, bf16[640,128]{1,0:T(8,128)(2,1)S(1)}, u32[]{:S(2)}, u32[]{:S(2)}) collective-permute-start(bf16[640,128]{1,0:T(8,128)(2,1)S(1)} %get-tuple-element.33), channel_id=1, source_target_pairs={{0,8},{1,24},{2,40},{3,56},{8,57},{9,9},{10,25},{11,41},{16,42},{1... | collective-permute-start | bytes 491528 | tf_op jit(solution)/shard_map/ppermute | solution.py:286
  100.2 0.7 copy-start.12
  100.9 1.6 copy-start.15
  102.5 8.1 %copy-start.6 = (bf16[640,640]{1,0:T(8,128)(2,1)S(1)}, bf16[640,640]{1,0:T(8,128)(2,1)}, u32[]{:S(2)}) copy-start(bf16[640,640]{1,0:T(8,128)(2,1)} %refs_1_.3) | copy-start | bytes 2457604
  105.3 7.1 %copy-start.10 = (f32[320,128]{1,0:T(8,128)}, f32[320,128]{1,0:T(8,128)S(1)}, u32[]{:S(2)}) copy-start(f32[320,128]{1,0:T(8,128)S(1)} %get-tuple-element.26.refs_1_) | copy-start | bytes 491524
  105.3 5.3 %collective-permute-start.4 = (bf16[320,1152]{1,0:T(8,128)(2,1)S(1)}, bf16[320,1152]{1,0:T(8,128)(2,1)S(1)}, u32[]{:S(2)}, u32[]{:S(2)}) collective-permute-start(bf16[320,1152]{1,0:T(8,128)(2,1)S(1)} %get-tuple-element.27.refs_2_), channel_id=1, source_target_pairs={{0,8},{8,0},{1,9},{9,1},{2,10},{10,2},{3,11},{11,3},{4,12},{12,4},... | collective-permute-start | bytes 2211848 | tf_op jit(solution)/shard_map/ppermute | solution.py:43
  110.6 1.8 %copy-start = (bf16[320,1152]{1,0:T(8,128)(2,1)}, bf16[320,1152]{1,0:T(8,128)(2,1)S(1)}, u32[]{:S(2)}) copy-start(bf16[320,1152]{1,0:T(8,128)(2,1)S(1)} %collective-permute-done.4.refs_3_.refs_2_) | copy-start | bytes 2211844
  136.3 28.8 %collective-permute-start.5 = (bf16[640,128]{1,0:T(8,128)(2,1)S(1)}, bf16[640,128]{1,0:T(8,128)(2,1)S(1)}, u32[]{:S(2)}, u32[]{:S(2)}) collective-permute-start(bf16[640,128]{1,0:T(8,128)(2,1)S(1)} %shard_map.100.refs_4_), channel_id=1, source_target_pairs={{0,4},{4,0},{1,5},{5,1},{2,6},{6,2},{3,7},{7,3},{8,12},{12,8},{9,1... | collective-permute-start | bytes 491528 | tf_op jit(solution)/shard_map/ppermute | solution.py:47
  151.0 1.3 copy-start.2
  152.3 3.1 %copy-start.1 = (bf16[320,1152]{1,0:T(8,128)(2,1)S(1)}, bf16[320,1152]{1,0:T(8,128)(2,1)}, u32[]{:S(2)}) copy-start(bf16[320,1152]{1,0:T(8,128)(2,1)} %copy-done) | copy-start | bytes 2211844
  152.3 3.1 %copy-start.3 = (f32[640,128]{1,0:T(8,128)S(1)}, f32[640,128]{1,0:T(8,128)}, u32[]{:S(2)}) copy-start(f32[640,128]{1,0:T(8,128)} %refs_3_.5) | copy-start | bytes 983044
  152.3 3.1 %copy-start.4 = (f32[640,128]{1,0:T(8,128)S(1)}, f32[640,128]{1,0:T(8,128)}, u32[]{:S(2)}) copy-start(f32[640,128]{1,0:T(8,128)} %refs_4_.5) | copy-start | bytes 983044
  152.3 3.1 %copy-start.11 = (f32[320,128]{1,0:T(8,128)S(1)}, f32[320,128]{1,0:T(8,128)}, u32[]{:S(2)}) copy-start(f32[320,128]{1,0:T(8,128)} %copy-done.10) | copy-start | bytes 491524
Sparse Core Ops, SparseCore 0:
  10.7 36.9 all-gather.9
  59.3 34.1 all-gather.7
  101.0 36.2 all-gather.11

commit v9 on v8

--- a/solution.py
+++ b/solution.py
@@ -206,11 +206,6 @@
         )
 
 
-def pair_kernel(where, first, second, out, mark):
-    out[...] = first[...] + second[...]
-    mark[...] = jnp.zeros_like(mark)
-
-
 def gram_kernel(where, near, far, paired, out, panel, other):
     for k in range(4):
         panel[:, 128 * k : 128 * k + 128] = near[k, :640]
@@ -279,12 +274,8 @@
             lax.dynamic_index_in_dim(far_all, at + t, 0, False)[:640],
         )
 
-    pair, paired_mark = call(
-        pair_kernel,
-        [shaped((640, 128), bf16), shaped((8, 128), f32)],
-        where,
-        *[lax.ppermute(piece(t), axes, left_source(t)) for t in range(2)],
-        moved=500_000,
+    pair = lax.ppermute(piece(0), axes, left_source(0)) + lax.ppermute(
+        piece(1), axes, left_source(1)
     )
 
     rows, right_gram = call(
@@ -303,7 +294,7 @@
         half,
         moments,
         basis,
-        after=(paired_mark,),
+        after=(pair[:16],),
         scratch=[pltpu.VMEM((320, 1024), bf16), pltpu.VMEM((320, 1024), f32)],
         flops=1_400_000_000,
         moved=6_000_000,

time: 173 us -> 173 us (level)
    unnamed x32 -> x30, local copies, waits for them, and re-layouts: 5.34 us -> 4.7 us
    pallas_call x10 -> x9, Pallas kernels: 18.3 us -> 17.7 us  [call(): pl.pallas_call(inner, out_shape=outs, in_specs=[pl.BlockSpec(memory_space...]
  transfers between devices with their start and end apart: 10 -> 10, of which waited for: 5 -> 5; matrix products, arithmetic and copies ran while one was open for 1% -> 2% of each run, Pallas kernels for 9% -> 9%
where the time goes in v9:
time: 173 us; the launch traced here: 172 us
  blocking collectives  67.9 us (39%)
  starting transfers between devices  45 us (26%)
  waiting for transfers between devices  19 us (11%)
  Pallas kernels  17.7 us (10%)
  between operations  13.9 us (8%)
  local copies, waits for them, and re-layouts  6.9 us (4%)
  other arithmetic  2.04 us (1%)
    ppermute x2, starting transfers between devices, other_half(): return lax.ppermute(value, 'zh', [(0, 1), (1, 0)])  29.6 us
    all_to_all x1, blocking collectives, body(): parts = lax.all_to_all(parts, 'y', 0, 0, tiled=True)  23.2 us
    pallas_call x9, Pallas kernels, call(): pl.pallas_call(inner, out_shape=outs, in_specs=[pl.BlockSpec(memory_space...  17.7 us
    all_to_all x1, blocking collectives, body(): summed = lax.all_to_all(summed, 'x', 0, 0, tiled=True)  16.3 us
    all_gather x1, blocking collectives, body(): far_all = lax.all_gather(far, 'y', axis=0)  14.4 us
    all_gather x1, blocking collectives, body(): near_all = lax.all_gather(mine, 'y', axis=0)  14 us
    ppermute x2, waiting for transfers between devices, other_half(): return lax.ppermute(value, 'zh', [(0, 1), (1, 0)])  9.85 us
    ppermute x1, waiting for transfers between devices, body(): lax.ppermute(piece(0), axes, left_source(0))  6.23 us
  transfers between devices with their start and end apart: 10, of which 5 were waited for; matrix products, arithmetic and copies ran while one was open for 2% of the time, Pallas kernels for 9%

profile of v9, /device:TPU:34, one launch (start us, length us, event | category | flops | bytes accessed | tf_op | source)
XLA Modules:
  0.0 172.5 jit_solution(684590506631977228)
XLA Ops:
  7.2 0.0 all-gather.10.cloned.1.call-start
  7.2 0.6 pad_add_fusion.refs_0_
  7.8 2.0 %shard_map.92 = (bf16[768,128]{1,0:T(8,128)(2,1)}, bf16[2,640,128]{2,1,0:T(8,128)(2,1)}) custom-call(s32[4]{0:T(128)} %pad_add_fusion.refs_0_, bf16[640,128]{1,0:T(8,128)(2,1)} %refs_3_.4, bf16[1024,128]{1,0:T(8,128)(2,1)} %refs_2_.1, f32[640,128]{1,0:T(8,128)} %refs_3_.5, f32[640,128]{1,0:T(8,128)} %refs_4_.5), custom_call_target="tpu_custom_call" | custom-call | bytes 1500000 | tf_op jit(solution)/shard_map/pallas_call | solution.py:78
  9.9 0.0 all-gather.10.cloned.1.call-update
  9.9 0.0 all-gather.8.cloned.1.call-start
  9.9 15.0 %collective-permute-start = (bf16[768,128]{1,0:T(8,128)(2,1)}, bf16[768,128]{1,0:T(8,128)(2,1)S(1)}, u32[]{:S(2)}, u32[]{:S(2)}) collective-permute-start(bf16[768,128]{1,0:T(8,128)(2,1)} %get-tuple-element.17), channel_id=1, source_target_pairs={{0,4},{4,0},{1,5},{5,1},{2,6},{6,2},{3,7},{7,3},{8,12},{12,8},{9,1... | collective-permute-start | bytes 589832 | tf_op jit(solution)/shard_map/ppermute | solution.py:47
  24.9 14.0 %all-gather = bf16[3072,128]{1,0:T(8,128)(2,1)S(1)} all-gather(bf16[768,128]{1,0:T(8,128)(2,1)} %get-tuple-element.17), channel_id=2, replica_groups=mesh['layer'=8,'x'=4,'core'=2,'zh'=2,'y'=4] {'y'}, dimensions={0}, use_global_device_ids=true | all-gather | bytes 983040 | tf_op jit(solution)/shard_map/all_gather | solution.py:236
  38.9 1.6 collective-permute-done
  40.6 14.4 %all-gather.1 = bf16[3072,128]{1,0:T(8,128)(2,1)S(1)} all-gather(bf16[768,128]{1,0:T(8,128)(2,1)S(1)} %collective-permute-done), channel_id=3, replica_groups=mesh['layer'=8,'x'=4,'core'=2,'zh'=2,'y'=4] {'y'}, dimensions={0}, use_global_device_ids=true | all-gather | bytes 983040 | tf_op jit(solution)/shard_map/all_gather | solution.py:239
  54.9 0.0 copy-done.13
  54.9 3.3 %shard_map.93 = (bf16[384,1024]{1,0:T(8,128)(2,1)S(1)}, bf16[384,1024]{1,0:T(8,128)(2,1)}, bf16[128,1024]{1,0:T(8,128)(2,1)}) custom-call(s32[4]{0:T(128)S(1)} %copy-done.13, bf16[4,768,128]{2,1,0:T(8,128)(2,1)S(1)} %bitcast.12, bf16[4,768,128]{2,1,0:T(8,128)(2,1)S(1)} %bitcast.15, bf16[640,128]{1,0:T(8,128)(2,1)S(1)} %copy-done.12, ...), custom_call_target="tpu_custom_call" | custom-call | flops 1000000000 | bytes 5000000 | tf_op jit(solution)/shard_map/pallas_call | solution.py:78
  58.2 0.9 copy-done.7
  59.2 0.0 all-gather.8.cloned.1.call-update
  59.2 1.9 %collective-permute-start.1 = (bf16[384,1024]{1,0:T(8,128)(2,1)}, bf16[384,1024]{1,0:T(8,128)(2,1)}, u32[]{:S(2)}, u32[]{:S(2)}) collective-permute-start(bf16[384,1024]{1,0:T(8,128)(2,1)} %get-tuple-element.19), channel_id=1, source_target_pairs={{0,8},{8,0},{1,9},{9,1},{2,10},{10,2},{3,11},{11,3},{4,12},{12,4},... | collective-permute-start | bytes 2359304 | tf_op jit(solution)/shard_map/ppermute | solution.py:43
  61.1 0.0 all-gather.10.cloned.1.call-done
  61.2 1.5 constant_dynamic-slice_fusion.refs_3_.refs_2_
  62.7 1.0 collective-permute-done.1.refs_2_
  63.7 1.3 shard_map.94
  65.0 16.3 %all_to_all.15.refs_1_ = bf16[4,384,256]{2,1,0:T(8,128)(2,1)S(1)} all-to-all(bf16[4,384,256]{2,1,0:T(8,128)(2,1)S(1)} %shard_map.94), channel_id=1, replica_groups=mesh['layer'=8,'x'=4,'core'=2,'zh'=2,'y'=4] {'x'}, dimensions={0} | all-to-all | bytes 1572864 | tf_op jit(solution)/shard_map/all_to_all | solution.py:264
  81.3 1.2 shard_map.95
  82.5 0.8 copy-done.9
  83.3 5.2 %all-to-all-start.1 = ((bf16[4,320,256]{2,1,0:T(8,128)(2,1)}), bf16[4,320,256]{2,1,0:T(8,128)(2,1)S(1)}, u32[]{:S(2)}, u32[]{:S(2)}) async-start(bf16[4,320,256]{2,1,0:T(8,128)(2,1)} %copy-done.9), calls=%async_computation.1 | async-start | bytes 1310720 | tf_op jit(solution)/shard_map/all_to_all | solution.py:288
  88.6 3.5 %collective-permute-start.2 = (bf16[640,128]{1,0:T(8,128)(2,1)S(1)}, bf16[640,128]{1,0:T(8,128)(2,1)S(1)}, u32[]{:S(2)}, u32[]{:S(2)}) collective-permute-start(bf16[640,128]{1,0:T(8,128)(2,1)S(1)} %get-tuple-element.30), channel_id=1, source_target_pairs={{0,0},{1,16},{2,32},{3,48},{8,49},{9,1},{10,17},{11,33},{16,34},{1... | collective-permute-start | bytes 491528 | tf_op jit(solution)/shard_map/ppermute | solution.py:277
  92.1 1.3 collective-permute-start.3
  93.4 6.2 %collective-permute-done.2 = bf16[640,128]{1,0:T(8,128)(2,1)S(1)} collective-permute-done((bf16[640,128]{1,0:T(8,128)(2,1)S(1)}, bf16[640,128]{1,0:T(8,128)(2,1)S(1)}, u32[]{:S(2)}, u32[]{:S(2)}) %collective-permute-start.2) | collective-permute-done | bytes 163872 | tf_op jit(solution)/shard_map/ppermute | solution.py:277
  99.6 0.0 collective-permute-done.3
  99.6 0.7 add.49
  100.3 0.0 all-gather.12.cloned.1.call-update
  100.3 0.7 slice.24.refs_4_
  101.0 0.0 all-to-all-done.1.refs_1_
  101.0 1.6 copy-done.14
  102.6 2.8 %shard_map.96 = (bf16[320,1152]{1,0:T(8,128)(2,1)S(1)}, f32[320,128]{1,0:T(8,128)S(1)}) custom-call(s32[4]{0:T(128)S(1)} %copy-done.13, bf16[4,320,256]{2,1,0:T(8,128)(2,1)S(1)} %all-to-all-done.1.refs_1_, bf16[8,2,320,128]{3,2,1,0:T(8,128)(2,1)S(1)} %constant_dynamic-slice_fusion.refs_3_.refs_2_, bf16[1024,1024]{1,0:T(8,128)(2,1)S(1)} %copy-done.14, ...), custom_call_target="tpu_custom_call" | custom-call | flops 1400000000 | bytes 6000000 | tf_op jit(solution)/shard_map/pallas_call | solution.py:78
  105.4 0.0 copy-start.10
  105.4 3.5 %collective-permute-start.4 = (bf16[320,1152]{1,0:T(8,128)(2,1)S(1)}, bf16[320,1152]{1,0:T(8,128)(2,1)S(1)}, u32[]{:S(2)}, u32[]{:S(2)}) collective-permute-start(bf16[320,1152]{1,0:T(8,128)(2,1)S(1)} %get-tuple-element.24.refs_2_), channel_id=1, source_target_pairs={{0,8},{8,0},{1,9},{9,1},{2,10},{10,2},{3,11},{11,3},{4,12},{12,4},... | collective-permute-start | bytes 2211848 | tf_op jit(solution)/shard_map/ppermute | solution.py:43
  108.9 1.8 %collective-permute-done.4.refs_3_.refs_2_ = bf16[320,1152]{1,0:T(8,128)(2,1)S(1)} collective-permute-done((bf16[320,1152]{1,0:T(8,128)(2,1)S(1)}, bf16[320,1152]{1,0:T(8,128)(2,1)S(1)}, u32[]{:S(2)}, u32[]{:S(2)}) %collective-permute-start.4) | collective-permute-done | bytes 737312 | tf_op jit(solution)/shard_map/ppermute | solution.py:43
  110.7 0.0 copy-done.6
  110.7 1.8 %shard_map.97 = bf16[4,1280,128]{2,1,0:T(8,128)(2,1)S(1)} custom-call(s32[4]{0:T(128)S(1)} %copy-done.13, bf16[640,640]{1,0:T(8,128)(2,1)S(1)} %copy-done.6, bf16[320,1152]{1,0:T(8,128)(2,1)S(1)} %get-tuple-element.24.refs_2_, bf16[320,1152]{1,0:T(8,128)(2,1)S(1)} %collective-permute-done.4.refs_3_.refs_2_), custom_call_target="tpu_custom_call" | custom-call | flops 840000000 | bytes 4000000 | tf_op jit(solution)/shard_map/pallas_call | solution.py:78
  112.6 23.2 %all_to_all.16.refs_5_.refs_1_ = bf16[4,1280,128]{2,1,0:T(8,128)(2,1)S(1)} all-to-all(bf16[4,1280,128]{2,1,0:T(8,128)(2,1)S(1)} %shard_map.97), channel_id=1, replica_groups=mesh['layer'=8,'x'=4,'core'=2,'zh'=2,'y'=4] {'y'}, dimensions={0} | all-to-all | bytes 2621440 | tf_op jit(solution)/shard_map/all_to_all | solution.py:314
  135.8 0.6 shard_map.99.refs_4_
  136.4 14.6 %collective-permute-start.5 = (bf16[640,128]{1,0:T(8,128)(2,1)S(1)}, bf16[640,128]{1,0:T(8,128)(2,1)S(1)}, u32[]{:S(2)}, u32[]{:S(2)}) collective-permute-start(bf16[640,128]{1,0:T(8,128)(2,1)S(1)} %shard_map.99.refs_4_), channel_id=1, source_target_pairs={{0,4},{4,0},{1,5},{5,1},{2,6},{6,2},{3,7},{7,3},{8,12},{12,8},{9,1... | collective-permute-start | bytes 491528 | tf_op jit(solution)/shard_map/ppermute | solution.py:47
  151.1 0.0 all-gather.12.cloned.1.call-done
  151.1 1.3 copy-done.2
  152.4 3.1 %shard_map.100 = f32[640,640]{1,0:T(8,128)} custom-call(s32[4]{0:T(128)S(1)} %copy-done.13, bf16[4,768,128]{2,1,0:T(8,128)(2,1)S(1)} %bitcast.14, bf16[4,768,128]{2,1,0:T(8,128)(2,1)S(1)} %bitcast.17, bf16[8,640,128]{2,1,0:T(8,128)(2,1)S(1)} %bitcast.18, bf16[640,128]{1,0:T(8,128)(2,1)S(1)} %shard_map.99.refs_4_), custom_call_target="tpu_custom_call" | custom-call | flops 10000 | bytes 10000 | tf_op jit(solution)/shard_map/pallas_call | solution.py:78
  155.5 0.0 copy-done.1
  155.5 0.0 copy-done.4
  155.6 1.5 shard_map.98
  157.0 8.2 %collective-permute-done.5 = bf16[640,128]{1,0:T(8,128)(2,1)S(1)} collective-permute-done((bf16[640,128]{1,0:T(8,128)(2,1)S(1)}, bf16[640,128]{1,0:T(8,128)(2,1)S(1)}, u32[]{:S(2)}, u32[]{:S(2)}) %collective-permute-start.5) | collective-permute-done | bytes 163872 | tf_op jit(solution)/shard_map/ppermute | solution.py:47
  165.3 0.7 add_convert_fusion
  (24 shorter events, 0.1 us)
Async XLA Ops:
  7.2 54.0 %all-gather.10.cloned.1.call-start = ((), (), s32[]{:S(2)}) async-start(), calls=%async_computation.4 | async-start | bytes 2949120 | tf_op jit(solution)/shard_map/all_gather | solution.py:238
  9.9 45.1 %copy-start.5 = (bf16[640,640]{1,0:T(8,128)(2,1)S(1)}, bf16[640,640]{1,0:T(8,128)(2,1)}, u32[]{:S(2)}) copy-start(bf16[640,640]{1,0:T(8,128)(2,1)} %refs_1_.3) | copy-start | bytes 2457604
  9.9 45.1 %copy-start.12 = (bf16[640,128]{1,0:T(8,128)(2,1)S(1)}, bf16[640,128]{1,0:T(8,128)(2,1)}, u32[]{:S(2)}) copy-start(bf16[640,128]{1,0:T(8,128)(2,1)} %refs_3_.4) | copy-start | bytes 491524
  9.9 45.1 %copy-start.13 = (s32[4]{0:T(128)S(1)}, s32[4]{0:T(128)}, u32[]{:S(2)}) copy-start(s32[4]{0:T(128)} %pad_add_fusion.refs_0_) | copy-start | bytes 52
  9.9 91.1 %all-gather.8.cloned.1.call-start = ((), (), s32[]{:S(2)}) async-start(), calls=%async_computation.3 | async-start | bytes 2359296 | tf_op jit(solution)/shard_map/all_gather | solution.py:253
  9.9 30.6 %collective-permute-start = (bf16[768,128]{1,0:T(8,128)(2,1)}, bf16[768,128]{1,0:T(8,128)(2,1)S(1)}, u32[]{:S(2)}, u32[]{:S(2)}) collective-permute-start(bf16[768,128]{1,0:T(8,128)(2,1)} %get-tuple-element.17), channel_id=1, source_target_pairs={{0,4},{4,0},{1,5},{5,1},{2,6},{6,2},{3,7},{7,3},{8,12},{12,8},{9,1... | collective-permute-start | bytes 589832 | tf_op jit(solution)/shard_map/ppermute | solution.py:47
  58.2 0.9 copy-start.7
  59.2 4.5 %collective-permute-start.1 = (bf16[384,1024]{1,0:T(8,128)(2,1)}, bf16[384,1024]{1,0:T(8,128)(2,1)}, u32[]{:S(2)}, u32[]{:S(2)}) collective-permute-start(bf16[384,1024]{1,0:T(8,128)(2,1)} %get-tuple-element.19), channel_id=1, source_target_pairs={{0,8},{8,0},{1,9},{9,1},{2,10},{10,2},{3,11},{11,3},{4,12},{12,4},... | collective-permute-start | bytes 2359304 | tf_op jit(solution)/shard_map/ppermute | solution.py:43
  61.1 2.6 %copy-start.8 = (bf16[384,1024]{1,0:T(8,128)(2,1)S(1)}, bf16[384,1024]{1,0:T(8,128)(2,1)}, u32[]{:S(2)}) copy-start(bf16[384,1024]{1,0:T(8,128)(2,1)} %copy-done.7) | copy-start | bytes 2359300
  82.5 0.8 copy-start.9
  83.3 17.7 %all-to-all-start.1 = ((bf16[4,320,256]{2,1,0:T(8,128)(2,1)}), bf16[4,320,256]{2,1,0:T(8,128)(2,1)S(1)}, u32[]{:S(2)}, u32[]{:S(2)}) async-start(bf16[4,320,256]{2,1,0:T(8,128)(2,1)} %copy-done.9), calls=%async_computation.1 | async-start | bytes 1310720 | tf_op jit(solution)/shard_map/all_to_all | solution.py:288
  88.5 62.6 %all-gather.12.cloned.1.call-start = ((), (), s32[]{:S(2)}) async-start(), calls=%async_computation.5 | async-start | bytes 1474560 | tf_op jit(solution)/shard_map/all_gather | solution.py:320
  88.6 11.0 %collective-permute-start.2 = (bf16[640,128]{1,0:T(8,128)(2,1)S(1)}, bf16[640,128]{1,0:T(8,128)(2,1)S(1)}, u32[]{:S(2)}, u32[]{:S(2)}) collective-permute-start(bf16[640,128]{1,0:T(8,128)(2,1)S(1)} %get-tuple-element.30), channel_id=1, source_target_pairs={{0,0},{1,16},{2,32},{3,48},{8,49},{9,1},{10,17},{11,33},{16,34},{1... | collective-permute-start | bytes 491528 | tf_op jit(solution)/shard_map/ppermute | solution.py:277
  92.1 7.5 %collective-permute-start.3 = (bf16[640,128]{1,0:T(8,128)(2,1)S(1)}, bf16[640,128]{1,0:T(8,128)(2,1)S(1)}, u32[]{:S(2)}, u32[]{:S(2)}) collective-permute-start(bf16[640,128]{1,0:T(8,128)(2,1)S(1)} %get-tuple-element.29), channel_id=1, source_target_pairs={{0,8},{1,24},{2,40},{3,56},{8,57},{9,9},{10,25},{11,41},{16,42},{1... | collective-permute-start | bytes 491528 | tf_op jit(solution)/shard_map/ppermute | solution.py:277
  101.0 1.6 copy-start.14
  102.6 8.1 %copy-start.6 = (bf16[640,640]{1,0:T(8,128)(2,1)S(1)}, bf16[640,640]{1,0:T(8,128)(2,1)}, u32[]{:S(2)}) copy-start(bf16[640,640]{1,0:T(8,128)(2,1)} %refs_1_.3) | copy-start | bytes 2457604
  105.4 7.1 %copy-start.10 = (f32[320,128]{1,0:T(8,128)}, f32[320,128]{1,0:T(8,128)S(1)}, u32[]{:S(2)}) copy-start(f32[320,128]{1,0:T(8,128)S(1)} %get-tuple-element.23.refs_1_) | copy-start | bytes 491524
  105.4 5.3 %collective-permute-start.4 = (bf16[320,1152]{1,0:T(8,128)(2,1)S(1)}, bf16[320,1152]{1,0:T(8,128)(2,1)S(1)}, u32[]{:S(2)}, u32[]{:S(2)}) collective-permute-start(bf16[320,1152]{1,0:T(8,128)(2,1)S(1)} %get-tuple-element.24.refs_2_), channel_id=1, source_target_pairs={{0,8},{8,0},{1,9},{9,1},{2,10},{10,2},{3,11},{11,3},{4,12},{12,4},... | collective-permute-start | bytes 2211848 | tf_op jit(solution)/shard_map/ppermute | solution.py:43
  110.7 1.8 %copy-start = (bf16[320,1152]{1,0:T(8,128)(2,1)}, bf16[320,1152]{1,0:T(8,128)(2,1)S(1)}, u32[]{:S(2)}) copy-start(bf16[320,1152]{1,0:T(8,128)(2,1)S(1)} %collective-permute-done.4.refs_3_.refs_2_) | copy-start | bytes 2211844
  136.4 28.8 %collective-permute-start.5 = (bf16[640,128]{1,0:T(8,128)(2,1)S(1)}, bf16[640,128]{1,0:T(8,128)(2,1)S(1)}, u32[]{:S(2)}, u32[]{:S(2)}) collective-permute-start(bf16[640,128]{1,0:T(8,128)(2,1)S(1)} %shard_map.99.refs_4_), channel_id=1, source_target_pairs={{0,4},{4,0},{1,5},{5,1},{2,6},{6,2},{3,7},{7,3},{8,12},{12,8},{9,1... | collective-permute-start | bytes 491528 | tf_op jit(solution)/shard_map/ppermute | solution.py:47
  151.1 1.3 copy-start.2
  152.4 3.1 %copy-start.1 = (bf16[320,1152]{1,0:T(8,128)(2,1)S(1)}, bf16[320,1152]{1,0:T(8,128)(2,1)}, u32[]{:S(2)}) copy-start(bf16[320,1152]{1,0:T(8,128)(2,1)} %copy-done) | copy-start | bytes 2211844
  152.4 3.1 %copy-start.3 = (f32[640,128]{1,0:T(8,128)S(1)}, f32[640,128]{1,0:T(8,128)}, u32[]{:S(2)}) copy-start(f32[640,128]{1,0:T(8,128)} %refs_3_.5) | copy-start | bytes 983044
  152.4 3.1 %copy-start.4 = (f32[640,128]{1,0:T(8,128)S(1)}, f32[640,128]{1,0:T(8,128)}, u32[]{:S(2)}) copy-start(f32[640,128]{1,0:T(8,128)} %refs_4_.5) | copy-start | bytes 983044
  152.4 3.1 %copy-start.11 = (f32[320,128]{1,0:T(8,128)S(1)}, f32[320,128]{1,0:T(8,128)}, u32[]{:S(2)}) copy-start(f32[320,128]{1,0:T(8,128)} %copy-done.10) | copy-start | bytes 491524
Sparse Core Ops, SparseCore 0:
  10.7 36.9 all-gather.9
  59.3 34.1 all-gather.7
  100.5 36.2 all-gather.11
